TPU v7x, 32 devices: a whole 2x2x4 slice. The times are simulated.
32 devices in a mesh: grp: 4 (over y, x), tp: 8 (over z, core).
Axes of the slice: x: 2, y: 2, z: 4, core: 2. Of those that a mesh axis runs over, the one named last changes fastest.
Arguments:
- features: bfloat16 [1024, 49152], P('grp', 'tp'), may hold values from -24 to 24
- weight: bfloat16 [49152, 8192], P('tp', 'grp'), may hold values from -0.049804688 to 0.049804688
- norm_gain: float32 [8192], P('grp'), may hold values from 0.1 to 1.9
- target: bfloat16 [1024, 8192], P(None, 'grp'), may hold values from -6 to 6
- counts: int32 [128], replicated, may hold values from 1 to 8
Outputs:
- weight_grad: bfloat16 [49152, 8192], P('tp', 'grp')
- draft_loss: float32 [], replicated
All inputs are finite; a program needn't handle non-finite values.
Results may differ from a plain program's by a relative error of at most 0.0085.
Values may be sent and summed in bfloat16 or wider, within the bound.
No kernel may reach another device: no remote copies, remote signals or barrier semaphores. Data moves between devices by JAX's collectives and lax.ppermute only.
A program may use at most 192 MiB of HBM per device.

v0:
```python
import jax
import jax.numpy as jnp
from jax import lax
from jax.sharding import PartitionSpec as P

DOUT = 8192
SPEC = 8


epsilon = 1e-06


def row_mask(counts, row_start, row_count):
    row_index = row_start + jnp.arange(row_count, dtype=jnp.int32)
    owner = jnp.take(counts, row_index // SPEC)
    return (row_index % SPEC < owner).astype(jnp.float32)[:, None]


def backward_rows(hidden, target_rows, row_live, norm_gain, accepted):
    gain_row = norm_gain[None, :]
    squares = lax.psum(jnp.sum(hidden * hidden, axis=1), "grp")
    inverse_rms = lax.rsqrt(squares / DOUT + epsilon)[:, None]
    normed = hidden * inverse_rms * gain_row
    deviation = normed - target_rows
    residual = row_live * deviation / accepted
    coupling = lax.psum(jnp.sum(gain_row * residual * hidden, axis=1), "grp")[:, None]
    act_grad = (
        inverse_rms * gain_row * residual - hidden * inverse_rms**3 * coupling / DOUT
    ).astype(jnp.bfloat16)
    partial_loss = 0.5 * jnp.sum(residual * deviation)
    return (act_grad, partial_loss)


def shards(features, weight, norm_gain, target, counts):
    gathered = lax.all_gather(features, "grp", axis=0, tiled=True)
    total_rows = gathered.shape[0]
    accepted = jnp.sum(counts).astype(jnp.float32)
    rows_here = total_rows // lax.axis_size("tp")
    row_start = lax.axis_index("tp") * rows_here
    hidden = lax.psum_scatter(
        jnp.dot(gathered, weight, preferred_element_type=jnp.float32).astype(jnp.bfloat16),
        "tp",
        scatter_dimension=0,
        tiled=True,
    ).astype(jnp.float32)
    target_rows = lax.dynamic_slice_in_dim(target, row_start, rows_here, 0).astype(jnp.float32)
    row_live = row_mask(counts, row_start, rows_here)
    act_grad, partial_loss = backward_rows(hidden, target_rows, row_live, norm_gain, accepted)
    all_grad = lax.all_gather(act_grad, "tp", axis=0, tiled=True)
    draft_loss = lax.psum(partial_loss, ("grp", "tp"))
    weight_grad = lax.dot_general(
        gathered, all_grad, (((0,), (0,)), ((), ())), preferred_element_type=jnp.float32
    ).astype(jnp.bfloat16)
    return (weight_grad, draft_loss)


def solution(mesh):
    placed = (P("grp", "tp"), P("tp", "grp"), P("grp"), P(None, "grp"), P())
    return jax.shard_map(
        shards, mesh=mesh, in_specs=placed, out_specs=(P("tp", "grp"), P()), check_vma=False
    )
```

profile of v0, /device:TPU:0, one launch (start us, length us, event | category | flops | bytes accessed | tf_op | source)
XLA Modules:
  0.0 361.7 jit_solution(6805438105381393411)
XLA Ops:
  7.2 0.0 all-gather.3.cloned.1.call-start
  7.2 0.7 all-gather.3.cloned.1.call-update
  7.9 0.0 copy-start
  7.9 0.0 copy-start.1
  7.9 0.0 reduce-scatter.2.cloned.1.call-start
  8.0 127.1 %all-gather.3.cloned.1.call-done = bf16[1024,6144]{1,0:T(8,128)(2,1)} async-done(((bf16[256,6144]{1,0:T(8,128)(2,1)}), bf16[1024,6144]{1,0:T(8,128)(2,1)}) %all-gather.3.cloned.1.call-update) | async-done | bytes 12582928 | tf_op jit(solution)/shard_map/all_gather | solution.py:35
  135.1 34.0 %convolution_convert_fusion = bf16[1024,2048]{1,0:T(8,128)(2,1)} fusion(bf16[1024,6144]{1,0:T(8,128)(2,1)} %all-gather.3.cloned.1.call-done, bf16[6144,2048]{1,0:T(8,128)(2,1)} %param.6), kind=kOutput, calls=%fused_computation.2 | convolution fusion | flops 25771900928 | bytes 41943040 | tf_op jit(solution)/shard_map/dot_general | solution.py:41
  169.1 0.0 reduce-scatter.2.cloned.1.call-update
  169.1 0.0 all-gather.5.cloned.1.call-start
  169.2 0.0 copy-done
  169.2 0.6 reduce_sum.37
  170.5 1.2 gather_fusion
  171.7 47.5 %reduce-scatter.2.cloned.1.call-done = bf16[128,2048]{1,0:T(8,128)(2,1)} async-done(((bf16[1024,2048]{1,0:T(8,128)(2,1)}), bf16[128,2048]{1,0:T(8,128)(2,1)}) %reduce-scatter.2.cloned.1.call-update) | async-done | bytes 524304 | tf_op jit(solution)/shard_map/reduce_scatter | solution.py:40
  219.3 1.2 fusion
  220.5 9.8 %psum.21 = f32[128]{0:T(128)S(1)} all-reduce(f32[128]{0:T(128)S(1)} %fusion), channel_id=1, replica_groups=mesh['grp'=4,'tp'=8] {'grp'}, use_global_device_ids=true, to_apply=%region_2.3 | all-reduce | flops 128 | bytes 1024 | tf_op jit(solution)/shard_map/psum | solution.py:21
  230.3 0.0 copy-done.1
  230.3 2.5 multiply_reduce_fusion
  232.9 7.9 %psum.22 = f32[128]{0:T(128)S(1)} all-reduce(f32[128]{0:T(128)S(1)} %get-tuple-element.7), channel_id=1, replica_groups=mesh['grp'=4,'tp'=8] {'grp'}, use_global_device_ids=true, to_apply=%region_5.6 | all-reduce | flops 128 | bytes 1024 | tf_op jit(solution)/shard_map/psum | solution.py:26
  240.8 2.6 fusion.6
  243.4 0.0 all-gather.5.cloned.1.call-update
  244.1 39.9 %psum.23 = f32[]{:T(128)} all-reduce(f32[]{:T(128)S(6)} %mul_shard_map.3), channel_id=1, replica_groups=mesh['grp'=4,'tp'=8] {'grp','tp'}, use_global_device_ids=true, to_apply=%region_7.8 | all-reduce | flops 1 | bytes 8 | tf_op jit(solution)/shard_map/psum | solution.py:50
  283.9 5.0 %all-gather.5.cloned.1.call-done = bf16[1024,2048]{1,0:T(8,128)(2,1)} async-done(((bf16[128,2048]{1,0:T(8,128)(2,1)}), bf16[1024,2048]{1,0:T(8,128)(2,1)}) %all-gather.5.cloned.1.call-update) | async-done | bytes 4194320 | tf_op jit(solution)/shard_map/all_gather | solution.py:49
  289.0 33.6 %convert_bitcast_fusion = bf16[6144,2048]{0,1:T(8,128)(2,1)} fusion(bf16[1024,2048]{1,0:T(8,128)(2,1)} %all-gather.5.cloned.1.call-done, bf16[1024,6144]{1,0:T(8,128)(2,1)} %all-gather.3.cloned.1.call-done), kind=kOutput, calls=%fused_computation.1 | convolution fusion | flops 25782386688 | bytes 41943040 | tf_op jit(solution)/shard_map/dot_general | solution.py:51
  322.6 32.6 %copy.8 = bf16[6144,2048]{1,0:T(8,128)(2,1)} copy(bf16[6144,2048]{0,1:T(8,128)(2,1)} %convert_bitcast_fusion) | data formatting | bytes 50331648
  (4 shorter events, 0.0 us)
Async XLA Ops:
  7.2 127.9 %all-gather.3.cloned.1.call-start = ((), (), s32[]{:S(2)}) async-start(), calls=%async_computation.1 | async-start | bytes 15728640 | tf_op jit(solution)/shard_map/all_gather | solution.py:35
  7.9 161.3 %copy-start = (s32[128]{0:T(128)S(1)}, s32[128]{0:T(128)}, u32[]{:S(2)}) copy-start(s32[128]{0:T(128)} %param.9) | copy-start | bytes 1540
  7.9 222.4 %copy-start.1 = (f32[2048]{0:T(1024)S(1)}, f32[2048]{0:T(1024)}, u32[]{:S(2)}) copy-start(f32[2048]{0:T(1024)} %param.7) | copy-start | bytes 24580
  7.9 211.3 %reduce-scatter.2.cloned.1.call-start = ((), (), s32[]{:S(2)}) async-start(), calls=%async_computation.2 | async-start | bytes 4718592 | tf_op jit(solution)/shard_map/reduce_scatter | solution.py:40
  169.1 119.9 %all-gather.5.cloned.1.call-start = ((), (), s32[]{:S(2)}) async-start(), calls=%async_computation.3 | async-start | bytes 4718592 | tf_op jit(solution)/shard_map/all_gather | solution.py:49
Sparse Core Ops, SparseCore 0:
  9.8 125.2 all-gather.2
  169.2 49.9 reduce-scatter.1
  243.5 45.3 all-gather.4
where the time goes:
time: 363 us; the launch traced here: 362 us
  waiting for transfers between devices  180 us (50%)
  matrix products  67.6 us (19%)
  blocking collectives  57.7 us (16%)
  local copies, waits for them, and re-layouts  33.8 us (9%)
  between operations  15.1 us (4%)
  other arithmetic  7.01 us (2%)
    all_gather x1, waiting for transfers between devices, shards(): gathered = lax.all_gather(features, 'grp', axis=0, tiled=True)  127 us
    reduce_scatter x1, waiting for transfers between devices, shards(): lax.psum_scatter(jnp.dot(gathered, weight, preferred_element_type=jnp.flo...  47.5 us
    psum x1, blocking collectives, shards(): draft_loss = lax.psum(partial_loss, ('grp', 'tp'))  39.9 us
    dot_general x1, matrix products, shards(): jnp.dot(gathered, weight, preferred_element_type=jnp.float32)  34 us
    dot_general x1, matrix products, shards(): lax.dot_general(gathered, all_grad, (((0,), (0,)), ((), ())), preferred_e...  33.6 us
    unnamed x5, local copies, waits for them, and re-layouts  32.6 us
    psum x1, blocking collectives, backward_rows(): squares = lax.psum(jnp.sum(hidden * hidden, axis=1), 'grp')  9.84 us
    psum x1, blocking collectives, backward_rows(): lax.psum(jnp.sum(gain_row * residual * hidden, axis=1), 'grp')[:, None]  7.95 us
  transfers between devices with their start and end apart: 3, of which 3 were waited for; matrix products, arithmetic and copies ran while one was open for 1% of the time, Pallas kernels for 0%

commit v1 on v0

v1 whole, which is shorter than its diff:
```python
import functools
import jax
import jax.numpy as jnp
from jax import lax
from jax.experimental import pallas as pl
from jax.experimental.pallas import tpu as pltpu
from jax.sharding import PartitionSpec as P

SPEC = 8
epsilon = 1e-06
MIB = 2**20
HBM = pl.BlockSpec(memory_space=pltpu.HBM)
SMEM = pl.BlockSpec(memory_space=pltpu.SMEM)
VMEM = pl.BlockSpec(memory_space=pltpu.VMEM)
bf16, f32 = jnp.bfloat16, jnp.float32


def exchange(value, axis, mask):
    size = lax.axis_size(axis)
    return lax.ppermute(value, axis, [(i, i ^ mask) for i in range(size)])


def after(value, *others):
    return lax.optimization_barrier((value, *others))[0]


def whole(shape):
    return pl.BlockSpec(shape, lambda _: (0,) * len(shape))


def params(mib):
    return pltpu.CompilerParams(vmem_limit_bytes=mib * MIB)


def cost(flops=1024, moved=1024):
    return pl.CostEstimate(flops=flops, bytes_accessed=moved, transcendentals=0)


def copy_kernel(ranges, place_ref, *refs):
    count = len(ranges)
    sources, targets, sems = refs[:count], refs[count : 2 * count], refs[2 * count]
    copies = [
        pltpu.make_async_copy(source.at[pl.ds(start, size), :], target, sems.at[i])
        for i, (source, target, (start, size)) in enumerate(zip(sources, targets, ranges))
    ]
    for copy in copies:
        copy.start()
    for copy in copies:
        copy.wait()


def copy_rows(place, pieces, in_vmem=()):
    shapes = [((size, array.shape[1]), array.dtype) for array, _, size in pieces]
    return pl.pallas_call(
        functools.partial(copy_kernel, [(start, size) for _, start, size in pieces]),
        in_specs=[SMEM] + [HBM] * len(pieces),
        out_specs=[VMEM if i in in_vmem else HBM for i in range(len(pieces))],
        out_shape=[
            pltpu.VMEM(*shape) if i in in_vmem else jax.ShapeDtypeStruct(*shape)
            for i, shape in enumerate(shapes)
        ],
        scratch_shapes=[pltpu.SemaphoreType.DMA((len(pieces),))],
        compiler_params=params(24),
        cost_estimate=cost(),
        name="copy_rows",
    )(place, *[array for array, _, _ in pieces])


def forward_kernel(pieces, tile, place_ref, *refs):
    parts = refs[:pieces]
    weight_ref, keep_out, send_out, rows_ref, keep_ref, send_ref, sems, out_sems = refs[pieces:]
    copies = []
    start = 0
    for i, part in enumerate(parts):
        size = part.shape[0]
        copies.append(pltpu.make_async_copy(part, rows_ref.at[pl.ds(start, size), :], sems.at[i]))
        start += size
    for copy in copies:
        copy.start()
    for copy in copies:
        copy.wait()
    first = place_ref[0] == 0
    turn = place_ref[1]
    slots, half, units = keep_ref.shape
    copies = []
    for step in range(units // tile):
        columns = pl.ds(step * tile, tile)
        product = jnp.dot(
            rows_ref[...], weight_ref[:, columns], preferred_element_type=f32
        )
        for block in range(slots):
            low = product[block * 2 * half : block * 2 * half + half]
            high = product[block * 2 * half + half : (block + 1) * 2 * half]
            slot = block ^ turn
            keep_ref[slot, :, columns] = jnp.where(first, low, high)
            send_ref[slot, :, columns] = jnp.where(first, high, low).astype(bf16)
        for i, (scratch, out) in enumerate(((keep_ref, keep_out), (send_ref, send_out))):
            copies.append(
                pltpu.make_async_copy(
                    scratch.at[:, :, columns], out.at[:, :, columns], out_sems.at[i, step]
                )
            )
            copies[-1].start()
    for copy in copies:
        copy.wait()


def forward(place, parts, weight):
    depth, units = weight.shape
    total_rows = sum(part.shape[0] for part in parts)
    slots = lax.axis_size("grp")
    half = total_rows // slots // 2
    tile = min(units, 512)
    shape = (slots, half, units)
    return pl.pallas_call(
        functools.partial(forward_kernel, len(parts), tile),
        in_specs=[SMEM] + [HBM] * len(parts) + [VMEM],
        out_specs=[HBM, HBM],
        out_shape=[jax.ShapeDtypeStruct(shape, f32), jax.ShapeDtypeStruct(shape, bf16)],
        scratch_shapes=[
            pltpu.VMEM((total_rows, depth), bf16),
            pltpu.VMEM(shape, f32),
            pltpu.VMEM(shape, bf16),
            pltpu.SemaphoreType.DMA((len(parts),)),
            pltpu.SemaphoreType.DMA((2, units // tile)),
        ],
        compiler_params=params(24),
        cost_estimate=cost(),
        name="forward",
    )(place, *parts, weight)


def pair_kernel(place_ref, keep_ref, arrived_ref, own_ref, *sends):
    own_ref[...] = keep_ref[0] + arrived_ref[0].astype(f32)
    for k, send_ref in enumerate(sends, 1):
        send_ref[...] = (keep_ref[k] + arrived_ref[k].astype(f32)).astype(bf16)


def sum_pair(place, keep, arrived):
    slots, half, units = keep.shape
    out = pl.pallas_call(
        pair_kernel,
        grid=(1,),
        in_specs=[SMEM, whole(keep.shape), whole(keep.shape)],
        out_specs=[whole((half, units))] * slots,
        out_shape=[jax.ShapeDtypeStruct((half, units), f32)]
        + [jax.ShapeDtypeStruct((half, units), bf16)] * (slots - 1),
        compiler_params=params(24),
        cost_estimate=cost(),
        name="sum_pair",
    )(place, keep, arrived)
    return out[0], out[1:]


def rows_kernel(place_ref, own_ref, gain_ref, target_ref, *refs):
    arrived, (hidden_ref, sums_ref) = refs[:-2], refs[-2:]
    hidden = own_ref[...]
    for value in arrived:
        hidden = hidden + value[...].astype(f32)
    hidden_ref[...] = hidden
    scaled = hidden * gain_ref[...]
    target = target_ref[...].astype(f32)
    lane = lax.broadcasted_iota(jnp.int32, sums_ref.shape, 1)
    sums = jnp.zeros(sums_ref.shape, f32)
    terms = (hidden * hidden, scaled * scaled, scaled * target, target * target)
    for i, term in enumerate(terms):
        sums = jnp.where(lane == i, jnp.sum(term, axis=1, keepdims=True), sums)
    sums_ref[...] = sums


def sum_planes(place, own, arrived, gain, target):
    half, units = own.shape
    return pl.pallas_call(
        rows_kernel,
        grid=(1,),
        in_specs=[SMEM, whole(own.shape), whole(gain.shape)] + [whole(own.shape)] * (1 + len(arrived)),
        out_specs=[whole(own.shape), whole((half, 128))],
        out_shape=[
            jax.ShapeDtypeStruct((half, units), f32),
            jax.ShapeDtypeStruct((half, 128), f32),
        ],
        compiler_params=params(24),
        cost_estimate=cost(),
        name="sum_planes",
    )(place, own, gain, target, *arrived)


def gradient_kernel(all_units, place_ref, hidden_ref, gain_ref, target_ref, share_ref, *refs):
    all_sums, (grad_ref, loss_ref) = refs[:-2], refs[-2:]
    sums = all_sums[0][...]
    for value in all_sums[1:]:
        sums = sums + value[...]
    squares, scaled_squares = sums[:, 0:1], sums[:, 1:2]
    products, target_squares = sums[:, 2:3], sums[:, 3:4]
    share = share_ref[:, 0:1]
    inverse_rms = lax.rsqrt(squares / all_units + epsilon)
    coupling = share * (inverse_rms * scaled_squares - products)
    loss = inverse_rms * (inverse_rms * scaled_squares - 2.0 * products) + target_squares
    loss_ref[...] = jnp.broadcast_to(
        jnp.sum(0.5 * share * loss, axis=0, keepdims=True), loss_ref.shape
    )
    hidden = hidden_ref[...]
    gain = gain_ref[...]
    residual = share * (hidden * inverse_rms * gain - target_ref[...].astype(f32))
    grad = inverse_rms * gain * residual - hidden * (inverse_rms**3 * coupling / all_units)
    grad_ref[...] = grad.astype(bf16)


def gradient(place, hidden, all_sums, gain, target, share, all_units):
    half, units = hidden.shape
    return pl.pallas_call(
        functools.partial(gradient_kernel, all_units),
        grid=(1,),
        in_specs=[SMEM, whole(hidden.shape), whole(gain.shape), whole(hidden.shape)]
        + [whole((half, 128))] * (1 + len(all_sums)),
        out_specs=[whole(hidden.shape), whole((1, 128))],
        out_shape=[
            jax.ShapeDtypeStruct((half, units), bf16),
            jax.ShapeDtypeStruct((1, 128), f32),
        ],
        compiler_params=params(24),
        cost_estimate=cost(),
        name="gradient",
    )(place, hidden, gain, target, share, *all_sums)


def backward_kernel(piece_counts, slots, has_base, place_ref, *refs):
    count = sum(piece_counts)
    parts, refs = refs[:count], refs[count:]
    grads, refs = refs[: 2 * slots * len(piece_counts)], refs[2 * slots * len(piece_counts) :]
    out_ref, rows_ref = refs[-2:]

    @pl.when(pl.program_id(0) == 0)
    def _():
        core = place_ref[0]
        turn = place_ref[1]
        start = 0
        for chunk in range(len(piece_counts)):
            here = grads[2 * slots * chunk : 2 * slots * (chunk + 1)]
            half = here[0].shape[0]
            for slot in range(slots):
                row = start + (slot ^ turn) * 2 * half
                rows_ref[pl.ds(pl.multiple_of(row + core * half, half), half), :] = here[slot][...]
                rows_ref[pl.ds(pl.multiple_of(row + (1 - core) * half, half), half), :] = here[
                    slots + slot
                ][...]
            start += slots * 2 * half

    left = jnp.concatenate([part[...] for part in parts], axis=0)
    product = lax.dot_general(
        left, rows_ref[...], (((0,), (0,)), ((), ())), preferred_element_type=f32
    )
    if has_base:
        product += refs[0][...].astype(f32)
    out_ref[...] = product.astype(bf16)


def backward(place, chunks, grads, base=None):
    parts = [part for pieces in chunks for part in pieces]
    flat = [grad for pieces in grads for grad in pieces]
    slots = len(grads[0]) // 2
    depth = parts[0].shape[1]
    units = flat[0].shape[1]
    total_rows = sum(part.shape[0] for part in parts)
    tile = min(depth, 512)
    out_spec = pl.BlockSpec((tile, units), lambda k: (k, 0))
    return pl.pallas_call(
        functools.partial(backward_kernel, [len(p) for p in chunks], slots, base is not None),
        grid=(depth // tile,),
        in_specs=[SMEM]
        + [pl.BlockSpec((part.shape[0], tile), lambda k: (0, k)) for part in parts]
        + [pl.BlockSpec(grad.shape, lambda k: (0, 0)) for grad in flat]
        + ([out_spec] if base is not None else []),
        out_specs=out_spec,
        out_shape=jax.ShapeDtypeStruct((depth, units), bf16),
        scratch_shapes=[pltpu.VMEM((total_rows, units), bf16)],
        compiler_params=params(34),
        cost_estimate=cost(2 * total_rows * depth * units, 4 * depth * units),
        name="backward",
    )(place, *parts, *flat, *([] if base is None else [base]))


def piece_rows(rows):
    return [rows // 4] * 4


def shards(features, weight, norm_gain, target, counts):
    groups = lax.axis_size("grp")
    group, place_tp = lax.axis_index("grp"), lax.axis_index("tp")
    core, plane = place_tp % 2, place_tp // 2
    place = jnp.stack([core, plane ^ group]).astype(jnp.int32)
    group_rows = features.shape[0]
    all_units = norm_gain.shape[0] * groups
    gain = norm_gain[None, :]

    sizes = piece_rows(group_rows)
    n = len(sizes)
    starts = [sum(sizes[:i]) for i in range(n)]

    accepted = jnp.sum(counts).astype(f32)
    requests = group_rows // SPEC
    here = lax.dynamic_slice_in_dim(counts, plane * requests, requests, 0)
    live = (jnp.arange(SPEC, dtype=jnp.int32)[None, :] < here[:, None]).astype(f32) / accepted
    live = jnp.broadcast_to(live.reshape(group_rows, 1), (group_rows, 128))
    shares, targets = [], []
    for start, size in zip(starts, sizes):
        row, half = start + core * (size // 2), size // 2
        shares.append(lax.dynamic_slice_in_dim(live, row, half, 0))
        targets.append(lax.dynamic_slice_in_dim(target, plane * group_rows + row, half, 0))

    last = [place]

    def turn(*waits):
        return after(place, *last, *waits)

    def ran(outputs):
        last[:] = jax.tree.leaves(outputs)
        return outputs

    own, edge, corner = ([None] * n for _ in range(3))
    keep, send, mine, sends, hidden, sums, grads = ([None] * n for _ in range(7))
    losses = [None] * n

    def send_own(i):
        if groups == 4:
            edge[i] = [exchange(own[i], "grp", 1), exchange(own[i], "grp", 2)]
            return
        blocks = [own[i]]
        mask = 1
        while mask < groups:
            blocks += [exchange(block, "grp", mask) for block in blocks]
            mask *= 2
        edge[i], corner[i] = blocks[1:], []

    def send_corner(i, *copied):
        pieces = [(features, starts[j], sizes[j]) for j in copied]
        if groups == 4:
            half = sizes[i] // 2
            pieces = [(edge[i][0], 0, half), (edge[i][1], half, half)] + pieces
        if not pieces:
            return
        out = ran(copy_rows(turn(*edge[i]), pieces))
        if groups == 4:
            corner[i] = [exchange(out[0], "grp", 2), exchange(out[1], "grp", 1)]
            out = out[2:]
        for j, value in zip(copied, out):
            own[j] = value
            send_own(j)

    def multiply(i, *waits):
        parts = [own[i], *edge[i], *corner[i]]
        keep[i], send[i] = ran(forward(turn(*parts, *waits), parts, weight_here))

    def add_pair(i):
        arrived = exchange(send[i], "tp", 1)
        mine[i], out = ran(sum_pair(turn(arrived), keep[i], arrived))
        sends[i] = [exchange(value, "tp", 2 * k) for k, value in enumerate(out, 1)]

    def add_planes(i):
        hidden[i], part = ran(
            sum_planes(turn(*sends[i]), mine[i], sends[i], gain, targets[i])
        )
        sums[i] = [part] + [exchange(part, "grp", mask) for mask in range(1, groups)]

    def differentiate(i):
        grad, losses[i] = ran(
            gradient(turn(*sums[i]), hidden[i], sums[i], gain, targets[i], shares[i], all_units)
        )
        slots = [grad] + [exchange(grad, "tp", 2 * k) for k in range(1, groups)]
        grads[i] = slots + [exchange(value, "tp", 1) for value in slots]

    own[0], own[1] = ran(copy_rows(turn(), [(features, starts[j], sizes[j]) for j in (0, 1)]))
    send_own(0)
    send_own(1)
    ran([*targets, *shares])
    send_corner(0, 2)
    send_corner(1, 3)
    (weight_here,) = copy_rows(turn(), [(weight, 0, weight.shape[0])], in_vmem=(0,))
    weight_here = pltpu.with_memory_space_constraint(weight_here, pltpu.VMEM)
    multiply(0)
    add_pair(0)
    send_corner(2)
    multiply(1)
    add_pair(1)
    add_planes(0)
    send_corner(3)
    differentiate(0)
    multiply(2)
    add_pair(2)
    add_planes(1)
    multiply(3)
    add_pair(3)
    differentiate(1)
    add_planes(2)
    add_planes(3)
    differentiate(2)
    differentiate(3)
    chunks = [[own[i], *edge[i], *corner[i]] for i in range(n)]
    loss = sum(losses)
    loss = loss + exchange(loss, "tp", 1)
    loss_parts = [loss] + [exchange(loss, "tp", 2 * k) for k in range(1, groups)]
    waits = [value for pieces in grads for value in pieces]
    weight_grad = backward(turn(loss, *waits), chunks, grads)
    draft_loss = sum(loss_parts)[0, 0]
    return (weight_grad, draft_loss)


def solution(mesh):
    placed = (P("grp", "tp"), P("tp", "grp"), P("grp"), P(None, "grp"), P())
    return jax.shard_map(
        shards, mesh=mesh, in_specs=placed, out_specs=(P("tp", "grp"), P()), check_vma=False
    )
```

time: 363 us -> 281 us (0.77)
  waiting for transfers between devices: 180 us -> 80.4 us
  starting transfers between devices: 0.12 us -> 96.6 us
  Pallas kernels: 0 us -> 93.4 us
  matrix products: 67.6 us -> 0 us
  blocking collectives: 57.7 us -> 0 us
  local copies, waits for them, and re-layouts: 33.8 us -> 6.1 us
  between operations: 15.1 us -> 1.73 us
  other arithmetic: 7.01 us -> 1.96 us
    all_gather x2 -> x0, waiting for transfers between devices: 132 us -> none  [the longest x1 127 us: shards(): gathered = lax.all_gather(features, 'grp', axis=0, tiled=True)]
    ppermute x0 -> x76, starting transfers between devices: none -> 96.6 us  [exchange(): return lax.ppermute(value, axis, [(i, i ^ mask) for i in range(size)])]
    pallas_call x0 -> x23, Pallas kernels: none -> 93.4 us  [the longest x4 36.4 us: forward(): pl.pallas_call(functools.partial(forward_kernel, len(parts), tile), in_sp...]
    ppermute x0 -> x76, waiting for transfers between devices: none -> 80.4 us  [exchange(): return lax.ppermute(value, axis, [(i, i ^ mask) for i in range(size)])]
    dot_general x2 -> x0, matrix products: 67.6 us -> none  [the longest x1 34 us: shards(): jnp.dot(gathered, weight, preferred_element_type=jnp.float32)]
    psum x3 -> x0, blocking collectives: 57.7 us -> none  [the longest x1 39.9 us: shards(): draft_loss = lax.psum(partial_loss, ('grp', 'tp'))]
    reduce_scatter x1 -> x0, waiting for transfers between devices: 47.5 us -> none  [shards(): lax.psum_scatter(jnp.dot(gathered, weight, preferred_element_type=jnp.flo...]
    unnamed x5 -> x6, local copies, waits for them, and re-layouts: 32.6 us -> 3.79 us
  transfers between devices with their start and end apart: 3 -> 76, of which waited for: 3 -> 29; matrix products, arithmetic and copies ran while one was open for 1% -> 1% of each run, Pallas kernels for 0% -> 15%
where the time goes in v1:
time: 281 us; the launch traced here: 280 us
  starting transfers between devices  96.6 us (34%)
  Pallas kernels  93.4 us (33%)
  waiting for transfers between devices  80.4 us (29%)
  local copies, waits for them, and re-layouts  6.1 us (2%)
    ppermute x76, starting transfers between devices, exchange(): return lax.ppermute(value, axis, [(i, i ^ mask) for i in range(size)])  96.6 us
    ppermute x76, waiting for transfers between devices, exchange(): return lax.ppermute(value, axis, [(i, i ^ mask) for i in range(size)])  80.4 us
    pallas_call x4, Pallas kernels, forward(): pl.pallas_call(functools.partial(forward_kernel, len(parts), tile), in_sp...  36.4 us
    pallas_call x1, Pallas kernels, backward(): pl.pallas_call(functools.partial(backward_kernel, [len(p) for p in chunks...  32.7 us
    pallas_call x6, Pallas kernels, copy_rows(): pl.pallas_call(functools.partial(copy_kernel, [(start, size) for _, start...  15.2 us
  transfers between devices with their start and end apart: 76, of which 29 were waited for; matrix products, arithmetic and copies ran while one was open for 1% of the time, Pallas kernels for 15%

profile of v1, /device:TPU:0, one launch (start us, length us, event | category | flops | bytes accessed | tf_op | source)
XLA Modules:
  0.0 280.2 jit_solution(1637088969237384543)
XLA Ops:
  0.7 1.9 copy-done
  4.3 3.0 %collective-permute-start = (bf16[64,6144]{1,0:T(8,128)(2,1)}, bf16[64,6144]{1,0:T(8,128)(2,1)S(1)}, u32[]{:S(2)}, u32[]{:S(2)}) collective-permute-start(bf16[64,6144]{1,0:T(8,128)(2,1)} %get-tuple-element.78.refs_0_), channel_id=1, source_target_pairs={{0,8},{8,0},{16,24},{24,16},{1,9},{9,1},{17,25},{25,17},{2,10},{10... | collective-permute-start | bytes 2359304 | tf_op jit(solution)/shard_map/ppermute | solution.py:20
  13.6 12.3 %collective-permute-done.refs_0_.refs_1_ = bf16[64,6144]{1,0:T(8,128)(2,1)S(1)} collective-permute-done((bf16[64,6144]{1,0:T(8,128)(2,1)}, bf16[64,6144]{1,0:T(8,128)(2,1)S(1)}, u32[]{:S(2)}, u32[]{:S(2)}) %collective-permute-start) | collective-permute-done | bytes 786464 | tf_op jit(solution)/shard_map/ppermute | solution.py:20
  25.9 2.1 collective-permute-done.1.refs_1_.refs_2_
  28.3 1.9 copy-done.1
  34.8 8.0 %collective-permute-done.2.refs_0_.refs_1_.refs_6_ = bf16[64,6144]{1,0:T(8,128)(2,1)S(1)} collective-permute-done((bf16[64,6144]{1,0:T(8,128)(2,1)}, bf16[64,6144]{1,0:T(8,128)(2,1)S(1)}, u32[]{:S(2)}, u32[]{:S(2)}) %collective-permute-start.2) | collective-permute-done | bytes 786464 | tf_op jit(solution)/shard_map/ppermute | solution.py:20
  42.8 2.1 collective-permute-start.8
  45.9 8.7 %copy_rows.9.refs_5_ = bf16[6144,2048]{1,0:T(8,128)(2,1)S(1)} custom-call(s32[2]{0:T(128)S(1)} %pad_add_fusion.place_ref, bf16[6144,2048]{1,0:T(8,128)(2,1)} %refs_0_.3), custom_call_target="tpu_custom_call" | custom-call | flops 1024 | bytes 1024 | tf_op jit(solution)/shard_map/copy_rows/pallas_call | solution.py:54
  54.6 9.3 %forward.4 = (f32[4,32,2048]{2,1,0:T(8,128)S(1)}, bf16[4,32,2048]{2,1,0:T(8,128)(2,1)S(1)}) custom-call(s32[2]{0:T(128)S(1)} %pad_add_fusion.place_ref, bf16[64,6144]{1,0:T(8,128)(2,1)} %get-tuple-element.78.refs_0_, bf16[64,6144]{1,0:T(8,128)(2,1)S(1)} %collective-permute-done.refs_0_.refs_1_, bf16[64,6144]{1,0:T(8,128)(2,1)S(1)} %collective-permute-done.1.refs_1_.refs_2_, ...), custom_call_target="tpu_custom_call" | custom-call | flops 1024 | bytes 1024 | tf_op jit(solution)/shard_map/forward/pallas_call | solution.py:115
  67.3 2.0 collective-permute-start.15
  69.2 2.4 collective-permute-start.16
  73.6 2.4 collective-permute-done.10.refs_4_.refs_9_
  77.5 9.3 %forward.5 = (f32[4,32,2048]{2,1,0:T(8,128)S(1)}, bf16[4,32,2048]{2,1,0:T(8,128)(2,1)S(1)}) custom-call(s32[2]{0:T(128)S(1)} %pad_add_fusion.place_ref, bf16[64,6144]{1,0:T(8,128)(2,1)} %get-tuple-element.83.refs_0_.refs_5_, bf16[64,6144]{1,0:T(8,128)(2,1)S(1)} %collective-permute-done.2.refs_0_.refs_1_.refs_6_, ...), custom_call_target="tpu_custom_call" | custom-call | flops 1024 | bytes 1024 | tf_op jit(solution)/shard_map/forward/pallas_call | solution.py:115
  88.6 2.6 collective-permute-start.13
  91.2 4.4 %collective-permute-done.12.refs_0_ = bf16[32,2048]{1,0:T(8,128)(2,1)S(1)} collective-permute-done((bf16[32,2048]{1,0:T(8,128)(2,1)S(1)}, bf16[32,2048]{1,0:T(8,128)(2,1)S(1)}, u32[]{:S(2)}, u32[]{:S(2)}) %collective-permute-start.12) | collective-permute-done | bytes 131104 | tf_op jit(solution)/shard_map/ppermute | solution.py:20
  95.5 2.4 collective-permute-start.20
  98.4 2.5 collective-permute-start.14
  102.2 3.1 %collective-permute-done.14.refs_2_ = bf16[32,2048]{1,0:T(8,128)(2,1)S(1)} collective-permute-done((bf16[32,2048]{1,0:T(8,128)(2,1)S(1)}, bf16[32,2048]{1,0:T(8,128)(2,1)S(1)}, u32[]{:S(2)}, u32[]{:S(2)}) %collective-permute-start.14) | collective-permute-done | bytes 131104 | tf_op jit(solution)/shard_map/ppermute | solution.py:20
  107.6 2.3 collective-permute-start.18
  111.7 2.9 %collective-permute-done.19.refs_3_ = f32[32,128]{1,0:T(8,128)S(1)} collective-permute-done((f32[32,128]{1,0:T(8,128)S(1)}, f32[32,128]{1,0:T(8,128)S(1)}, u32[]{:S(2)}, u32[]{:S(2)}) %collective-permute-start.19) | collective-permute-done | bytes 16416 | tf_op jit(solution)/shard_map/ppermute | solution.py:20
  115.3 8.9 %forward.6 = (f32[4,32,2048]{2,1,0:T(8,128)S(1)}, bf16[4,32,2048]{2,1,0:T(8,128)(2,1)S(1)}) custom-call(s32[2]{0:T(128)S(1)} %pad_add_fusion.place_ref, bf16[64,6144]{1,0:T(8,128)(2,1)S(1)} %get-tuple-element.82.refs_0_.refs_10_, bf16[64,6144]{1,0:T(8,128)(2,1)S(1)} %collective-permute-done.7.refs_0_.refs_1_.refs_11_, ...), custom_call_target="tpu_custom_call" | custom-call | flops 1024 | bytes 1024 | tf_op jit(solution)/shard_map/forward/pallas_call | solution.py:115
  126.1 1.8 collective-permute-start.24
  130.0 2.2 collective-permute-done.23.refs_0_
  132.2 6.8 %collective-permute-done.24.refs_1_ = bf16[32,2048]{1,0:T(8,128)(2,1)S(1)} collective-permute-done((bf16[32,2048]{1,0:T(8,128)(2,1)}, bf16[32,2048]{1,0:T(8,128)(2,1)S(1)}, u32[]{:S(2)}, u32[]{:S(2)}) %collective-permute-start.24) | collective-permute-done | bytes 131104 | tf_op jit(solution)/shard_map/ppermute | solution.py:20
  139.8 8.9 %forward.7 = (f32[4,32,2048]{2,1,0:T(8,128)S(1)}, bf16[4,32,2048]{2,1,0:T(8,128)(2,1)S(1)}) custom-call(s32[2]{0:T(128)S(1)} %pad_add_fusion.place_ref, bf16[64,6144]{1,0:T(8,128)(2,1)S(1)} %get-tuple-element.87.refs_0_.refs_15_, bf16[64,6144]{1,0:T(8,128)(2,1)S(1)} %collective-permute-done.15.refs_0_.refs_1_.refs_16_, ...), custom_call_target="tpu_custom_call" | custom-call | flops 1024 | bytes 1024 | tf_op jit(solution)/shard_map/forward/pallas_call | solution.py:115
  148.8 2.2 collective-permute-start.45
  151.3 2.2 collective-permute-start.47
  157.2 2.0 collective-permute-start.34
  159.2 4.8 %collective-permute-done.46.refs_22_ = bf16[32,2048]{1,0:T(8,128)(2,1)S(1)} collective-permute-done((bf16[32,2048]{1,0:T(8,128)(2,1)S(1)}, bf16[32,2048]{1,0:T(8,128)(2,1)S(1)}, u32[]{:S(2)}, u32[]{:S(2)}) %collective-permute-start.46) | collective-permute-done | bytes 131104 | tf_op jit(solution)/shard_map/ppermute | solution.py:20
  164.0 1.8 collective-permute-start.29
  165.8 2.0 collective-permute-done.29.refs_1_
  167.7 1.8 collective-permute-start.30
  169.5 1.9 collective-permute-done.30.refs_2_
  171.5 2.9 %collective-permute-start.31 = (f32[32,128]{1,0:T(8,128)S(1)}, f32[32,128]{1,0:T(8,128)S(1)}, u32[]{:S(2)}, u32[]{:S(2)}) collective-permute-start(f32[32,128]{1,0:T(8,128)S(1)} %get-tuple-element.127.refs_0_), channel_id=1, source_target_pairs={{0,24},{8,16},{16,8},{24,0},{1,25},{9,17},{17,9},{25,1},{2,26},{10... | collective-permute-start | bytes 49160 | tf_op jit(solution)/shard_map/ppermute | solution.py:20
  176.1 9.2 %collective-permute-start.36 = (bf16[32,2048]{1,0:T(8,128)(2,1)S(1)}, bf16[32,2048]{1,0:T(8,128)(2,1)S(1)}, u32[]{:S(2)}, u32[]{:S(2)}) collective-permute-start(bf16[32,2048]{1,0:T(8,128)(2,1)S(1)} %get-tuple-element.134), channel_id=1, source_target_pairs={{0,4},{1,5},{2,6},{3,7},{4,0},{5,1},{6,2},{7,3},{8,12},{9,13},{10,... | collective-permute-start | bytes 393224 | tf_op jit(solution)/shard_map/ppermute | solution.py:20
  185.3 2.2 collective-permute-start.37
  189.6 1.8 collective-permute-start.38
  200.0 2.5 collective-permute-start.43
  213.7 6.2 %collective-permute-done.53.refs_30_ = bf16[32,2048]{1,0:T(8,128)(2,1)S(1)} collective-permute-done((bf16[32,2048]{1,0:T(8,128)(2,1)S(1)}, bf16[32,2048]{1,0:T(8,128)(2,1)S(1)}, u32[]{:S(2)}, u32[]{:S(2)}) %collective-permute-start.53) | collective-permute-done | bytes 131104 | tf_op jit(solution)/shard_map/ppermute | solution.py:20
  219.9 5.7 %collective-permute-start.74 = (f32[1,128]{1,0:T(1,128)S(1)}, f32[1,128]{1,0:T(1,128)S(1)}, u32[]{:S(2)}, u32[]{:S(2)}) collective-permute-start(f32[1,128]{1,0:T(1,128)S(1)} %add.92), channel_id=1, source_target_pairs={{0,4},{1,5},{2,6},{3,7},{4,0},{5,1},{6,2},{7,3},{8,12},{9,13},{10,... | collective-permute-start | bytes 1544 | tf_op jit(solution)/shard_map/ppermute | solution.py:20
  225.6 1.8 collective-permute-start.75
  227.4 2.0 collective-permute-start.61
  231.5 2.6 collective-permute-done.61.refs_39_
  234.2 2.6 collective-permute-start.67
  236.8 1.8 collective-permute-start.68
  239.1 2.1 collective-permute-done.66.refs_45_
  241.2 4.2 %collective-permute-done.67.refs_46_ = bf16[32,2048]{1,0:T(8,128)(2,1)S(1)} collective-permute-done((bf16[32,2048]{1,0:T(8,128)(2,1)S(1)}, bf16[32,2048]{1,0:T(8,128)(2,1)S(1)}, u32[]{:S(2)}, u32[]{:S(2)}) %collective-permute-start.67) | collective-permute-done | bytes 131104 | tf_op jit(solution)/shard_map/ppermute | solution.py:20
  247.5 32.7 %backward.1 = bf16[6144,2048]{1,0:T(8,128)(2,1)} custom-call(s32[2]{0:T(128)S(1)} %pad_add_fusion.place_ref, bf16[64,6144]{1,0:T(8,128)(2,1)} %get-tuple-element.78.refs_0_, bf16[64,6144]{1,0:T(8,128)(2,1)S(1)} %collective-permute-done.refs_0_.refs_1_, bf16[64,6144]{1,0:T(8,128)(2,1)S(1)} %collective-permute-done.1.refs_1_.refs_2_, ...), custom_call_target="tpu_custom_call" | custom-call | flops 25769803776 | bytes 50331648 | tf_op jit(solution)/shard_map/backward/pallas_call | solution.py:267
  (147 shorter events, 65.3 us)
Async XLA Ops:
  4.3 21.6 %collective-permute-start = (bf16[64,6144]{1,0:T(8,128)(2,1)}, bf16[64,6144]{1,0:T(8,128)(2,1)S(1)}, u32[]{:S(2)}, u32[]{:S(2)}) collective-permute-start(bf16[64,6144]{1,0:T(8,128)(2,1)} %get-tuple-element.78.refs_0_), channel_id=1, source_target_pairs={{0,8},{8,0},{16,24},{24,16},{1,9},{9,1},{17,25},{25,17},{2,10},{10... | collective-permute-start | bytes 2359304 | tf_op jit(solution)/shard_map/ppermute | solution.py:20
  7.3 20.7 %collective-permute-start.1 = (bf16[64,6144]{1,0:T(8,128)(2,1)}, bf16[64,6144]{1,0:T(8,128)(2,1)S(1)}, u32[]{:S(2)}, u32[]{:S(2)}) collective-permute-start(bf16[64,6144]{1,0:T(8,128)(2,1)} %get-tuple-element.78.refs_0_), channel_id=1, source_target_pairs={{0,16},{8,24},{16,0},{24,8},{1,17},{9,25},{17,1},{25,9},{2,18},{10... | collective-permute-start | bytes 2359304 | tf_op jit(solution)/shard_map/ppermute | solution.py:20
  8.9 33.9 %collective-permute-start.2 = (bf16[64,6144]{1,0:T(8,128)(2,1)}, bf16[64,6144]{1,0:T(8,128)(2,1)S(1)}, u32[]{:S(2)}, u32[]{:S(2)}) collective-permute-start(bf16[64,6144]{1,0:T(8,128)(2,1)} %get-tuple-element.83.refs_0_.refs_5_), channel_id=1, source_target_pairs={{0,8},{8,0},{16,24},{24,16},{1,9},{9,1},{17,25},{25,17},{2,10},{10... | collective-permute-start | bytes 2359304 | tf_op jit(solution)/shard_map/ppermute | solution.py:20
  9.4 35.5 %collective-permute-start.3 = (bf16[64,6144]{1,0:T(8,128)(2,1)}, bf16[64,6144]{1,0:T(8,128)(2,1)S(1)}, u32[]{:S(2)}, u32[]{:S(2)}) collective-permute-start(bf16[64,6144]{1,0:T(8,128)(2,1)} %get-tuple-element.83.refs_0_.refs_5_), channel_id=1, source_target_pairs={{0,16},{8,24},{16,0},{24,8},{1,17},{9,25},{17,1},{25,9},{2,18},{10... | collective-permute-start | bytes 2359304 | tf_op jit(solution)/shard_map/ppermute | solution.py:20
  31.2 23.4 %collective-permute-start.4 = (bf16[32,6144]{1,0:T(8,128)(2,1)S(1)}, bf16[32,6144]{1,0:T(8,128)(2,1)S(1)}, u32[]{:S(2)}, u32[]{:S(2)}) collective-permute-start(bf16[32,6144]{1,0:T(8,128)(2,1)S(1)} %get-tuple-element.80), channel_id=1, source_target_pairs={{0,16},{8,24},{16,0},{24,8},{1,17},{9,25},{17,1},{25,9},{2,18},{10... | collective-permute-start | bytes 1179656 | tf_op jit(solution)/shard_map/ppermute | solution.py:20
  32.8 21.8 %collective-permute-start.5 = (bf16[32,6144]{1,0:T(8,128)(2,1)S(1)}, bf16[32,6144]{1,0:T(8,128)(2,1)S(1)}, u32[]{:S(2)}, u32[]{:S(2)}) collective-permute-start(bf16[32,6144]{1,0:T(8,128)(2,1)S(1)} %get-tuple-element.81), channel_id=1, source_target_pairs={{0,8},{8,0},{16,24},{24,16},{1,9},{9,1},{17,25},{25,17},{2,10},{10... | collective-permute-start | bytes 1179656 | tf_op jit(solution)/shard_map/ppermute | solution.py:20
  33.3 33.9 %collective-permute-start.7 = (bf16[64,6144]{1,0:T(8,128)(2,1)S(1)}, bf16[64,6144]{1,0:T(8,128)(2,1)S(1)}, u32[]{:S(2)}, u32[]{:S(2)}) collective-permute-start(bf16[64,6144]{1,0:T(8,128)(2,1)S(1)} %get-tuple-element.82.refs_0_.refs_10_), channel_id=1, source_target_pairs={{0,8},{8,0},{16,24},{24,16},{1,9},{9,1},{17,25},{25,17},{2,10},{10... | collective-permute-start | bytes 2359304 | tf_op jit(solution)/shard_map/ppermute | solution.py:20
  42.8 29.5 %collective-permute-start.8 = (bf16[64,6144]{1,0:T(8,128)(2,1)S(1)}, bf16[64,6144]{1,0:T(8,128)(2,1)S(1)}, u32[]{:S(2)}, u32[]{:S(2)}) collective-permute-start(bf16[64,6144]{1,0:T(8,128)(2,1)S(1)} %get-tuple-element.82.refs_0_.refs_10_), channel_id=1, source_target_pairs={{0,16},{8,24},{16,0},{24,8},{1,17},{9,25},{17,1},{25,9},{2,18},{10... | collective-permute-start | bytes 2359304 | tf_op jit(solution)/shard_map/ppermute | solution.py:20
  64.0 12.0 %collective-permute-start.10 = (bf16[32,6144]{1,0:T(8,128)(2,1)S(1)}, bf16[32,6144]{1,0:T(8,128)(2,1)S(1)}, u32[]{:S(2)}, u32[]{:S(2)}) collective-permute-start(bf16[32,6144]{1,0:T(8,128)(2,1)S(1)} %get-tuple-element.86), channel_id=1, source_target_pairs={{0,8},{8,0},{16,24},{24,16},{1,9},{9,1},{17,25},{25,17},{2,10},{10... | collective-permute-start | bytes 1179656 | tf_op jit(solution)/shard_map/ppermute | solution.py:20
  65.6 12.0 %collective-permute-start.9 = (bf16[32,6144]{1,0:T(8,128)(2,1)S(1)}, bf16[32,6144]{1,0:T(8,128)(2,1)S(1)}, u32[]{:S(2)}, u32[]{:S(2)}) collective-permute-start(bf16[32,6144]{1,0:T(8,128)(2,1)S(1)} %get-tuple-element.85), channel_id=1, source_target_pairs={{0,16},{8,24},{16,0},{24,8},{1,17},{9,25},{17,1},{25,9},{2,18},{10... | collective-permute-start | bytes 1179656 | tf_op jit(solution)/shard_map/ppermute | solution.py:20
  67.3 40.4 %collective-permute-start.15 = (bf16[64,6144]{1,0:T(8,128)(2,1)S(1)}, bf16[64,6144]{1,0:T(8,128)(2,1)S(1)}, u32[]{:S(2)}, u32[]{:S(2)}) collective-permute-start(bf16[64,6144]{1,0:T(8,128)(2,1)S(1)} %get-tuple-element.87.refs_0_.refs_15_), channel_id=1, source_target_pairs={{0,8},{8,0},{16,24},{24,16},{1,9},{9,1},{17,25},{25,17},{2,10},{10... | collective-permute-start | bytes 2359304 | tf_op jit(solution)/shard_map/ppermute | solution.py:20
  69.2 40.7 %collective-permute-start.16 = (bf16[64,6144]{1,0:T(8,128)(2,1)S(1)}, bf16[64,6144]{1,0:T(8,128)(2,1)S(1)}, u32[]{:S(2)}, u32[]{:S(2)}) collective-permute-start(bf16[64,6144]{1,0:T(8,128)(2,1)S(1)} %get-tuple-element.87.refs_0_.refs_15_), channel_id=1, source_target_pairs={{0,16},{8,24},{16,0},{24,8},{1,17},{9,25},{17,1},{25,9},{2,18},{10... | collective-permute-start | bytes 2359304 | tf_op jit(solution)/shard_map/ppermute | solution.py:20
  86.9 11.6 %collective-permute-start.11 = (bf16[4,32,2048]{2,1,0:T(8,128)(2,1)S(1)}, bf16[4,32,2048]{2,1,0:T(8,128)(2,1)S(1)}, u32[]{:S(2)}, u32[]{:S(2)}) collective-permute-start(bf16[4,32,2048]{2,1,0:T(8,128)(2,1)S(1)} %get-tuple-element.102), channel_id=1, source_target_pairs={{0,1},{1,0},{2,3},{3,2},{4,5},{5,4},{6,7},{7,6},{8,9},{9,8},{10,11... | collective-permute-start | bytes 1572872 | tf_op jit(solution)/shard_map/ppermute | solution.py:20
  86.9 8.6 %collective-permute-start.12 = (bf16[32,2048]{1,0:T(8,128)(2,1)S(1)}, bf16[32,2048]{1,0:T(8,128)(2,1)S(1)}, u32[]{:S(2)}, u32[]{:S(2)}) collective-permute-start(bf16[32,2048]{1,0:T(8,128)(2,1)S(1)} %get-tuple-element.94), channel_id=1, source_target_pairs={{0,2},{1,3},{2,0},{3,1},{4,6},{5,7},{6,4},{7,5},{8,10},{9,11},{10,... | collective-permute-start | bytes 393224 | tf_op jit(solution)/shard_map/ppermute | solution.py:20
  88.6 9.3 %collective-permute-start.13 = (bf16[32,2048]{1,0:T(8,128)(2,1)S(1)}, bf16[32,2048]{1,0:T(8,128)(2,1)S(1)}, u32[]{:S(2)}, u32[]{:S(2)}) collective-permute-start(bf16[32,2048]{1,0:T(8,128)(2,1)S(1)} %get-tuple-element.95), channel_id=1, source_target_pairs={{0,4},{1,5},{2,6},{3,7},{4,0},{5,1},{6,2},{7,3},{8,12},{9,13},{10,... | collective-permute-start | bytes 393224 | tf_op jit(solution)/shard_map/ppermute | solution.py:20
  95.5 19.8 %collective-permute-start.20 = (bf16[32,6144]{1,0:T(8,128)(2,1)}, bf16[32,6144]{1,0:T(8,128)(2,1)S(1)}, u32[]{:S(2)}, u32[]{:S(2)}) collective-permute-start(bf16[32,6144]{1,0:T(8,128)(2,1)} %get-tuple-element.98), channel_id=1, source_target_pairs={{0,16},{8,24},{16,0},{24,8},{1,17},{9,25},{17,1},{25,9},{2,18},{10... | collective-permute-start | bytes 1179656 | tf_op jit(solution)/shard_map/ppermute | solution.py:20
  97.9 17.4 %collective-permute-start.21 = (bf16[32,6144]{1,0:T(8,128)(2,1)S(1)}, bf16[32,6144]{1,0:T(8,128)(2,1)S(1)}, u32[]{:S(2)}, u32[]{:S(2)}) collective-permute-start(bf16[32,6144]{1,0:T(8,128)(2,1)S(1)} %get-tuple-element.99), channel_id=1, source_target_pairs={{0,8},{8,0},{16,24},{24,16},{1,9},{9,1},{17,25},{25,17},{2,10},{10... | collective-permute-start | bytes 1179656 | tf_op jit(solution)/shard_map/ppermute | solution.py:20
  98.4 6.9 %collective-permute-start.14 = (bf16[32,2048]{1,0:T(8,128)(2,1)S(1)}, bf16[32,2048]{1,0:T(8,128)(2,1)S(1)}, u32[]{:S(2)}, u32[]{:S(2)}) collective-permute-start(bf16[32,2048]{1,0:T(8,128)(2,1)S(1)} %get-tuple-element.96), channel_id=1, source_target_pairs={{0,6},{1,7},{2,4},{3,5},{4,2},{5,3},{6,0},{7,1},{8,14},{9,15},{10,... | collective-permute-start | bytes 393224 | tf_op jit(solution)/shard_map/ppermute | solution.py:20
  124.3 15.4 %collective-permute-start.26 = (bf16[32,6144]{1,0:T(8,128)(2,1)}, bf16[32,6144]{1,0:T(8,128)(2,1)S(1)}, u32[]{:S(2)}, u32[]{:S(2)}) collective-permute-start(bf16[32,6144]{1,0:T(8,128)(2,1)} %get-tuple-element.112), channel_id=1, source_target_pairs={{0,16},{8,24},{16,0},{24,8},{1,17},{9,25},{17,1},{25,9},{2,18},{10... | collective-permute-start | bytes 1179656 | tf_op jit(solution)/shard_map/ppermute | solution.py:20
  124.5 15.3 %collective-permute-start.27 = (bf16[32,6144]{1,0:T(8,128)(2,1)}, bf16[32,6144]{1,0:T(8,128)(2,1)S(1)}, u32[]{:S(2)}, u32[]{:S(2)}) collective-permute-start(bf16[32,6144]{1,0:T(8,128)(2,1)} %get-tuple-element.113), channel_id=1, source_target_pairs={{0,8},{8,0},{16,24},{24,16},{1,9},{9,1},{17,25},{25,17},{2,10},{10... | collective-permute-start | bytes 1179656 | tf_op jit(solution)/shard_map/ppermute | solution.py:20
  125.0 7.2 %collective-permute-start.23 = (bf16[32,2048]{1,0:T(8,128)(2,1)}, bf16[32,2048]{1,0:T(8,128)(2,1)S(1)}, u32[]{:S(2)}, u32[]{:S(2)}) collective-permute-start(bf16[32,2048]{1,0:T(8,128)(2,1)} %get-tuple-element.105), channel_id=1, source_target_pairs={{0,2},{1,3},{2,0},{3,1},{4,6},{5,7},{6,4},{7,5},{8,10},{9,11},{10,... | collective-permute-start | bytes 393224 | tf_op jit(solution)/shard_map/ppermute | solution.py:20
  126.1 12.9 %collective-permute-start.24 = (bf16[32,2048]{1,0:T(8,128)(2,1)}, bf16[32,2048]{1,0:T(8,128)(2,1)S(1)}, u32[]{:S(2)}, u32[]{:S(2)}) collective-permute-start(bf16[32,2048]{1,0:T(8,128)(2,1)} %get-tuple-element.106), channel_id=1, source_target_pairs={{0,4},{1,5},{2,6},{3,7},{4,0},{5,1},{6,2},{7,3},{8,12},{9,13},{10,... | collective-permute-start | bytes 393224 | tf_op jit(solution)/shard_map/ppermute | solution.py:20
  127.9 11.1 %collective-permute-start.25 = (bf16[32,2048]{1,0:T(8,128)(2,1)S(1)}, bf16[32,2048]{1,0:T(8,128)(2,1)S(1)}, u32[]{:S(2)}, u32[]{:S(2)}) collective-permute-start(bf16[32,2048]{1,0:T(8,128)(2,1)S(1)} %get-tuple-element.107), channel_id=1, source_target_pairs={{0,6},{1,7},{2,4},{3,5},{4,2},{5,3},{6,0},{7,1},{8,14},{9,15},{10,... | collective-permute-start | bytes 393224 | tf_op jit(solution)/shard_map/ppermute | solution.py:20
  148.8 8.4 %collective-permute-start.45 = (bf16[32,2048]{1,0:T(8,128)(2,1)S(1)}, bf16[32,2048]{1,0:T(8,128)(2,1)S(1)}, u32[]{:S(2)}, u32[]{:S(2)}) collective-permute-start(bf16[32,2048]{1,0:T(8,128)(2,1)S(1)} %get-tuple-element.115.refs_20_), channel_id=1, source_target_pairs={{0,2},{1,3},{2,0},{3,1},{4,6},{5,7},{6,4},{7,5},{8,10},{9,11},{10,... | collective-permute-start | bytes 393224 | tf_op jit(solution)/shard_map/ppermute | solution.py:20
  151.0 12.9 %collective-permute-start.46 = (bf16[32,2048]{1,0:T(8,128)(2,1)S(1)}, bf16[32,2048]{1,0:T(8,128)(2,1)S(1)}, u32[]{:S(2)}, u32[]{:S(2)}) collective-permute-start(bf16[32,2048]{1,0:T(8,128)(2,1)S(1)} %get-tuple-element.115.refs_20_), channel_id=1, source_target_pairs={{0,4},{1,5},{2,6},{3,7},{4,0},{5,1},{6,2},{7,3},{8,12},{9,13},{10,... | collective-permute-start | bytes 393224 | tf_op jit(solution)/shard_map/ppermute | solution.py:20
  151.3 12.7 %collective-permute-start.47 = (bf16[32,2048]{1,0:T(8,128)(2,1)S(1)}, bf16[32,2048]{1,0:T(8,128)(2,1)S(1)}, u32[]{:S(2)}, u32[]{:S(2)}) collective-permute-start(bf16[32,2048]{1,0:T(8,128)(2,1)S(1)} %get-tuple-element.115.refs_20_), channel_id=1, source_target_pairs={{0,6},{1,7},{2,4},{3,5},{4,2},{5,3},{6,0},{7,1},{8,14},{9,15},{10,... | collective-permute-start | bytes 393224 | tf_op jit(solution)/shard_map/ppermute | solution.py:20
  153.5 31.8 %collective-permute-start.32 = (bf16[32,2048]{1,0:T(8,128)(2,1)S(1)}, bf16[32,2048]{1,0:T(8,128)(2,1)S(1)}, u32[]{:S(2)}, u32[]{:S(2)}) collective-permute-start(bf16[32,2048]{1,0:T(8,128)(2,1)S(1)} %get-tuple-element.122), channel_id=1, source_target_pairs={{0,2},{1,3},{2,0},{3,1},{4,6},{5,7},{6,4},{7,5},{8,10},{9,11},{10,... | collective-permute-start | bytes 393224 | tf_op jit(solution)/shard_map/ppermute | solution.py:20
  154.5 32.9 %collective-permute-start.33 = (bf16[32,2048]{1,0:T(8,128)(2,1)S(1)}, bf16[32,2048]{1,0:T(8,128)(2,1)S(1)}, u32[]{:S(2)}, u32[]{:S(2)}) collective-permute-start(bf16[32,2048]{1,0:T(8,128)(2,1)S(1)} %get-tuple-element.123), channel_id=1, source_target_pairs={{0,4},{1,5},{2,6},{3,7},{4,0},{5,1},{6,2},{7,3},{8,12},{9,13},{10,... | collective-permute-start | bytes 393224 | tf_op jit(solution)/shard_map/ppermute | solution.py:20
  157.2 30.2 %collective-permute-start.34 = (bf16[32,2048]{1,0:T(8,128)(2,1)S(1)}, bf16[32,2048]{1,0:T(8,128)(2,1)S(1)}, u32[]{:S(2)}, u32[]{:S(2)}) collective-permute-start(bf16[32,2048]{1,0:T(8,128)(2,1)S(1)} %get-tuple-element.124), channel_id=1, source_target_pairs={{0,6},{1,7},{2,4},{3,5},{4,2},{5,3},{6,0},{7,1},{8,14},{9,15},{10,... | collective-permute-start | bytes 393224 | tf_op jit(solution)/shard_map/ppermute | solution.py:20
  164.0 24.0 %collective-permute-start.35 = (bf16[32,2048]{1,0:T(8,128)(2,1)S(1)}, bf16[32,2048]{1,0:T(8,128)(2,1)S(1)}, u32[]{:S(2)}, u32[]{:S(2)}) collective-permute-start(bf16[32,2048]{1,0:T(8,128)(2,1)S(1)} %get-tuple-element.133), channel_id=1, source_target_pairs={{0,2},{1,3},{2,0},{3,1},{4,6},{5,7},{6,4},{7,5},{8,10},{9,11},{10,... | collective-permute-start | bytes 393224 | tf_op jit(solution)/shard_map/ppermute | solution.py:20
  176.1 13.4 %collective-permute-start.36 = (bf16[32,2048]{1,0:T(8,128)(2,1)S(1)}, bf16[32,2048]{1,0:T(8,128)(2,1)S(1)}, u32[]{:S(2)}, u32[]{:S(2)}) collective-permute-start(bf16[32,2048]{1,0:T(8,128)(2,1)S(1)} %get-tuple-element.134), channel_id=1, source_target_pairs={{0,4},{1,5},{2,6},{3,7},{4,0},{5,1},{6,2},{7,3},{8,12},{9,13},{10,... | collective-permute-start | bytes 393224 | tf_op jit(solution)/shard_map/ppermute | solution.py:20
  187.5 19.4 %collective-permute-start.48 = (bf16[32,2048]{1,0:T(8,128)(2,1)S(1)}, bf16[32,2048]{1,0:T(8,128)(2,1)S(1)}, u32[]{:S(2)}, u32[]{:S(2)}) collective-permute-start(bf16[32,2048]{1,0:T(8,128)(2,1)S(1)} %get-tuple-element.115.refs_20_), channel_id=1, source_target_pairs={{0,1},{1,0},{2,3},{3,2},{4,5},{5,4},{6,7},{7,6},{8,9},{9,8},{10,11... | collective-permute-start | bytes 393224 | tf_op jit(solution)/shard_map/ppermute | solution.py:20
  187.5 20.7 %collective-permute-start.49 = (bf16[32,2048]{1,0:T(8,128)(2,1)S(1)}, bf16[32,2048]{1,0:T(8,128)(2,1)S(1)}, u32[]{:S(2)}, u32[]{:S(2)}) collective-permute-start(bf16[32,2048]{1,0:T(8,128)(2,1)S(1)} %collective-permute-done.45.refs_21_), channel_id=1, source_target_pairs={{0,1},{1,0},{2,3},{3,2},{4,5},{5,4},{6,7},{7,6},{8,9},{9,8},{10,11... | collective-permute-start | bytes 393224 | tf_op jit(solution)/shard_map/ppermute | solution.py:20
  188.0 21.9 %collective-permute-start.50 = (bf16[32,2048]{1,0:T(8,128)(2,1)S(1)}, bf16[32,2048]{1,0:T(8,128)(2,1)S(1)}, u32[]{:S(2)}, u32[]{:S(2)}) collective-permute-start(bf16[32,2048]{1,0:T(8,128)(2,1)S(1)} %collective-permute-done.46.refs_22_), channel_id=1, source_target_pairs={{0,1},{1,0},{2,3},{3,2},{4,5},{5,4},{6,7},{7,6},{8,9},{9,8},{10,11... | collective-permute-start | bytes 393224 | tf_op jit(solution)/shard_map/ppermute | solution.py:20
  206.9 13.0 %collective-permute-start.53 = (bf16[32,2048]{1,0:T(8,128)(2,1)S(1)}, bf16[32,2048]{1,0:T(8,128)(2,1)S(1)}, u32[]{:S(2)}, u32[]{:S(2)}) collective-permute-start(bf16[32,2048]{1,0:T(8,128)(2,1)S(1)} %get-tuple-element.137.refs_28_), channel_id=1, source_target_pairs={{0,4},{1,5},{2,6},{3,7},{4,0},{5,1},{6,2},{7,3},{8,12},{9,13},{10,... | collective-permute-start | bytes 393224 | tf_op jit(solution)/shard_map/ppermute | solution.py:20
  208.2 11.8 %collective-permute-start.54 = (bf16[32,2048]{1,0:T(8,128)(2,1)S(1)}, bf16[32,2048]{1,0:T(8,128)(2,1)S(1)}, u32[]{:S(2)}, u32[]{:S(2)}) collective-permute-start(bf16[32,2048]{1,0:T(8,128)(2,1)S(1)} %get-tuple-element.137.refs_28_), channel_id=1, source_target_pairs={{0,6},{1,7},{2,4},{3,5},{4,2},{5,3},{6,0},{7,1},{8,14},{9,15},{10,... | collective-permute-start | bytes 393224 | tf_op jit(solution)/shard_map/ppermute | solution.py:20
  209.9 15.7 %collective-permute-start.55 = (bf16[32,2048]{1,0:T(8,128)(2,1)S(1)}, bf16[32,2048]{1,0:T(8,128)(2,1)S(1)}, u32[]{:S(2)}, u32[]{:S(2)}) collective-permute-start(bf16[32,2048]{1,0:T(8,128)(2,1)S(1)} %get-tuple-element.137.refs_28_), channel_id=1, source_target_pairs={{0,1},{1,0},{2,3},{3,2},{4,5},{5,4},{6,7},{7,6},{8,9},{9,8},{10,11... | collective-permute-start | bytes 393224 | tf_op jit(solution)/shard_map/ppermute | solution.py:20
  211.0 19.9 %collective-permute-start.59 = (bf16[32,2048]{1,0:T(8,128)(2,1)S(1)}, bf16[32,2048]{1,0:T(8,128)(2,1)S(1)}, u32[]{:S(2)}, u32[]{:S(2)}) collective-permute-start(bf16[32,2048]{1,0:T(8,128)(2,1)S(1)} %get-tuple-element.146.refs_36_), channel_id=1, source_target_pairs={{0,2},{1,3},{2,0},{3,1},{4,6},{5,7},{6,4},{7,5},{8,10},{9,11},{10,... | collective-permute-start | bytes 393224 | tf_op jit(solution)/shard_map/ppermute | solution.py:20
  212.3 19.2 %collective-permute-start.60 = (bf16[32,2048]{1,0:T(8,128)(2,1)S(1)}, bf16[32,2048]{1,0:T(8,128)(2,1)S(1)}, u32[]{:S(2)}, u32[]{:S(2)}) collective-permute-start(bf16[32,2048]{1,0:T(8,128)(2,1)S(1)} %get-tuple-element.146.refs_36_), channel_id=1, source_target_pairs={{0,4},{1,5},{2,6},{3,7},{4,0},{5,1},{6,2},{7,3},{8,12},{9,13},{10,... | collective-permute-start | bytes 393224 | tf_op jit(solution)/shard_map/ppermute | solution.py:20
  219.9 7.5 %collective-permute-start.73 = (f32[1,128]{1,0:T(1,128)S(1)}, f32[1,128]{1,0:T(1,128)S(1)}, u32[]{:S(2)}, u32[]{:S(2)}) collective-permute-start(f32[1,128]{1,0:T(1,128)S(1)} %add.92), channel_id=1, source_target_pairs={{0,2},{1,3},{2,0},{3,1},{4,6},{5,7},{6,4},{7,5},{8,10},{9,11},{10,... | collective-permute-start | bytes 1544 | tf_op jit(solution)/shard_map/ppermute | solution.py:20
  219.9 9.5 %collective-permute-start.74 = (f32[1,128]{1,0:T(1,128)S(1)}, f32[1,128]{1,0:T(1,128)S(1)}, u32[]{:S(2)}, u32[]{:S(2)}) collective-permute-start(f32[1,128]{1,0:T(1,128)S(1)} %add.92), channel_id=1, source_target_pairs={{0,4},{1,5},{2,6},{3,7},{4,0},{5,1},{6,2},{7,3},{8,12},{9,13},{10,... | collective-permute-start | bytes 1544 | tf_op jit(solution)/shard_map/ppermute | solution.py:20
  230.9 7.6 %collective-permute-start.57 = (bf16[32,2048]{1,0:T(8,128)(2,1)S(1)}, bf16[32,2048]{1,0:T(8,128)(2,1)S(1)}, u32[]{:S(2)}, u32[]{:S(2)}) collective-permute-start(bf16[32,2048]{1,0:T(8,128)(2,1)S(1)} %collective-permute-done.53.refs_30_), channel_id=1, source_target_pairs={{0,1},{1,0},{2,3},{3,2},{4,5},{5,4},{6,7},{7,6},{8,9},{9,8},{10,11... | collective-permute-start | bytes 393224 | tf_op jit(solution)/shard_map/ppermute | solution.py:20
  231.5 7.1 %collective-permute-start.58 = (bf16[32,2048]{1,0:T(8,128)(2,1)S(1)}, bf16[32,2048]{1,0:T(8,128)(2,1)S(1)}, u32[]{:S(2)}, u32[]{:S(2)}) collective-permute-start(bf16[32,2048]{1,0:T(8,128)(2,1)S(1)} %collective-permute-done.54.refs_31_), channel_id=1, source_target_pairs={{0,1},{1,0},{2,3},{3,2},{4,5},{5,4},{6,7},{7,6},{8,9},{9,8},{10,11... | collective-permute-start | bytes 393224 | tf_op jit(solution)/shard_map/ppermute | solution.py:20
  234.2 7.0 %collective-permute-start.66 = (bf16[32,2048]{1,0:T(8,128)(2,1)S(1)}, bf16[32,2048]{1,0:T(8,128)(2,1)S(1)}, u32[]{:S(2)}, u32[]{:S(2)}) collective-permute-start(bf16[32,2048]{1,0:T(8,128)(2,1)S(1)} %get-tuple-element.149.refs_44_), channel_id=1, source_target_pairs={{0,2},{1,3},{2,0},{3,1},{4,6},{5,7},{6,4},{7,5},{8,10},{9,11},{10,... | collective-permute-start | bytes 393224 | tf_op jit(solution)/shard_map/ppermute | solution.py:20
  234.2 11.2 %collective-permute-start.67 = (bf16[32,2048]{1,0:T(8,128)(2,1)S(1)}, bf16[32,2048]{1,0:T(8,128)(2,1)S(1)}, u32[]{:S(2)}, u32[]{:S(2)}) collective-permute-start(bf16[32,2048]{1,0:T(8,128)(2,1)S(1)} %get-tuple-element.149.refs_44_), channel_id=1, source_target_pairs={{0,4},{1,5},{2,6},{3,7},{4,0},{5,1},{6,2},{7,3},{8,12},{9,13},{10,... | collective-permute-start | bytes 393224 | tf_op jit(solution)/shard_map/ppermute | solution.py:20
  236.8 8.7 %collective-permute-start.68 = (bf16[32,2048]{1,0:T(8,128)(2,1)S(1)}, bf16[32,2048]{1,0:T(8,128)(2,1)S(1)}, u32[]{:S(2)}, u32[]{:S(2)}) collective-permute-start(bf16[32,2048]{1,0:T(8,128)(2,1)S(1)} %get-tuple-element.149.refs_44_), channel_id=1, source_target_pairs={{0,6},{1,7},{2,4},{3,5},{4,2},{5,3},{6,0},{7,1},{8,14},{9,15},{10,... | collective-permute-start | bytes 393224 | tf_op jit(solution)/shard_map/ppermute | solution.py:20
  238.6 7.4 %collective-permute-start.69 = (bf16[32,2048]{1,0:T(8,128)(2,1)S(1)}, bf16[32,2048]{1,0:T(8,128)(2,1)S(1)}, u32[]{:S(2)}, u32[]{:S(2)}) collective-permute-start(bf16[32,2048]{1,0:T(8,128)(2,1)S(1)} %get-tuple-element.149.refs_44_), channel_id=1, source_target_pairs={{0,1},{1,0},{2,3},{3,2},{4,5},{5,4},{6,7},{7,6},{8,9},{9,8},{10,11... | collective-permute-start | bytes 393224 | tf_op jit(solution)/shard_map/ppermute | solution.py:20
  238.6 7.4 %collective-permute-start.63 = (bf16[32,2048]{1,0:T(8,128)(2,1)S(1)}, bf16[32,2048]{1,0:T(8,128)(2,1)S(1)}, u32[]{:S(2)}, u32[]{:S(2)}) collective-permute-start(bf16[32,2048]{1,0:T(8,128)(2,1)S(1)} %collective-permute-done.59.refs_37_), channel_id=1, source_target_pairs={{0,1},{1,0},{2,3},{3,2},{4,5},{5,4},{6,7},{7,6},{8,9},{9,8},{10,11... | collective-permute-start | bytes 393224 | tf_op jit(solution)/shard_map/ppermute | solution.py:20
  (31 other events, 178.2 us)

commit v2 on v0

v2 whole, which is shorter than its diff:
```python
import functools
import jax
import jax.numpy as jnp
from jax import lax
from jax.experimental import pallas as pl
from jax.experimental.pallas import tpu as pltpu
from jax.sharding import PartitionSpec as P

SPEC = 8
epsilon = 1e-06
MIB = 2**20
ROWS = 16
PARTS = 2
HBM = pl.BlockSpec(memory_space=pltpu.HBM)
SMEM = pl.BlockSpec(memory_space=pltpu.SMEM)
VMEM = pl.BlockSpec(memory_space=pltpu.VMEM)
bf16, f32 = jnp.bfloat16, jnp.float32


def exchange(value, axis, mask):
    size = lax.axis_size(axis)
    return lax.ppermute(value, axis, [(i, i ^ mask) for i in range(size)])


def in_hbm(*arrays):
    return [pltpu.with_memory_space_constraint(array, pltpu.HBM) for array in arrays]


def after(value, *others):
    return lax.optimization_barrier((value, *others))[0]


def whole(shape):
    return pl.BlockSpec(shape, lambda _: (0,) * len(shape))


def params(mib):
    return pltpu.CompilerParams(vmem_limit_bytes=mib * MIB)


def cost(flops=1024, moved=1024):
    return pl.CostEstimate(flops=flops, bytes_accessed=moved, transcendentals=0)


def run_copies(copies):
    for copy in copies:
        copy.start()
    for copy in copies:
        copy.wait()


def copy_kernel(ranges, place_ref, *refs):
    count = len(ranges)
    sources, targets, holds, sems = refs[:count], refs[count : 2 * count], refs[2 * count : -1], refs[-1]
    into = [
        pltpu.make_async_copy(source.at[pl.ds(start, size), :], hold, sems.at[0, i])
        for i, (source, hold, (start, size)) in enumerate(zip(sources, holds, ranges))
    ]
    out = [
        pltpu.make_async_copy(hold, target, sems.at[1, i])
        for i, (hold, target) in enumerate(zip(holds, targets))
    ]
    for copy in into:
        copy.start()
    for first, second in zip(into, out):
        first.wait()
        second.start()
    for copy in out:
        copy.wait()


def copy_rows(place, pieces):
    shapes = [((size, array.shape[1]), array.dtype) for array, _, size in pieces]
    return pl.pallas_call(
        functools.partial(copy_kernel, [(start, size) for _, start, size in pieces]),
        in_specs=[SMEM] + [HBM] * len(pieces),
        out_specs=[HBM] * len(pieces),
        out_shape=[pltpu.HBM(*shape) for shape in shapes],
        scratch_shapes=[pltpu.VMEM(*shape) for shape in shapes]
        + [pltpu.SemaphoreType.DMA((2, len(pieces)))],
        compiler_params=params(12),
        cost_estimate=cost(),
        name="copy_rows",
    )(place, *in_hbm(*[array for array, _, _ in pieces]))


def load_kernel(place_ref, source_ref, target_ref, sem):
    run_copies([pltpu.make_async_copy(source_ref, target_ref, sem)])


def load(place, array):
    held = pl.pallas_call(
        load_kernel,
        in_specs=[SMEM, HBM],
        out_specs=VMEM,
        out_shape=pltpu.VMEM(array.shape, array.dtype),
        scratch_shapes=[pltpu.SemaphoreType.DMA],
        compiler_params=params(12),
        cost_estimate=cost(),
        name="load",
    )(place, *in_hbm(array))
    return pltpu.with_memory_space_constraint(held, pltpu.VMEM)


def forward_kernel(pieces, tile, place_ref, *refs):
    parts = refs[:pieces]
    weight_ref, keep_out, send_out, rows_ref, keep_ref, send_ref, sems, out_sems = refs[pieces:]
    copies = []
    start = 0
    for i, part in enumerate(parts):
        size = part.shape[0]
        copies.append(pltpu.make_async_copy(part, rows_ref.at[pl.ds(start, size), :], sems.at[i]))
        start += size
    run_copies(copies)
    shape = keep_ref.shape[:-1]
    units = keep_ref.shape[-1]
    for column in range(0, units, tile):
        columns = slice(column, column + tile)
        product = jnp.dot(
            rows_ref[...], weight_ref[:, columns], preferred_element_type=f32
        ).reshape(*shape, tile)
        keep_ref[..., columns] = product
        send_ref[..., columns] = product.astype(bf16)
    core, plane = place_ref[0], place_ref[1]
    copies = []
    for slot in range(keep_out.shape[0]):
        owner = (plane ^ slot) * 2
        copies += [
            pltpu.make_async_copy(
                keep_ref.at[:, owner + core], keep_out.at[slot], out_sems.at[0, slot]
            ),
            pltpu.make_async_copy(
                send_ref.at[:, owner + 1 - core], send_out.at[slot], out_sems.at[1, slot]
            ),
        ]
    run_copies(copies)


def forward(place, blocks, weight, slots):
    depth, units = weight.shape
    parts = [part for block in blocks for part in block]
    total_rows = sum(part.shape[0] for part in parts)
    count = len(blocks)
    tile = min(units, 512)
    scratch = (count, 2 * slots, ROWS, units)
    shape = (slots, count, ROWS, units)
    keep, send = pl.pallas_call(
        functools.partial(forward_kernel, len(parts), tile),
        in_specs=[SMEM] + [HBM] * len(parts) + [VMEM],
        out_specs=[HBM, HBM],
        out_shape=[pltpu.HBM(shape, f32), pltpu.HBM(shape, bf16)],
        scratch_shapes=[
            pltpu.VMEM((total_rows, depth), bf16),
            pltpu.VMEM(scratch, f32),
            pltpu.VMEM(scratch, bf16),
            pltpu.SemaphoreType.DMA((len(parts),)),
            pltpu.SemaphoreType.DMA((2, slots)),
        ],
        compiler_params=params(12),
        cost_estimate=cost(),
        name="forward",
    )(place, *in_hbm(*parts), weight)
    shape = (slots, count * ROWS, units)
    return keep.reshape(shape), send.reshape(shape)


def pair_kernel(count, place_ref, *refs):
    keeps, arrived = refs[:count], refs[count : 2 * count]
    own_ref, *sends = refs[2 * count :]
    start = 0
    for keep_ref, arrived_ref in zip(keeps, arrived):
        rows = pl.ds(start, keep_ref.shape[1])
        own_ref[rows, :] = keep_ref[0] + arrived_ref[0].astype(f32)
        for k, send_ref in enumerate(sends, 1):
            send_ref[rows, :] = (keep_ref[k] + arrived_ref[k].astype(f32)).astype(bf16)
        start += keep_ref.shape[1]


def sum_pair(place, events):
    keeps, arrived = zip(*events)
    slots, _, units = keeps[0].shape
    rows = sum(keep.shape[1] for keep in keeps)
    out = pl.pallas_call(
        functools.partial(pair_kernel, len(keeps)),
        grid=(1,),
        in_specs=[SMEM] + [whole(keep.shape) for keep in keeps] * 2,
        out_specs=[whole((rows, units))] * slots,
        out_shape=[jax.ShapeDtypeStruct((rows, units), f32)]
        + [jax.ShapeDtypeStruct((rows, units), bf16)] * (slots - 1),
        compiler_params=params(12),
        cost_estimate=cost(),
        name="sum_pair",
    )(place, *keeps, *arrived)
    return out[0], out[1:]


def planes_kernel(place_ref, own_ref, *refs):
    arrived, hidden_ref = refs[:-1], refs[-1]
    hidden = own_ref[...]
    for value in arrived:
        hidden = hidden + value[...].astype(f32)
    hidden_ref[...] = hidden


def sum_planes(place, own, arrived):
    return pl.pallas_call(
        planes_kernel,
        grid=(1,),
        in_specs=[SMEM] + [whole(own.shape)] * (1 + len(arrived)),
        out_specs=whole(own.shape),
        out_shape=jax.ShapeDtypeStruct(own.shape, f32),
        compiler_params=params(12),
        cost_estimate=cost(),
        name="sum_planes",
    )(place, own, *arrived)


def targets_kernel(group_rows, sets, groups, place_ref, target_ref, out_ref, hold_ref, sems):
    core, plane, group = place_ref[0], place_ref[1], place_ref[2]
    span = group_rows // sets
    copies = []
    for i in range(sets):
        for block in range(groups):
            row = (group ^ block) * group_rows + i * span + (plane * 2 + core) * ROWS
            copies.append(
                pltpu.make_async_copy(
                    target_ref.at[pl.ds(pl.multiple_of(row, ROWS), ROWS), :],
                    hold_ref.at[pl.ds((i * groups + block) * ROWS, ROWS), :],
                    sems.at[i * groups + block],
                )
            )
    run_copies(copies)
    run_copies([pltpu.make_async_copy(hold_ref, out_ref, sems.at[sets * groups])])


def take_targets(place, target, group_rows, sets, groups):
    shape = (sets * groups * ROWS, target.shape[1])
    return pl.pallas_call(
        functools.partial(targets_kernel, group_rows, sets, groups),
        in_specs=[SMEM, HBM],
        out_specs=HBM,
        out_shape=pltpu.HBM(shape, bf16),
        scratch_shapes=[
            pltpu.VMEM(shape, bf16),
            pltpu.SemaphoreType.DMA((sets * groups + 1,)),
        ],
        compiler_params=params(12),
        cost_estimate=cost(),
        name="take_targets",
    )(place, *in_hbm(target))


def rows_kernel(ranges, late, place_ref, gain_ref, target_ref, *refs):
    early, (own_ref, *arrived), (hidden_ref, sums_ref) = (
        refs[: len(ranges)],
        refs[len(ranges) : len(ranges) + 1 + late],
        refs[-2:],
    )
    last = own_ref[...]
    for value in arrived:
        last = last + value[...].astype(f32)
    parts = [ref[start : start + size, :] for ref, (start, size) in zip(early, ranges)]
    hidden = jnp.concatenate(parts + [last], axis=0)
    hidden_ref[...] = hidden
    scaled = hidden * gain_ref[...]
    target = target_ref[...].astype(f32)
    lane = lax.broadcasted_iota(jnp.int32, sums_ref.shape, 1)
    sums = jnp.zeros(sums_ref.shape, f32)
    terms = (hidden * hidden, scaled * scaled, scaled * target, target * target)
    for i, term in enumerate(terms):
        sums = jnp.where(lane == i, jnp.sum(term, axis=1, keepdims=True), sums)
    sums_ref[...] = sums


def sum_rows(place, early, own, arrived, gain, target):
    rows, units = target.shape
    return pl.pallas_call(
        functools.partial(rows_kernel, [(b, c) for _, b, c in early], len(arrived)),
        grid=(1,),
        in_specs=[SMEM, whole(gain.shape), whole(target.shape)]
        + [whole(array.shape) for array, _, _ in early]
        + [whole(own.shape)] * (1 + len(arrived)),
        out_specs=[whole((rows, units)), whole((rows, 128))],
        out_shape=[
            jax.ShapeDtypeStruct((rows, units), f32),
            jax.ShapeDtypeStruct((rows, 128), f32),
        ],
        compiler_params=params(12),
        cost_estimate=cost(),
        name="sum_rows",
    )(place, gain, target, *[array for array, _, _ in early], own, *arrived)


def gradient_kernel(all_units, place_ref, hidden_ref, gain_ref, target_ref, share_ref, *refs):
    all_sums, grads = refs[:-PARTS], refs[-PARTS:]
    rows = hidden_ref.shape[0]
    sums = jnp.concatenate(
        [
            sum(ref[(block ^ k) * ROWS : ((block ^ k) + 1) * ROWS, :] for k, ref in enumerate(all_sums))
            for block in range(rows // ROWS)
        ],
        axis=0,
    )
    squares, scaled_squares = sums[:, 0:1], sums[:, 1:2]
    products, target_squares = sums[:, 2:3], sums[:, 3:4]
    share = share_ref[:, 0:1]
    inverse_rms = lax.rsqrt(squares / all_units + epsilon)
    coupling = share * (inverse_rms * scaled_squares - products)
    loss = inverse_rms * (inverse_rms * scaled_squares - 2.0 * products) + target_squares
    loss = jnp.broadcast_to(jnp.sum(0.5 * share * loss, axis=0, keepdims=True), (loss.shape[0], 128))
    first = loss.astype(bf16)
    second = (loss - first.astype(f32)).astype(bf16)
    third = (loss - first.astype(f32) - second.astype(f32)).astype(bf16)
    lane = lax.broadcasted_iota(jnp.int32, loss.shape, 1)
    third = jnp.where(lane == 2, third.astype(f32), 0.0)
    loss = jnp.where(lane == 1, second.astype(f32), third)
    loss = jnp.where(lane == 0, first.astype(f32), loss).astype(bf16)
    hidden = hidden_ref[...]
    gain = gain_ref[...]
    residual = share * (hidden * inverse_rms * gain - target_ref[...].astype(f32))
    grad = inverse_rms * gain * residual - hidden * (inverse_rms**3 * coupling / all_units)
    width = hidden.shape[1] // PARTS
    for i, grad_ref in enumerate(grads):
        grad_ref[:, :width] = grad[:, i * width : (i + 1) * width].astype(bf16)
        if i == 0:
            grad_ref[:, width:] = loss


def gradient(place, hidden, all_sums, gain, target, share, all_units):
    rows, units = hidden.shape
    shapes = [(rows, units // PARTS + (128 if i == 0 else 0)) for i in range(PARTS)]
    return pl.pallas_call(
        functools.partial(gradient_kernel, all_units),
        grid=(1,),
        in_specs=[SMEM, whole(hidden.shape), whole(gain.shape), whole(hidden.shape)]
        + [whole((rows, 128))] * (1 + len(all_sums)),
        out_specs=[whole(shape) for shape in shapes],
        out_shape=[jax.ShapeDtypeStruct(shape, bf16) for shape in shapes],
        compiler_params=params(12),
        cost_estimate=cost(),
        name="gradient",
    )(place, hidden, gain, target, share, *all_sums)


def piece_copies(place_ref, pieces, target, sems):
    core, plane = place_ref[0], place_ref[1]
    slots = len(pieces) // 2
    copies = []
    for i, piece in enumerate(pieces):
        owner = (plane ^ (i % slots)) * 2 + (core if i < slots else 1 - core)
        copies.append(
            pltpu.make_async_copy(piece, target.at[:, owner], sems.at[i])
        )
    return copies


def by_block(pieces):
    return in_hbm(*[piece.reshape(piece.shape[0] // ROWS, ROWS, -1) for piece in pieces])


def backward_kernel(part_count, piece_count, place_ref, *refs):
    parts, refs = refs[:part_count], refs[part_count:]
    pieces, refs = refs[:piece_count], refs[piece_count:]
    rows_ref, sems = refs[-2:]
    out_ref, *loss = refs[-4:-2] if refs[-3].shape[-1] == 128 else refs[-3:-2]
    units = out_ref.shape[-1]

    @pl.when(pl.program_id(0) == 0)
    def _():
        run_copies(piece_copies(place_ref, pieces, rows_ref, sems))
        for loss_ref in loss:
            total = jnp.zeros(loss_ref.shape, f32)
            for owner in range(rows_ref.shape[1]):
                total += rows_ref[0, owner, :, units:].astype(f32)
            loss_ref[...] = total

    left = jnp.concatenate([part[...] for part in parts], axis=0)
    out_ref[...] = lax.dot_general(
        left,
        rows_ref[..., :units].reshape(left.shape[0], units),
        (((0,), (0,)), ((), ())),
        preferred_element_type=f32,
    ).astype(bf16)


def backward(place, parts, pieces, index, units, result=None):
    depth = parts[0].shape[1]
    tile = min(depth, 1024)
    width = units // PARTS
    blocks = pieces[0].shape[0] // ROWS
    operands = [place, *in_hbm(*parts), *by_block(pieces)]
    first = result is None
    out = pl.pallas_call(
        functools.partial(backward_kernel, len(parts), len(pieces)),
        grid=(depth // tile,),
        in_specs=[SMEM]
        + [pl.BlockSpec((part.shape[0], tile), lambda k: (0, k)) for part in parts]
        + [HBM] * (len(pieces) + (not first)),
        out_specs=[pl.BlockSpec((tile, width), lambda k: (k, index))]
        + [pl.BlockSpec((ROWS, 128), lambda k: (0, 0))] * first,
        out_shape=[jax.ShapeDtypeStruct((depth, units), bf16)]
        + [jax.ShapeDtypeStruct((ROWS, 128), f32)] * first,
        scratch_shapes=[
            pltpu.VMEM((blocks, len(pieces), ROWS, pieces[0].shape[1]), bf16),
            pltpu.SemaphoreType.DMA((len(pieces),)),
        ],
        input_output_aliases={} if first else {len(operands): 0},
        compiler_params=params(24),
        cost_estimate=cost(),
        name="backward",
    )(*operands, *([] if first else [result]))
    return out if first else [out[0], None]


def shards(features, weight, norm_gain, target, counts):
    groups, tp = lax.axis_size("grp"), lax.axis_size("tp")
    group, place_tp = lax.axis_index("grp"), lax.axis_index("tp")
    core, plane = place_tp % 2, place_tp // 2
    slots = tp // 2
    place = jnp.stack([core, plane, group]).astype(jnp.int32)
    group_rows = features.shape[0]
    all_units = norm_gain.shape[0] * groups
    gain = norm_gain[None, :]
    span = ROWS * tp
    sets = range(group_rows // span)

    accepted = jnp.sum(counts).astype(f32)
    blocks = group ^ jnp.arange(groups, dtype=jnp.int32)
    index = (
        jnp.arange(len(sets), dtype=jnp.int32)[:, None, None] * span
        + blocks[None, :, None] * group_rows
        + (plane * 2 + core) * ROWS
        + jnp.arange(ROWS, dtype=jnp.int32)[None, None, :]
    ).reshape(len(sets), groups * ROWS)
    live = (index % SPEC < jnp.take(counts, index // SPEC)).astype(f32) / accepted
    share = jnp.broadcast_to(live.reshape(-1, 1), (live.size, 128))

    last = [place]

    def turn(*waits):
        return after(place, *last, *waits)

    def ran(outputs):
        last[:] = jax.tree.leaves(outputs)
        return outputs

    own = ran(copy_rows(turn(), [(features, i * span, span) for i in sets]))
    block_rows = [{0: [own[i]]} for i in sets]
    for i in sets:
        if groups == 4:
            block_rows[i][1] = [exchange(own[i], "grp", 1)]
            block_rows[i][2] = [exchange(own[i], "grp", 2)]
        else:
            mask = 1
            while mask < groups:
                for block in range(mask):
                    block_rows[i][block ^ mask] = [exchange(block_rows[i][block][0], "grp", mask)]
                mask *= 2

    def send_corner(i):
        (first,), (second,) = block_rows[i][1], block_rows[i][2]
        half = span // 2
        low, high = ran(copy_rows(turn(first, second), [(first, 0, half), (second, half, half)]))
        block_rows[i][3] = [exchange(low, "grp", 2), exchange(high, "grp", 1)]

    def multiply(pieces):
        rows = [block_rows[i][block] for i, block in pieces]
        keep, send = ran(
            forward(turn(*[part for parts in rows for part in parts]), rows, weight_here, slots)
        )
        return keep, exchange(send, "tp", 1)

    def add_pair(*events):
        own_sum, out = ran(sum_pair(turn(*[arrived for _, arrived in events]), events))
        return own_sum, [exchange(value, "tp", 2 * k) for k, value in enumerate(out, 1)]

    def add_planes(own_sum, arrived):
        return ran(sum_planes(turn(*arrived), own_sum, arrived))

    def add_rows(early, own_sum, arrived):
        hidden, part = ran(sum_rows(turn(*arrived), early, own_sum, arrived, gain, targets))
        return hidden, [part] + [exchange(part, "grp", mask) for mask in range(1, groups)]

    def differentiate(hidden, sums):
        return ran(gradient(turn(*sums), hidden, sums, gain, targets, share, all_units))

    def spread(grad, *waits):
        grad = after(grad, *waits)
        return [grad] + [exchange(grad, "tp", 2 * k) for k in range(1, slots)]

    def spread_pair(pieces, *waits):
        return pieces + [exchange(after(value, *waits), "tp", 1) for value in pieces]

    weight_here = load(turn(), weight)
    targets = ran(take_targets(turn(share), target, group_rows, len(sets), groups))
    own_pair = multiply([(i, 0) for i in sets])
    own_planes = add_pair(own_pair)
    if groups == 4 and len(sets) == 2:
        send_corner(0)
        edge0 = multiply([(0, 1), (0, 2)])
        own_hidden = add_planes(*own_planes)
        edge0 = add_pair(edge0)
        send_corner(1)
        edge1 = multiply([(1, 1), (1, 2)])
        hidden0 = add_planes(*edge0)
        corner0 = multiply([(0, 3)])
        late1 = add_pair(edge1, corner0)
        corner1 = add_pair(multiply([(1, 3)]))
        hidden1 = add_planes(*late1)
        early = [
            (own_hidden, 0, ROWS),
            (hidden0, 0, 2 * ROWS),
            (hidden1, 2 * ROWS, ROWS),
            (own_hidden, ROWS, ROWS),
            (hidden1, 0, 2 * ROWS),
        ]
        rows = add_rows(early, *corner1)
    else:
        own_hidden = add_planes(*own_planes)
        early = []
        for i in sets:
            early.append((own_hidden, i * ROWS, ROWS))
            for block in range(1, groups):
                pair = add_pair(multiply([(i, block)]))
                if (i, block) != (sets[-1], groups - 1):
                    early.append((add_planes(*pair), 0, ROWS))
        rows = add_rows(early, *pair)
    grads = differentiate(*rows)
    parts = [part for i in sets for block in range(groups) for part in block_rows[i][block]]
    planes = []
    for grad in grads:
        planes.append(spread(grad, *[pieces[1] for pieces in planes[-1:]]))
    result = loss = None
    for i, pieces in enumerate(planes):
        pieces = spread_pair(pieces, *([] if i == 0 else [loss]))
        result, total = backward(turn(*pieces), parts, pieces, i, gain.shape[1], result)
        loss = total if i == 0 else loss
        ran(loss)
    return (result, jnp.sum(loss[0]))


def solution(mesh):
    placed = (P("grp", "tp"), P("tp", "grp"), P("grp"), P(None, "grp"), P())
    return jax.shard_map(
        shards, mesh=mesh, in_specs=placed, out_specs=(P("tp", "grp"), P()), check_vma=False
    )
```

time: 363 us -> 232 us (0.64)
  waiting for transfers between devices: 180 us -> 61.3 us
  Pallas kernels: 0 us -> 110 us
  matrix products: 67.6 us -> 0 us
  blocking collectives: 57.7 us -> 0 us
  starting transfers between devices: 0.12 us -> 44.1 us
  local copies, waits for them, and re-layouts: 33.8 us -> 12.1 us
  between operations: 15.1 us -> 2.07 us
  other arithmetic: 7.01 us -> 1.44 us
    all_gather x2 -> x0, waiting for transfers between devices: 132 us -> none  [the longest x1 127 us: shards(): gathered = lax.all_gather(features, 'grp', axis=0, tiled=True)]
    pallas_call x0 -> x21, Pallas kernels: none -> 110 us  [the longest x5 44.6 us: forward(): pl.pallas_call(functools.partial(forward_kernel, len(parts), tile), in_sp...]
    dot_general x2 -> x0, matrix products: 67.6 us -> none  [the longest x1 34 us: shards(): jnp.dot(gathered, weight, preferred_element_type=jnp.float32)]
    ppermute x0 -> x42, waiting for transfers between devices: none -> 61.3 us  [exchange(): return lax.ppermute(value, axis, [(i, i ^ mask) for i in range(size)])]
    psum x3 -> x0, blocking collectives: 57.7 us -> none  [the longest x1 39.9 us: shards(): draft_loss = lax.psum(partial_loss, ('grp', 'tp'))]
    reduce_scatter x1 -> x0, waiting for transfers between devices: 47.5 us -> none  [shards(): lax.psum_scatter(jnp.dot(gathered, weight, preferred_element_type=jnp.flo...]
    ppermute x0 -> x42, starting transfers between devices: none -> 44.1 us  [exchange(): return lax.ppermute(value, axis, [(i, i ^ mask) for i in range(size)])]
    unnamed x5 -> x64, local copies, waits for them, and re-layouts: 32.6 us -> 10.2 us
  transfers between devices with their start and end apart: 3 -> 42, of which waited for: 3 -> 18; matrix products, arithmetic and copies ran while one was open for 1% -> 1% of each run, Pallas kernels for 0% -> 34%
where the time goes in v2:
time: 232 us; the launch traced here: 231 us
  Pallas kernels  110 us (47%)
  waiting for transfers between devices  61.3 us (26%)
  starting transfers between devices  44.1 us (19%)
  local copies, waits for them, and re-layouts  12.1 us (5%)
    ppermute x42, waiting for transfers between devices, exchange(): return lax.ppermute(value, axis, [(i, i ^ mask) for i in range(size)])  61.3 us
    pallas_call x5, Pallas kernels, forward(): pl.pallas_call(functools.partial(forward_kernel, len(parts), tile), in_sp...  44.6 us
    ppermute x42, starting transfers between devices, exchange(): return lax.ppermute(value, axis, [(i, i ^ mask) for i in range(size)])  44.1 us
    pallas_call x2, Pallas kernels, backward(): pl.pallas_call(functools.partial(backward_kernel, len(parts), len(pieces)...  38.4 us
    unnamed x64, local copies, waits for them, and re-layouts  10.2 us
    pallas_call x3, Pallas kernels, copy_rows(): pl.pallas_call(functools.partial(copy_kernel, [(start, size) for _, start...  9.4 us
    pallas_call x1, Pallas kernels, load(): pl.pallas_call(load_kernel, in_specs=[SMEM, HBM], out_specs=VMEM, out_sha...  8.71 us
  transfers between devices with their start and end apart: 42, of which 18 were waited for; matrix products, arithmetic and copies ran while one was open for 1% of the time, Pallas kernels for 34%

profile of v2, /device:TPU:0, one launch (start us, length us, event | category | flops | bytes accessed | tf_op | source)
XLA Modules:
  0.0 231.4 jit_solution(17812353649229165924)
XLA Ops:
  0.7 3.6 %copy_rows.3 = (bf16[128,6144]{1,0:T(8,128)(2,1)}, bf16[128,6144]{1,0:T(8,128)(2,1)}) custom-call(s32[3]{0:T(128)S(1)} %pad_add_fusion.place_ref, bf16[256,6144]{1,0:T(8,128)(2,1)} %refs_1_.1, bf16[256,6144]{1,0:T(8,128)(2,1)} %refs_1_.1), custom_call_target="tpu_custom_call" | custom-call | flops 1024 | bytes 1024 | tf_op jit(solution)/shard_map/copy_rows/pallas_call | solution.py:74
  4.4 3.0 %collective-permute-start.2 = (bf16[128,6144]{1,0:T(8,128)(2,1)}, bf16[128,6144]{1,0:T(8,128)(2,1)S(1)}, u32[]{:S(2)}, u32[]{:S(2)}) collective-permute-start(bf16[128,6144]{1,0:T(8,128)(2,1)} %get-tuple-element.67.refs_0_), channel_id=1, source_target_pairs={{0,16},{8,24},{16,0},{24,8},{1,17},{9,25},{17,1},{25,9},{2,18},{10... | collective-permute-start | bytes 4718600 | tf_op jit(solution)/shard_map/ppermute | solution.py:22
  7.4 1.5 collective-permute-start.1
  11.5 1.2 gather_fusion
  12.9 2.5 %take_targets.1.target_ref = bf16[128,2048]{1,0:T(8,128)(2,1)} custom-call(s32[3]{0:T(128)S(1)} %pad_add_fusion.place_ref, bf16[1024,2048]{1,0:T(8,128)(2,1)} %target_ref.1), custom_call_target="tpu_custom_call" | custom-call | flops 1024 | bytes 1024 | tf_op jit(solution)/shard_map/take_targets/pallas_call | solution.py:238
  15.4 8.7 %load.1.refs_2_ = bf16[6144,2048]{1,0:T(8,128)(2,1)S(1)} custom-call(s32[3]{0:T(128)S(1)} %pad_add_fusion.place_ref, bf16[6144,2048]{1,0:T(8,128)(2,1)} %source_ref.1), custom_call_target="tpu_custom_call" | custom-call | flops 1024 | bytes 1024 | tf_op jit(solution)/shard_map/load/pallas_call | solution.py:92
  24.1 10.5 %forward.5 = (f32[4,2,16,2048]{3,2,1,0:T(8,128)}, bf16[4,2,16,2048]{3,2,1,0:T(8,128)(2,1)}) custom-call(s32[3]{0:T(128)S(1)} %pad_add_fusion.place_ref, bf16[128,6144]{1,0:T(8,128)(2,1)} %get-tuple-element.67.refs_0_, bf16[128,6144]{1,0:T(8,128)(2,1)} %get-tuple-element.68.refs_1_.refs_5_, bf16[6144,2048]{1,0:T(8,128)(2,1)S(1)} %load.1.refs_2_), custom_call_target="tpu_custom_call" | custom-call | flops 1024 | bytes 1024 | tf_op jit(solution)/shard_map/forward/pallas_call | solution.py:147
  34.7 2.1 collective-permute-done.refs_1_
  36.8 1.2 copy-done.3
  38.6 4.2 %collective-permute-done.2.refs_1_.refs_2_ = bf16[128,6144]{1,0:T(8,128)(2,1)S(1)} collective-permute-done((bf16[128,6144]{1,0:T(8,128)(2,1)}, bf16[128,6144]{1,0:T(8,128)(2,1)S(1)}, u32[]{:S(2)}, u32[]{:S(2)}) %collective-permute-start.2) | collective-permute-done | bytes 1572896 | tf_op jit(solution)/shard_map/ppermute | solution.py:22
  42.8 2.1 collective-permute-done.1.refs_0_.refs_1_
  44.9 1.2 copy-done.11
  46.2 2.8 %copy_rows.4 = (bf16[64,6144]{1,0:T(8,128)(2,1)}, bf16[64,6144]{1,0:T(8,128)(2,1)}) custom-call(s32[3]{0:T(128)S(1)} %pad_add_fusion.place_ref, bf16[128,6144]{1,0:T(8,128)(2,1)} %copy-done.11, bf16[128,6144]{1,0:T(8,128)(2,1)} %copy-done.10), custom_call_target="tpu_custom_call" | custom-call | flops 1024 | bytes 1024 | tf_op jit(solution)/shard_map/copy_rows/pallas_call | solution.py:74
  49.0 10.5 %forward.6 = (f32[4,2,16,2048]{3,2,1,0:T(8,128)}, bf16[4,2,16,2048]{3,2,1,0:T(8,128)(2,1)}) custom-call(s32[3]{0:T(128)S(1)} %pad_add_fusion.place_ref, bf16[128,6144]{1,0:T(8,128)(2,1)} %copy-done.11, bf16[128,6144]{1,0:T(8,128)(2,1)} %copy-done.10, bf16[6144,2048]{1,0:T(8,128)(2,1)S(1)} %load.1.refs_2_), custom_call_target="tpu_custom_call" | custom-call | flops 1024 | bytes 1024 | tf_op jit(solution)/shard_map/forward/pallas_call | solution.py:147
  59.6 1.6 collective-permute-start.3
  61.2 2.6 %collective-permute-start.4 = (bf16[32,2048]{1,0:T(8,128)(2,1)S(1)}, bf16[32,2048]{1,0:T(8,128)(2,1)S(1)}, u32[]{:S(2)}, u32[]{:S(2)}) collective-permute-start(bf16[32,2048]{1,0:T(8,128)(2,1)S(1)} %get-tuple-element.77), channel_id=1, source_target_pairs={{0,4},{1,5},{2,6},{3,7},{4,0},{5,1},{6,2},{7,3},{8,12},{9,13},{10,... | collective-permute-start | bytes 393224 | tf_op jit(solution)/shard_map/ppermute | solution.py:22
  63.8 4.4 %collective-permute-done.3.refs_0_ = bf16[32,2048]{1,0:T(8,128)(2,1)S(1)} collective-permute-done((bf16[32,2048]{1,0:T(8,128)(2,1)S(1)}, bf16[32,2048]{1,0:T(8,128)(2,1)S(1)}, u32[]{:S(2)}, u32[]{:S(2)}) %collective-permute-start.3) | collective-permute-done | bytes 131104 | tf_op jit(solution)/shard_map/ppermute | solution.py:22
  68.2 2.5 %collective-permute-start.5 = (bf16[32,2048]{1,0:T(8,128)(2,1)S(1)}, bf16[32,2048]{1,0:T(8,128)(2,1)S(1)}, u32[]{:S(2)}, u32[]{:S(2)}) collective-permute-start(bf16[32,2048]{1,0:T(8,128)(2,1)S(1)} %get-tuple-element.78), channel_id=1, source_target_pairs={{0,6},{1,7},{2,4},{3,5},{4,2},{5,3},{6,0},{7,1},{8,14},{9,15},{10,... | collective-permute-start | bytes 393224 | tf_op jit(solution)/shard_map/ppermute | solution.py:22
  71.2 3.8 %collective-permute-done.5.refs_2_ = bf16[32,2048]{1,0:T(8,128)(2,1)S(1)} collective-permute-done((bf16[32,2048]{1,0:T(8,128)(2,1)S(1)}, bf16[32,2048]{1,0:T(8,128)(2,1)S(1)}, u32[]{:S(2)}, u32[]{:S(2)}) %collective-permute-start.5) | collective-permute-done | bytes 131104 | tf_op jit(solution)/shard_map/ppermute | solution.py:22
  75.0 1.5 collective-permute-start.13
  79.0 1.8 collective-permute-start.9
  80.8 1.6 collective-permute-start.10
  82.3 2.9 %copy_rows.5 = (bf16[64,6144]{1,0:T(8,128)(2,1)}, bf16[64,6144]{1,0:T(8,128)(2,1)}) custom-call(s32[3]{0:T(128)S(1)} %pad_add_fusion.place_ref, bf16[128,6144]{1,0:T(8,128)(2,1)} %collective-permute-done.7.refs_0_.refs_6_, bf16[128,6144]{1,0:T(8,128)(2,1)} %collective-permute-done.8.refs_1_.refs_7_), custom_call_target="tpu_custom_call" | custom-call | flops 1024 | bytes 1024 | tf_op jit(solution)/shard_map/copy_rows/pallas_call | solution.py:74
  86.4 3.1 %collective-permute-done.10.refs_1_ = bf16[32,2048]{1,0:T(8,128)(2,1)S(1)} collective-permute-done((bf16[32,2048]{1,0:T(8,128)(2,1)S(1)}, bf16[32,2048]{1,0:T(8,128)(2,1)S(1)}, u32[]{:S(2)}, u32[]{:S(2)}) %collective-permute-start.10) | collective-permute-done | bytes 131104 | tf_op jit(solution)/shard_map/ppermute | solution.py:22
  89.5 2.0 collective-permute-start.11
  91.4 10.7 %forward.7 = (f32[4,2,16,2048]{3,2,1,0:T(8,128)}, bf16[4,2,16,2048]{3,2,1,0:T(8,128)(2,1)}) custom-call(s32[3]{0:T(128)S(1)} %pad_add_fusion.place_ref, bf16[128,6144]{1,0:T(8,128)(2,1)} %collective-permute-done.7.refs_0_.refs_6_, bf16[128,6144]{1,0:T(8,128)(2,1)} %collective-permute-done.8.refs_1_.refs_7_, bf16[6144,2048]{1,0:T(8,128)(2,1)S(1)} %load.1.refs_2_), custom_call_target="tpu_custom_call" | custom-call | flops 1024 | bytes 1024 | tf_op jit(solution)/shard_map/forward/pallas_call | solution.py:147
  104.6 6.5 %forward.8 = (f32[4,1,16,2048]{3,2,1,0:T(8,128)}, bf16[4,1,16,2048]{3,2,1,0:T(8,128)(2,1)}) custom-call(s32[3]{0:T(128)S(1)} %pad_add_fusion.place_ref, bf16[64,6144]{1,0:T(8,128)(2,1)} %copy-done.12, bf16[64,6144]{1,0:T(8,128)(2,1)} %copy-done.13, bf16[6144,2048]{1,0:T(8,128)(2,1)S(1)} %load.1.refs_2_), custom_call_target="tpu_custom_call" | custom-call | flops 1024 | bytes 1024 | tf_op jit(solution)/shard_map/forward/pallas_call | solution.py:147
  111.7 1.4 collective-permute-done.15.refs_3_
  116.1 6.5 %forward.9 = (f32[4,1,16,2048]{3,2,1,0:T(8,128)}, bf16[4,1,16,2048]{3,2,1,0:T(8,128)(2,1)}) custom-call(s32[3]{0:T(128)S(1)} %pad_add_fusion.place_ref, bf16[64,6144]{1,0:T(8,128)(2,1)} %copy-done.14, bf16[64,6144]{1,0:T(8,128)(2,1)} %copy-done.15, bf16[6144,2048]{1,0:T(8,128)(2,1)S(1)} %load.1.refs_2_), custom_call_target="tpu_custom_call" | custom-call | flops 1024 | bytes 1024 | tf_op jit(solution)/shard_map/forward/pallas_call | solution.py:147
  123.0 2.4 %collective-permute-start.20 = (bf16[48,2048]{1,0:T(8,128)(2,1)S(1)}, bf16[48,2048]{1,0:T(8,128)(2,1)S(1)}, u32[]{:S(2)}, u32[]{:S(2)}) collective-permute-start(bf16[48,2048]{1,0:T(8,128)(2,1)S(1)} %get-tuple-element.104), channel_id=1, source_target_pairs={{0,4},{1,5},{2,6},{3,7},{4,0},{5,1},{6,2},{7,3},{8,12},{9,13},{10,... | collective-permute-start | bytes 589832 | tf_op jit(solution)/shard_map/ppermute | solution.py:22
  125.4 2.0 collective-permute-start.21
  129.1 2.4 %collective-permute-start.23 = (bf16[16,2048]{1,0:T(8,128)(2,1)S(1)}, bf16[16,2048]{1,0:T(8,128)(2,1)S(1)}, u32[]{:S(2)}, u32[]{:S(2)}) collective-permute-start(bf16[16,2048]{1,0:T(8,128)(2,1)S(1)} %get-tuple-element.112), channel_id=1, source_target_pairs={{0,4},{1,5},{2,6},{3,7},{4,0},{5,1},{6,2},{7,3},{8,12},{9,13},{10,... | collective-permute-start | bytes 196616 | tf_op jit(solution)/shard_map/ppermute | solution.py:22
  131.5 2.8 %collective-permute-done.19.refs_0_ = bf16[48,2048]{1,0:T(8,128)(2,1)S(1)} collective-permute-done((bf16[48,2048]{1,0:T(8,128)(2,1)S(1)}, bf16[48,2048]{1,0:T(8,128)(2,1)S(1)}, u32[]{:S(2)}, u32[]{:S(2)}) %collective-permute-start.19) | collective-permute-done | bytes 196640 | tf_op jit(solution)/shard_map/ppermute | solution.py:22
  134.3 1.9 collective-permute-start.24
  136.1 6.8 %collective-permute-done.20.refs_1_ = bf16[48,2048]{1,0:T(8,128)(2,1)S(1)} collective-permute-done((bf16[48,2048]{1,0:T(8,128)(2,1)S(1)}, bf16[48,2048]{1,0:T(8,128)(2,1)S(1)}, u32[]{:S(2)}, u32[]{:S(2)}) %collective-permute-start.20) | collective-permute-done | bytes 196640 | tf_op jit(solution)/shard_map/ppermute | solution.py:22
  143.6 4.9 %collective-permute-done.23.refs_7_ = bf16[16,2048]{1,0:T(8,128)(2,1)S(1)} collective-permute-done((bf16[16,2048]{1,0:T(8,128)(2,1)S(1)}, bf16[16,2048]{1,0:T(8,128)(2,1)S(1)}, u32[]{:S(2)}, u32[]{:S(2)}) %collective-permute-start.23) | collective-permute-done | bytes 65568 | tf_op jit(solution)/shard_map/ppermute | solution.py:22
  150.1 1.5 collective-permute-start.26
  151.6 1.5 collective-permute-start.25
  153.1 1.8 collective-permute-done.27.refs_3_
  155.8 1.3 gradient.1
  157.2 1.9 collective-permute-start.30
  159.9 1.7 collective-permute-start.28
  161.6 7.4 %collective-permute-done.30 = bf16[128,1152]{1,0:T(8,128)(2,1)S(1)} collective-permute-done((bf16[128,1152]{1,0:T(8,128)(2,1)S(1)}, bf16[128,1152]{1,0:T(8,128)(2,1)S(1)}, u32[]{:S(2)}, u32[]{:S(2)}) %collective-permute-start.30) | collective-permute-done | bytes 294944 | tf_op jit(solution)/shard_map/ppermute | solution.py:22
  169.0 14.5 %collective-permute-done.29 = bf16[128,1152]{1,0:T(8,128)(2,1)S(1)} collective-permute-done((bf16[128,1152]{1,0:T(8,128)(2,1)S(1)}, bf16[128,1152]{1,0:T(8,128)(2,1)S(1)}, u32[]{:S(2)}, u32[]{:S(2)}) %collective-permute-start.29) | collective-permute-done | bytes 294944 | tf_op jit(solution)/shard_map/ppermute | solution.py:22
  184.0 1.9 collective-permute-start.37
  185.9 2.5 %collective-permute-start.35 = (bf16[128,1024]{1,0:T(8,128)(2,1)S(1)}, bf16[128,1024]{1,0:T(8,128)(2,1)S(1)}, u32[]{:S(2)}, u32[]{:S(2)}) collective-permute-start(bf16[128,1024]{1,0:T(8,128)(2,1)S(1)} %get-tuple-element.124), channel_id=1, source_target_pairs={{0,2},{1,3},{2,0},{3,1},{4,6},{5,7},{6,4},{7,5},{8,10},{9,11},{10,... | collective-permute-start | bytes 786440 | tf_op jit(solution)/shard_map/ppermute | solution.py:22
  189.3 19.2 %backward.2 = (bf16[6144,2048]{1,0:T(8,128)(2,1)}, f32[16,128]{1,0:T(8,128)S(1)}) custom-call(s32[3]{0:T(128)S(1)} %pad_add_fusion.place_ref, bf16[128,6144]{1,0:T(8,128)(2,1)} %get-tuple-element.67.refs_0_, bf16[128,6144]{1,0:T(8,128)(2,1)} %copy-done.11, bf16[128,6144]{1,0:T(8,128)(2,1)} %copy-done.10, bf16[64,6144]{1,0:T(8,128)(2,1)} %copy-done.12, ...), custom_call_target="tpu_custom_call" | custom-call | flops 1024 | bytes 1024 | tf_op jit(solution)/shard_map/backward/pallas_call | solution.py:393
  212.0 19.2 %backward.3 = bf16[6144,2048]{1,0:T(8,128)(2,1)} custom-call(s32[3]{0:T(128)S(1)} %pad_add_fusion.place_ref, bf16[128,6144]{1,0:T(8,128)(2,1)} %get-tuple-element.67.refs_0_, bf16[128,6144]{1,0:T(8,128)(2,1)} %copy-done.11, bf16[128,6144]{1,0:T(8,128)(2,1)} %copy-done.10, bf16[64,6144]{1,0:T(8,128)(2,1)} %copy-done.12, ...), custom_call_target="tpu_custom_call", output_to_operand_aliasing={{}: (19, {})} | custom-call | flops 1024 | bytes 1024 | tf_op jit(solution)/shard_map/backward/pallas_call | solution.py:393
  (142 shorter events, 23.9 us)
Async XLA Ops:
  4.4 38.5 %collective-permute-start.2 = (bf16[128,6144]{1,0:T(8,128)(2,1)}, bf16[128,6144]{1,0:T(8,128)(2,1)S(1)}, u32[]{:S(2)}, u32[]{:S(2)}) collective-permute-start(bf16[128,6144]{1,0:T(8,128)(2,1)} %get-tuple-element.67.refs_0_), channel_id=1, source_target_pairs={{0,16},{8,24},{16,0},{24,8},{1,17},{9,25},{17,1},{25,9},{2,18},{10... | collective-permute-start | bytes 4718600 | tf_op jit(solution)/shard_map/ppermute | solution.py:22
  7.4 37.5 %collective-permute-start.1 = (bf16[128,6144]{1,0:T(8,128)(2,1)}, bf16[128,6144]{1,0:T(8,128)(2,1)S(1)}, u32[]{:S(2)}, u32[]{:S(2)}) collective-permute-start(bf16[128,6144]{1,0:T(8,128)(2,1)} %get-tuple-element.67.refs_0_), channel_id=1, source_target_pairs={{0,8},{8,0},{16,24},{24,16},{1,9},{9,1},{17,25},{25,17},{2,10},{10... | collective-permute-start | bytes 4718600 | tf_op jit(solution)/shard_map/ppermute | solution.py:22
  8.9 71.9 %collective-permute-start.8 = (bf16[128,6144]{1,0:T(8,128)(2,1)}, bf16[128,6144]{1,0:T(8,128)(2,1)}, u32[]{:S(2)}, u32[]{:S(2)}) collective-permute-start(bf16[128,6144]{1,0:T(8,128)(2,1)} %get-tuple-element.68.refs_1_.refs_5_), channel_id=1, source_target_pairs={{0,16},{8,24},{16,0},{24,8},{1,17},{9,25},{17,1},{25,9},{2,18},{10... | collective-permute-start | bytes 4718600 | tf_op jit(solution)/shard_map/ppermute | solution.py:22
  9.4 72.9 %collective-permute-start.7 = (bf16[128,6144]{1,0:T(8,128)(2,1)}, bf16[128,6144]{1,0:T(8,128)(2,1)}, u32[]{:S(2)}, u32[]{:S(2)}) collective-permute-start(bf16[128,6144]{1,0:T(8,128)(2,1)} %get-tuple-element.68.refs_1_.refs_5_), channel_id=1, source_target_pairs={{0,8},{8,0},{16,24},{24,16},{1,9},{9,1},{17,25},{25,17},{2,10},{10... | collective-permute-start | bytes 4718600 | tf_op jit(solution)/shard_map/ppermute | solution.py:22
  34.6 2.2 collective-permute-start
  49.0 21.7 %copy-start.31 = (bf16[64,6144]{1,0:T(8,128)(2,1)S(1)}, bf16[64,6144]{1,0:T(8,128)(2,1)}, u32[]{:S(2)}) copy-start(bf16[64,6144]{1,0:T(8,128)(2,1)} %get-tuple-element.80) | copy-start | bytes 2359300
  49.0 26.0 %copy-start.30 = (bf16[64,6144]{1,0:T(8,128)(2,1)S(1)}, bf16[64,6144]{1,0:T(8,128)(2,1)}, u32[]{:S(2)}) copy-start(bf16[64,6144]{1,0:T(8,128)(2,1)} %get-tuple-element.81) | copy-start | bytes 2359300
  59.5 17.6 %collective-permute-start.6 = (bf16[4,32,2048]{2,1,0:T(8,128)(2,1)}, bf16[4,32,2048]{2,1,0:T(8,128)(2,1)S(1)}, u32[]{:S(2)}, u32[]{:S(2)}) collective-permute-start(bf16[4,32,2048]{2,1,0:T(8,128)(2,1)} %bitcast.57), channel_id=1, source_target_pairs={{0,1},{1,0},{2,3},{3,2},{4,5},{5,4},{6,7},{7,6},{8,9},{9,8},{10,11... | collective-permute-start | bytes 1572872 | tf_op jit(solution)/shard_map/ppermute | solution.py:22
  59.6 8.6 %collective-permute-start.3 = (bf16[32,2048]{1,0:T(8,128)(2,1)S(1)}, bf16[32,2048]{1,0:T(8,128)(2,1)S(1)}, u32[]{:S(2)}, u32[]{:S(2)}) collective-permute-start(bf16[32,2048]{1,0:T(8,128)(2,1)S(1)} %get-tuple-element.76), channel_id=1, source_target_pairs={{0,2},{1,3},{2,0},{3,1},{4,6},{5,7},{6,4},{7,5},{8,10},{9,11},{10,... | collective-permute-start | bytes 393224 | tf_op jit(solution)/shard_map/ppermute | solution.py:22
  61.2 9.4 %collective-permute-start.4 = (bf16[32,2048]{1,0:T(8,128)(2,1)S(1)}, bf16[32,2048]{1,0:T(8,128)(2,1)S(1)}, u32[]{:S(2)}, u32[]{:S(2)}) collective-permute-start(bf16[32,2048]{1,0:T(8,128)(2,1)S(1)} %get-tuple-element.77), channel_id=1, source_target_pairs={{0,4},{1,5},{2,6},{3,7},{4,0},{5,1},{6,2},{7,3},{8,12},{9,13},{10,... | collective-permute-start | bytes 393224 | tf_op jit(solution)/shard_map/ppermute | solution.py:22
  68.2 6.8 %collective-permute-start.5 = (bf16[32,2048]{1,0:T(8,128)(2,1)S(1)}, bf16[32,2048]{1,0:T(8,128)(2,1)S(1)}, u32[]{:S(2)}, u32[]{:S(2)}) collective-permute-start(bf16[32,2048]{1,0:T(8,128)(2,1)S(1)} %get-tuple-element.78), channel_id=1, source_target_pairs={{0,6},{1,7},{2,4},{3,5},{4,2},{5,3},{6,0},{7,1},{8,14},{9,15},{10,... | collective-permute-start | bytes 393224 | tf_op jit(solution)/shard_map/ppermute | solution.py:22
  70.7 32.2 %collective-permute-start.12 = (bf16[64,6144]{1,0:T(8,128)(2,1)S(1)}, bf16[64,6144]{1,0:T(8,128)(2,1)S(1)}, u32[]{:S(2)}, u32[]{:S(2)}) collective-permute-start(bf16[64,6144]{1,0:T(8,128)(2,1)S(1)} %copy-done.31), channel_id=1, source_target_pairs={{0,16},{8,24},{16,0},{24,8},{1,17},{9,25},{17,1},{25,9},{2,18},{10... | collective-permute-start | bytes 2359304 | tf_op jit(solution)/shard_map/ppermute | solution.py:22
  75.0 27.8 %collective-permute-start.13 = (bf16[64,6144]{1,0:T(8,128)(2,1)S(1)}, bf16[64,6144]{1,0:T(8,128)(2,1)S(1)}, u32[]{:S(2)}, u32[]{:S(2)}) collective-permute-start(bf16[64,6144]{1,0:T(8,128)(2,1)S(1)} %copy-done.30), channel_id=1, source_target_pairs={{0,8},{8,0},{16,24},{24,16},{1,9},{9,1},{17,25},{25,17},{2,10},{10... | collective-permute-start | bytes 2359304 | tf_op jit(solution)/shard_map/ppermute | solution.py:22
  79.0 6.9 %collective-permute-start.9 = (bf16[32,2048]{1,0:T(8,128)(2,1)S(1)}, bf16[32,2048]{1,0:T(8,128)(2,1)S(1)}, u32[]{:S(2)}, u32[]{:S(2)}) collective-permute-start(bf16[32,2048]{1,0:T(8,128)(2,1)S(1)} %get-tuple-element.88), channel_id=1, source_target_pairs={{0,2},{1,3},{2,0},{3,1},{4,6},{5,7},{6,4},{7,5},{8,10},{9,11},{10,... | collective-permute-start | bytes 393224 | tf_op jit(solution)/shard_map/ppermute | solution.py:22
  80.8 8.7 %collective-permute-start.10 = (bf16[32,2048]{1,0:T(8,128)(2,1)S(1)}, bf16[32,2048]{1,0:T(8,128)(2,1)S(1)}, u32[]{:S(2)}, u32[]{:S(2)}) collective-permute-start(bf16[32,2048]{1,0:T(8,128)(2,1)S(1)} %get-tuple-element.89), channel_id=1, source_target_pairs={{0,4},{1,5},{2,6},{3,7},{4,0},{5,1},{6,2},{7,3},{8,12},{9,13},{10,... | collective-permute-start | bytes 393224 | tf_op jit(solution)/shard_map/ppermute | solution.py:22
  85.3 29.5 %collective-permute-start.16 = (bf16[64,6144]{1,0:T(8,128)(2,1)}, bf16[64,6144]{1,0:T(8,128)(2,1)S(1)}, u32[]{:S(2)}, u32[]{:S(2)}) collective-permute-start(bf16[64,6144]{1,0:T(8,128)(2,1)} %get-tuple-element.92), channel_id=1, source_target_pairs={{0,16},{8,24},{16,0},{24,8},{1,17},{9,25},{17,1},{25,9},{2,18},{10... | collective-permute-start | bytes 2359304 | tf_op jit(solution)/shard_map/ppermute | solution.py:22
  85.9 29.0 %collective-permute-start.17 = (bf16[64,6144]{1,0:T(8,128)(2,1)}, bf16[64,6144]{1,0:T(8,128)(2,1)S(1)}, u32[]{:S(2)}, u32[]{:S(2)}) collective-permute-start(bf16[64,6144]{1,0:T(8,128)(2,1)} %get-tuple-element.93), channel_id=1, source_target_pairs={{0,8},{8,0},{16,24},{24,16},{1,9},{9,1},{17,25},{25,17},{2,10},{10... | collective-permute-start | bytes 2359304 | tf_op jit(solution)/shard_map/ppermute | solution.py:22
  89.5 12.6 %collective-permute-start.11 = (bf16[32,2048]{1,0:T(8,128)(2,1)S(1)}, bf16[32,2048]{1,0:T(8,128)(2,1)S(1)}, u32[]{:S(2)}, u32[]{:S(2)}) collective-permute-start(bf16[32,2048]{1,0:T(8,128)(2,1)S(1)} %get-tuple-element.90), channel_id=1, source_target_pairs={{0,6},{1,7},{2,4},{3,5},{4,2},{5,3},{6,0},{7,1},{8,14},{9,15},{10,... | collective-permute-start | bytes 393224 | tf_op jit(solution)/shard_map/ppermute | solution.py:22
  102.1 9.6 %collective-permute-start.14 = (bf16[4,32,2048]{2,1,0:T(8,128)(2,1)}, bf16[4,32,2048]{2,1,0:T(8,128)(2,1)S(1)}, u32[]{:S(2)}, u32[]{:S(2)}) collective-permute-start(bf16[4,32,2048]{2,1,0:T(8,128)(2,1)} %bitcast.58), channel_id=1, source_target_pairs={{0,1},{1,0},{2,3},{3,2},{4,5},{5,4},{6,7},{7,6},{8,9},{9,8},{10,11... | collective-permute-start | bytes 1572872 | tf_op jit(solution)/shard_map/ppermute | solution.py:22
  111.1 1.9 collective-permute-start.15
  116.1 32.4 %copy-start = (bf16[128,2048]{1,0:T(8,128)(2,1)S(1)}, bf16[128,2048]{1,0:T(8,128)(2,1)}, u32[]{:S(2)}) copy-start(bf16[128,2048]{1,0:T(8,128)(2,1)} %take_targets.1.target_ref) | copy-start | bytes 1572868
  116.1 32.4 %copy-start.8 = (f32[2048]{0:T(1024)S(1)}, f32[2048]{0:T(1024)}, u32[]{:S(2)}) copy-start(f32[2048]{0:T(1024)} %param.7) | copy-start | bytes 24580
  122.5 4.8 %collective-permute-start.18 = (bf16[4,16,2048]{2,1,0:T(8,128)(2,1)}, bf16[4,16,2048]{2,1,0:T(8,128)(2,1)S(1)}, u32[]{:S(2)}, u32[]{:S(2)}) collective-permute-start(bf16[4,16,2048]{2,1,0:T(8,128)(2,1)} %bitcast.60), channel_id=1, source_target_pairs={{0,1},{1,0},{2,3},{3,2},{4,5},{5,4},{6,7},{7,6},{8,9},{9,8},{10,11... | collective-permute-start | bytes 786440 | tf_op jit(solution)/shard_map/ppermute | solution.py:22
  123.0 11.3 %collective-permute-start.19 = (bf16[48,2048]{1,0:T(8,128)(2,1)S(1)}, bf16[48,2048]{1,0:T(8,128)(2,1)S(1)}, u32[]{:S(2)}, u32[]{:S(2)}) collective-permute-start(bf16[48,2048]{1,0:T(8,128)(2,1)S(1)} %get-tuple-element.103), channel_id=1, source_target_pairs={{0,2},{1,3},{2,0},{3,1},{4,6},{5,7},{6,4},{7,5},{8,10},{9,11},{10,... | collective-permute-start | bytes 589832 | tf_op jit(solution)/shard_map/ppermute | solution.py:22
  123.0 20.0 %collective-permute-start.20 = (bf16[48,2048]{1,0:T(8,128)(2,1)S(1)}, bf16[48,2048]{1,0:T(8,128)(2,1)S(1)}, u32[]{:S(2)}, u32[]{:S(2)}) collective-permute-start(bf16[48,2048]{1,0:T(8,128)(2,1)S(1)} %get-tuple-element.104), channel_id=1, source_target_pairs={{0,4},{1,5},{2,6},{3,7},{4,0},{5,1},{6,2},{7,3},{8,12},{9,13},{10,... | collective-permute-start | bytes 589832 | tf_op jit(solution)/shard_map/ppermute | solution.py:22
  125.4 17.6 %collective-permute-start.21 = (bf16[48,2048]{1,0:T(8,128)(2,1)S(1)}, bf16[48,2048]{1,0:T(8,128)(2,1)S(1)}, u32[]{:S(2)}, u32[]{:S(2)}) collective-permute-start(bf16[48,2048]{1,0:T(8,128)(2,1)S(1)} %get-tuple-element.105), channel_id=1, source_target_pairs={{0,6},{1,7},{2,4},{3,5},{4,2},{5,3},{6,0},{7,1},{8,14},{9,15},{10,... | collective-permute-start | bytes 589832 | tf_op jit(solution)/shard_map/ppermute | solution.py:22
  129.0 14.6 %collective-permute-start.22 = (bf16[16,2048]{1,0:T(8,128)(2,1)S(1)}, bf16[16,2048]{1,0:T(8,128)(2,1)S(1)}, u32[]{:S(2)}, u32[]{:S(2)}) collective-permute-start(bf16[16,2048]{1,0:T(8,128)(2,1)S(1)} %get-tuple-element.111), channel_id=1, source_target_pairs={{0,2},{1,3},{2,0},{3,1},{4,6},{5,7},{6,4},{7,5},{8,10},{9,11},{10,... | collective-permute-start | bytes 196616 | tf_op jit(solution)/shard_map/ppermute | solution.py:22
  129.1 19.4 %collective-permute-start.23 = (bf16[16,2048]{1,0:T(8,128)(2,1)S(1)}, bf16[16,2048]{1,0:T(8,128)(2,1)S(1)}, u32[]{:S(2)}, u32[]{:S(2)}) collective-permute-start(bf16[16,2048]{1,0:T(8,128)(2,1)S(1)} %get-tuple-element.112), channel_id=1, source_target_pairs={{0,4},{1,5},{2,6},{3,7},{4,0},{5,1},{6,2},{7,3},{8,12},{9,13},{10,... | collective-permute-start | bytes 196616 | tf_op jit(solution)/shard_map/ppermute | solution.py:22
  134.3 14.2 %collective-permute-start.24 = (bf16[16,2048]{1,0:T(8,128)(2,1)S(1)}, bf16[16,2048]{1,0:T(8,128)(2,1)S(1)}, u32[]{:S(2)}, u32[]{:S(2)}) collective-permute-start(bf16[16,2048]{1,0:T(8,128)(2,1)S(1)} %get-tuple-element.113), channel_id=1, source_target_pairs={{0,6},{1,7},{2,4},{3,5},{4,2},{5,3},{6,0},{7,1},{8,14},{9,15},{10,... | collective-permute-start | bytes 196616 | tf_op jit(solution)/shard_map/ppermute | solution.py:22
  149.5 5.3 %collective-permute-start.27 = (f32[128,128]{1,0:T(8,128)S(1)}, f32[128,128]{1,0:T(8,128)S(1)}, u32[]{:S(2)}, u32[]{:S(2)}) collective-permute-start(f32[128,128]{1,0:T(8,128)S(1)} %get-tuple-element.117.refs_0_), channel_id=1, source_target_pairs={{0,24},{8,16},{16,8},{24,0},{1,25},{9,17},{17,9},{25,1},{2,26},{10... | collective-permute-start | bytes 196616 | tf_op jit(solution)/shard_map/ppermute | solution.py:22
  150.1 5.0 %collective-permute-start.26 = (f32[128,128]{1,0:T(8,128)S(1)}, f32[128,128]{1,0:T(8,128)S(1)}, u32[]{:S(2)}, u32[]{:S(2)}) collective-permute-start(f32[128,128]{1,0:T(8,128)S(1)} %get-tuple-element.117.refs_0_), channel_id=1, source_target_pairs={{0,16},{8,24},{16,0},{24,8},{1,17},{9,25},{17,1},{25,9},{2,18},{10... | collective-permute-start | bytes 196616 | tf_op jit(solution)/shard_map/ppermute | solution.py:22
  151.6 4.3 %collective-permute-start.25 = (f32[128,128]{1,0:T(8,128)S(1)}, f32[128,128]{1,0:T(8,128)S(1)}, u32[]{:S(2)}, u32[]{:S(2)}) collective-permute-start(f32[128,128]{1,0:T(8,128)S(1)} %get-tuple-element.117.refs_0_), channel_id=1, source_target_pairs={{0,8},{8,0},{16,24},{24,16},{1,9},{9,1},{17,25},{25,17},{2,10},{10... | collective-permute-start | bytes 196616 | tf_op jit(solution)/shard_map/ppermute | solution.py:22
  157.1 31.3 %copy-start.6 = (bf16[128,1152]{1,0:T(8,128)(2,1)}, bf16[128,1152]{1,0:T(8,128)(2,1)S(1)}, u32[]{:S(2)}) copy-start(bf16[128,1152]{1,0:T(8,128)(2,1)S(1)} %get-tuple-element.119) | copy-start | bytes 884740
  157.1 51.4 %copy-start.7 = (bf16[128,1024]{1,0:T(8,128)(2,1)}, bf16[128,1024]{1,0:T(8,128)(2,1)S(1)}, u32[]{:S(2)}) copy-start(bf16[128,1024]{1,0:T(8,128)(2,1)S(1)} %get-tuple-element.124) | copy-start | bytes 786436
  157.2 11.8 %collective-permute-start.30 = (bf16[128,1152]{1,0:T(8,128)(2,1)S(1)}, bf16[128,1152]{1,0:T(8,128)(2,1)S(1)}, u32[]{:S(2)}, u32[]{:S(2)}) collective-permute-start(bf16[128,1152]{1,0:T(8,128)(2,1)S(1)} %get-tuple-element.119), channel_id=1, source_target_pairs={{0,6},{1,7},{2,4},{3,5},{4,2},{5,3},{6,0},{7,1},{8,14},{9,15},{10,... | collective-permute-start | bytes 884744 | tf_op jit(solution)/shard_map/ppermute | solution.py:22
  159.1 24.4 %collective-permute-start.29 = (bf16[128,1152]{1,0:T(8,128)(2,1)S(1)}, bf16[128,1152]{1,0:T(8,128)(2,1)S(1)}, u32[]{:S(2)}, u32[]{:S(2)}) collective-permute-start(bf16[128,1152]{1,0:T(8,128)(2,1)S(1)} %get-tuple-element.119), channel_id=1, source_target_pairs={{0,4},{1,5},{2,6},{3,7},{4,0},{5,1},{6,2},{7,3},{8,12},{9,13},{10,... | collective-permute-start | bytes 884744 | tf_op jit(solution)/shard_map/ppermute | solution.py:22
  159.9 23.6 %collective-permute-start.28 = (bf16[128,1152]{1,0:T(8,128)(2,1)S(1)}, bf16[128,1152]{1,0:T(8,128)(2,1)S(1)}, u32[]{:S(2)}, u32[]{:S(2)}) collective-permute-start(bf16[128,1152]{1,0:T(8,128)(2,1)S(1)} %get-tuple-element.119), channel_id=1, source_target_pairs={{0,2},{1,3},{2,0},{3,1},{4,6},{5,7},{6,4},{7,5},{8,10},{9,11},{10,... | collective-permute-start | bytes 884744 | tf_op jit(solution)/shard_map/ppermute | solution.py:22
  161.6 24.3 %collective-permute-start.31 = (bf16[128,1152]{1,0:T(8,128)(2,1)S(1)}, bf16[128,1152]{1,0:T(8,128)(2,1)S(1)}, u32[]{:S(2)}, u32[]{:S(2)}) collective-permute-start(bf16[128,1152]{1,0:T(8,128)(2,1)S(1)} %get-tuple-element.119), channel_id=1, source_target_pairs={{0,1},{1,0},{2,3},{3,2},{4,5},{5,4},{6,7},{7,6},{8,9},{9,8},{10,11... | collective-permute-start | bytes 884744 | tf_op jit(solution)/shard_map/ppermute | solution.py:22
  169.0 17.0 %collective-permute-start.34 = (bf16[128,1152]{1,0:T(8,128)(2,1)S(1)}, bf16[128,1152]{1,0:T(8,128)(2,1)S(1)}, u32[]{:S(2)}, u32[]{:S(2)}) collective-permute-start(bf16[128,1152]{1,0:T(8,128)(2,1)S(1)} %collective-permute-done.30), channel_id=1, source_target_pairs={{0,1},{1,0},{2,3},{3,2},{4,5},{5,4},{6,7},{7,6},{8,9},{9,8},{10,11... | collective-permute-start | bytes 884744 | tf_op jit(solution)/shard_map/ppermute | solution.py:22
  183.5 4.9 %collective-permute-start.33 = (bf16[128,1152]{1,0:T(8,128)(2,1)S(1)}, bf16[128,1152]{1,0:T(8,128)(2,1)S(1)}, u32[]{:S(2)}, u32[]{:S(2)}) collective-permute-start(bf16[128,1152]{1,0:T(8,128)(2,1)S(1)} %collective-permute-done.29), channel_id=1, source_target_pairs={{0,1},{1,0},{2,3},{3,2},{4,5},{5,4},{6,7},{7,6},{8,9},{9,8},{10,11... | collective-permute-start | bytes 884744 | tf_op jit(solution)/shard_map/ppermute | solution.py:22
  183.5 4.9 %collective-permute-start.32 = (bf16[128,1152]{1,0:T(8,128)(2,1)S(1)}, bf16[128,1152]{1,0:T(8,128)(2,1)S(1)}, u32[]{:S(2)}, u32[]{:S(2)}) collective-permute-start(bf16[128,1152]{1,0:T(8,128)(2,1)S(1)} %collective-permute-done.28), channel_id=1, source_target_pairs={{0,1},{1,0},{2,3},{3,2},{4,5},{5,4},{6,7},{7,6},{8,9},{9,8},{10,11... | collective-permute-start | bytes 884744 | tf_op jit(solution)/shard_map/ppermute | solution.py:22
  184.0 24.4 %collective-permute-start.37 = (bf16[128,1024]{1,0:T(8,128)(2,1)S(1)}, bf16[128,1024]{1,0:T(8,128)(2,1)S(1)}, u32[]{:S(2)}, u32[]{:S(2)}) collective-permute-start(bf16[128,1024]{1,0:T(8,128)(2,1)S(1)} %get-tuple-element.124), channel_id=1, source_target_pairs={{0,6},{1,7},{2,4},{3,5},{4,2},{5,3},{6,0},{7,1},{8,14},{9,15},{10,... | collective-permute-start | bytes 786440 | tf_op jit(solution)/shard_map/ppermute | solution.py:22
  185.9 22.6 %collective-permute-start.36 = (bf16[128,1024]{1,0:T(8,128)(2,1)S(1)}, bf16[128,1024]{1,0:T(8,128)(2,1)S(1)}, u32[]{:S(2)}, u32[]{:S(2)}) collective-permute-start(bf16[128,1024]{1,0:T(8,128)(2,1)S(1)} %get-tuple-element.124), channel_id=1, source_target_pairs={{0,4},{1,5},{2,6},{3,7},{4,0},{5,1},{6,2},{7,3},{8,12},{9,13},{10,... | collective-permute-start | bytes 786440 | tf_op jit(solution)/shard_map/ppermute | solution.py:22
  185.9 22.6 %collective-permute-start.35 = (bf16[128,1024]{1,0:T(8,128)(2,1)S(1)}, bf16[128,1024]{1,0:T(8,128)(2,1)S(1)}, u32[]{:S(2)}, u32[]{:S(2)}) collective-permute-start(bf16[128,1024]{1,0:T(8,128)(2,1)S(1)} %get-tuple-element.124), channel_id=1, source_target_pairs={{0,2},{1,3},{2,0},{3,1},{4,6},{5,7},{6,4},{7,5},{8,10},{9,11},{10,... | collective-permute-start | bytes 786440 | tf_op jit(solution)/shard_map/ppermute | solution.py:22
  208.5 1.7 collective-permute-start.38
  208.6 1.9 collective-permute-start.39
  209.1 1.8 collective-permute-start.40
  209.2 2.1 collective-permute-start.41
  (26 other events, 78.9 us)

commit v3 on v2

--- a/solution.py
+++ b/solution.py
@@ -251,16 +251,16 @@
 
 
 def rows_kernel(ranges, late, place_ref, gain_ref, target_ref, *refs):
-    early, (own_ref, *arrived), (hidden_ref, sums_ref) = (
-        refs[: len(ranges)],
-        refs[len(ranges) : len(ranges) + 1 + late],
-        refs[-2:],
-    )
+    own_ref, *arrived = refs[: 1 + late]
+    early, (hidden_ref, sums_ref) = list(refs[1 + late : -2]), refs[-2:]
     last = own_ref[...]
     for value in arrived:
         last = last + value[...].astype(f32)
-    parts = [ref[start : start + size, :] for ref, (start, size) in zip(early, ranges)]
-    hidden = jnp.concatenate(parts + [last], axis=0)
+    parts = []
+    for is_early, start, size in ranges:
+        part = early.pop(0)[...] if is_early else last
+        parts.append(part[start : start + size, :])
+    hidden = jnp.concatenate(parts, axis=0)
     hidden_ref[...] = hidden
     scaled = hidden * gain_ref[...]
     target = target_ref[...].astype(f32)
@@ -272,14 +272,16 @@
     sums_ref[...] = sums
 
 
-def sum_rows(place, early, own, arrived, gain, target):
+def sum_rows(place, parts, own, arrived, gain, target):
     rows, units = target.shape
+    early = [array for array, _, _ in parts if array is not None]
+    ranges = [(array is not None, start, size) for array, start, size in parts]
     return pl.pallas_call(
-        functools.partial(rows_kernel, [(b, c) for _, b, c in early], len(arrived)),
+        functools.partial(rows_kernel, ranges, len(arrived)),
         grid=(1,),
         in_specs=[SMEM, whole(gain.shape), whole(target.shape)]
-        + [whole(array.shape) for array, _, _ in early]
-        + [whole(own.shape)] * (1 + len(arrived)),
+        + [whole(own.shape)] * (1 + len(arrived))
+        + [whole(array.shape) for array in early],
         out_specs=[whole((rows, units)), whole((rows, 128))],
         out_shape=[
             jax.ShapeDtypeStruct((rows, units), f32),
@@ -288,7 +290,7 @@
         compiler_params=params(12),
         cost_estimate=cost(),
         name="sum_rows",
-    )(place, gain, target, *[array for array, _, _ in early], own, *arrived)
+    )(place, gain, target, own, *arrived, *early)
 
 
 def gradient_kernel(all_units, place_ref, hidden_ref, gain_ref, target_ref, share_ref, *refs):
@@ -468,9 +470,10 @@
         keep, send = ran(
             forward(turn(*[part for parts in rows for part in parts]), rows, weight_here, slots)
         )
-        return keep, exchange(send, "tp", 1)
+        return keep, send
 
     def add_pair(*events):
+        events = [(keep, exchange(after(send, *last), "tp", 1)) for keep, send in events]
         own_sum, out = ran(sum_pair(turn(*[arrived for _, arrived in events]), events))
         return own_sum, [exchange(value, "tp", 2 * k) for k, value in enumerate(out, 1)]
 
@@ -503,18 +506,19 @@
         send_corner(1)
         edge1 = multiply([(1, 1), (1, 2)])
         hidden0 = add_planes(*edge0)
+        edge1 = add_pair(edge1)
         corner0 = multiply([(0, 3)])
-        late1 = add_pair(edge1, corner0)
-        corner1 = add_pair(multiply([(1, 3)]))
-        hidden1 = add_planes(*late1)
+        corner1 = multiply([(1, 3)])
+        hidden1 = add_planes(*edge1)
         early = [
             (own_hidden, 0, ROWS),
             (hidden0, 0, 2 * ROWS),
-            (hidden1, 2 * ROWS, ROWS),
+            (None, 0, ROWS),
             (own_hidden, ROWS, ROWS),
             (hidden1, 0, 2 * ROWS),
+            (None, ROWS, ROWS),
         ]
-        rows = add_rows(early, *corner1)
+        rows = add_rows(early, *add_pair(corner0, corner1))
     else:
         own_hidden = add_planes(*own_planes)
         early = []
@@ -524,7 +528,7 @@
                 pair = add_pair(multiply([(i, block)]))
                 if (i, block) != (sets[-1], groups - 1):
                     early.append((add_planes(*pair), 0, ROWS))
-        rows = add_rows(early, *pair)
+        rows = add_rows(early + [(None, 0, ROWS)], *pair)
     grads = differentiate(*rows)
     parts = [part for i in sets for block in range(groups) for part in block_rows[i][block]]
     planes = []

time: 232 us -> 225 us (0.970)
  waiting for transfers between devices: 61.3 us -> 53.2 us
  starting transfers between devices: 44.1 us -> 47.7 us
  local copies, waits for them, and re-layouts: 12.1 us -> 9.33 us
    ppermute x42, waiting for transfers between devices: 61.3 us -> 53.2 us  [exchange(): return lax.ppermute(value, axis, [(i, i ^ mask) for i in range(size)])]
    ppermute x42, starting transfers between devices: 44.1 us -> 47.7 us  [exchange(): return lax.ppermute(value, axis, [(i, i ^ mask) for i in range(size)])]
    unnamed x64 -> x66, local copies, waits for them, and re-layouts: 10.2 us -> 7.45 us
  transfers between devices with their start and end apart: 42 -> 42, of which waited for: 18 -> 17; matrix products, arithmetic and copies ran while one was open for 1% -> 1% of each run, Pallas kernels for 34% -> 37%
where the time goes in v3:
time: 225 us; the launch traced here: 224 us
  Pallas kernels  110 us (49%)
  waiting for transfers between devices  53.2 us (24%)
  starting transfers between devices  47.7 us (21%)
  local copies, waits for them, and re-layouts  9.33 us (4%)
    ppermute x42, waiting for transfers between devices, exchange(): return lax.ppermute(value, axis, [(i, i ^ mask) for i in range(size)])  53.2 us
    ppermute x42, starting transfers between devices, exchange(): return lax.ppermute(value, axis, [(i, i ^ mask) for i in range(size)])  47.7 us
    pallas_call x5, Pallas kernels, forward(): pl.pallas_call(functools.partial(forward_kernel, len(parts), tile), in_sp...  44.6 us
    pallas_call x2, Pallas kernels, backward(): pl.pallas_call(functools.partial(backward_kernel, len(parts), len(pieces)...  38.4 us
    pallas_call x3, Pallas kernels, copy_rows(): pl.pallas_call(functools.partial(copy_kernel, [(start, size) for _, start...  9.39 us
    pallas_call x1, Pallas kernels, load(): pl.pallas_call(load_kernel, in_specs=[SMEM, HBM], out_specs=VMEM, out_sha...  8.71 us
    unnamed x66, local copies, waits for them, and re-layouts  7.45 us
  transfers between devices with their start and end apart: 42, of which 17 were waited for; matrix products, arithmetic and copies ran while one was open for 1% of the time, Pallas kernels for 37%

profile of v3, /device:TPU:0, one launch (start us, length us, event | category | flops | bytes accessed | tf_op | source)
XLA Modules:
  0.0 224.1 jit_solution(228481406235145533)
XLA Ops:
  0.7 3.6 %copy_rows.3 = (bf16[128,6144]{1,0:T(8,128)(2,1)}, bf16[128,6144]{1,0:T(8,128)(2,1)}) custom-call(s32[3]{0:T(128)S(1)} %pad_add_fusion.place_ref, bf16[256,6144]{1,0:T(8,128)(2,1)} %refs_1_.1, bf16[256,6144]{1,0:T(8,128)(2,1)} %refs_1_.1), custom_call_target="tpu_custom_call" | custom-call | flops 1024 | bytes 1024 | tf_op jit(solution)/shard_map/copy_rows/pallas_call | solution.py:74
  4.4 3.0 %collective-permute-start.2 = (bf16[128,6144]{1,0:T(8,128)(2,1)}, bf16[128,6144]{1,0:T(8,128)(2,1)S(1)}, u32[]{:S(2)}, u32[]{:S(2)}) collective-permute-start(bf16[128,6144]{1,0:T(8,128)(2,1)} %get-tuple-element.72.refs_0_), channel_id=1, source_target_pairs={{0,16},{8,24},{16,0},{24,8},{1,17},{9,25},{17,1},{25,9},{2,18},{10... | collective-permute-start | bytes 4718600 | tf_op jit(solution)/shard_map/ppermute | solution.py:22
  7.4 1.5 collective-permute-start.1
  11.5 1.2 gather_fusion
  12.9 2.5 %take_targets.1.target_ref = bf16[128,2048]{1,0:T(8,128)(2,1)} custom-call(s32[3]{0:T(128)S(1)} %pad_add_fusion.place_ref, bf16[1024,2048]{1,0:T(8,128)(2,1)} %target_ref.1), custom_call_target="tpu_custom_call" | custom-call | flops 1024 | bytes 1024 | tf_op jit(solution)/shard_map/take_targets/pallas_call | solution.py:238
  15.4 8.7 %load.1.refs_2_ = bf16[6144,2048]{1,0:T(8,128)(2,1)S(1)} custom-call(s32[3]{0:T(128)S(1)} %pad_add_fusion.place_ref, bf16[6144,2048]{1,0:T(8,128)(2,1)} %source_ref.1), custom_call_target="tpu_custom_call" | custom-call | flops 1024 | bytes 1024 | tf_op jit(solution)/shard_map/load/pallas_call | solution.py:92
  24.1 10.5 %forward.5 = (f32[4,2,16,2048]{3,2,1,0:T(8,128)}, bf16[4,2,16,2048]{3,2,1,0:T(8,128)(2,1)}) custom-call(s32[3]{0:T(128)S(1)} %pad_add_fusion.place_ref, bf16[128,6144]{1,0:T(8,128)(2,1)} %get-tuple-element.72.refs_0_, bf16[128,6144]{1,0:T(8,128)(2,1)} %get-tuple-element.73.refs_1_.refs_5_, bf16[6144,2048]{1,0:T(8,128)(2,1)S(1)} %load.1.refs_2_), custom_call_target="tpu_custom_call" | custom-call | flops 1024 | bytes 1024 | tf_op jit(solution)/shard_map/forward/pallas_call | solution.py:147
  34.7 2.1 collective-permute-done.refs_1_
  36.8 1.2 copy-done.3
  38.6 2.1 collective-permute-start.3
  40.7 2.1 collective-permute-done.2.refs_1_.refs_2_
  42.8 3.1 %collective-permute-start.4 = (bf16[32,2048]{1,0:T(8,128)(2,1)S(1)}, bf16[32,2048]{1,0:T(8,128)(2,1)S(1)}, u32[]{:S(2)}, u32[]{:S(2)}) collective-permute-start(bf16[32,2048]{1,0:T(8,128)(2,1)S(1)} %get-tuple-element.83), channel_id=1, source_target_pairs={{0,4},{1,5},{2,6},{3,7},{4,0},{5,1},{6,2},{7,3},{8,12},{9,13},{10,... | collective-permute-start | bytes 393224 | tf_op jit(solution)/shard_map/ppermute | solution.py:22
  46.0 2.6 %collective-permute-start.5 = (bf16[32,2048]{1,0:T(8,128)(2,1)S(1)}, bf16[32,2048]{1,0:T(8,128)(2,1)S(1)}, u32[]{:S(2)}, u32[]{:S(2)}) collective-permute-start(bf16[32,2048]{1,0:T(8,128)(2,1)S(1)} %get-tuple-element.84), channel_id=1, source_target_pairs={{0,6},{1,7},{2,4},{3,5},{4,2},{5,3},{6,0},{7,1},{8,14},{9,15},{10,... | collective-permute-start | bytes 393224 | tf_op jit(solution)/shard_map/ppermute | solution.py:22
  48.5 2.8 %copy_rows.4 = (bf16[64,6144]{1,0:T(8,128)(2,1)}, bf16[64,6144]{1,0:T(8,128)(2,1)}) custom-call(s32[3]{0:T(128)S(1)} %pad_add_fusion.place_ref, bf16[128,6144]{1,0:T(8,128)(2,1)} %copy-done.11, bf16[128,6144]{1,0:T(8,128)(2,1)} %copy-done.10), custom_call_target="tpu_custom_call" | custom-call | flops 1024 | bytes 1024 | tf_op jit(solution)/shard_map/copy_rows/pallas_call | solution.py:74
  51.4 10.5 %forward.6 = (f32[4,2,16,2048]{3,2,1,0:T(8,128)}, bf16[4,2,16,2048]{3,2,1,0:T(8,128)(2,1)}) custom-call(s32[3]{0:T(128)S(1)} %pad_add_fusion.place_ref, bf16[128,6144]{1,0:T(8,128)(2,1)} %copy-done.11, bf16[128,6144]{1,0:T(8,128)(2,1)} %copy-done.10, bf16[6144,2048]{1,0:T(8,128)(2,1)S(1)} %load.1.refs_2_), custom_call_target="tpu_custom_call" | custom-call | flops 1024 | bytes 1024 | tf_op jit(solution)/shard_map/forward/pallas_call | solution.py:147
  62.6 2.1 collective-permute-done.6.refs_1_
  64.7 1.2 copy-done.1
  66.9 1.6 collective-permute-start.10
  68.5 1.5 collective-permute-start.13
  70.0 6.7 %collective-permute-done.8.refs_1_.refs_7_ = bf16[128,6144]{1,0:T(8,128)(2,1)} collective-permute-done((bf16[128,6144]{1,0:T(8,128)(2,1)}, bf16[128,6144]{1,0:T(8,128)(2,1)}, u32[]{:S(2)}, u32[]{:S(2)}) %collective-permute-start.8) | collective-permute-done | bytes 1572896 | tf_op jit(solution)/shard_map/ppermute | solution.py:22
  76.6 2.0 collective-permute-start.14
  78.7 3.6 %collective-permute-start.11 = (bf16[32,2048]{1,0:T(8,128)(2,1)S(1)}, bf16[32,2048]{1,0:T(8,128)(2,1)S(1)}, u32[]{:S(2)}, u32[]{:S(2)}) collective-permute-start(bf16[32,2048]{1,0:T(8,128)(2,1)S(1)} %get-tuple-element.97), channel_id=1, source_target_pairs={{0,6},{1,7},{2,4},{3,5},{4,2},{5,3},{6,0},{7,1},{8,14},{9,15},{10,... | collective-permute-start | bytes 393224 | tf_op jit(solution)/shard_map/ppermute | solution.py:22
  82.3 2.9 %copy_rows.5 = (bf16[64,6144]{1,0:T(8,128)(2,1)}, bf16[64,6144]{1,0:T(8,128)(2,1)}) custom-call(s32[3]{0:T(128)S(1)} %pad_add_fusion.place_ref, bf16[128,6144]{1,0:T(8,128)(2,1)} %collective-permute-done.7.refs_0_.refs_6_, bf16[128,6144]{1,0:T(8,128)(2,1)} %collective-permute-done.8.refs_1_.refs_7_), custom_call_target="tpu_custom_call" | custom-call | flops 1024 | bytes 1024 | tf_op jit(solution)/shard_map/copy_rows/pallas_call | solution.py:74
  85.2 1.6 collective-permute-start.15
  87.4 10.7 %forward.7 = (f32[4,2,16,2048]{3,2,1,0:T(8,128)}, bf16[4,2,16,2048]{3,2,1,0:T(8,128)(2,1)}) custom-call(s32[3]{0:T(128)S(1)} %pad_add_fusion.place_ref, bf16[128,6144]{1,0:T(8,128)(2,1)} %collective-permute-done.7.refs_0_.refs_6_, bf16[128,6144]{1,0:T(8,128)(2,1)} %collective-permute-done.8.refs_1_.refs_7_, bf16[6144,2048]{1,0:T(8,128)(2,1)S(1)} %load.1.refs_2_), custom_call_target="tpu_custom_call" | custom-call | flops 1024 | bytes 1024 | tf_op jit(solution)/shard_map/forward/pallas_call | solution.py:147
  98.7 2.1 collective-permute-done.12.refs_1_
  100.8 1.2 copy-done.2
  103.5 3.6 %collective-permute-start.19 = (bf16[32,2048]{1,0:T(8,128)(2,1)S(1)}, bf16[32,2048]{1,0:T(8,128)(2,1)S(1)}, u32[]{:S(2)}, u32[]{:S(2)}) collective-permute-start(bf16[32,2048]{1,0:T(8,128)(2,1)S(1)} %get-tuple-element.110), channel_id=1, source_target_pairs={{0,6},{1,7},{2,4},{3,5},{4,2},{5,3},{6,0},{7,1},{8,14},{9,15},{10,... | collective-permute-start | bytes 393224 | tf_op jit(solution)/shard_map/ppermute | solution.py:22
  107.2 6.5 %forward.8 = (f32[4,1,16,2048]{3,2,1,0:T(8,128)}, bf16[4,1,16,2048]{3,2,1,0:T(8,128)(2,1)}) custom-call(s32[3]{0:T(128)S(1)} %pad_add_fusion.place_ref, bf16[64,6144]{1,0:T(8,128)(2,1)} %copy-done.12, bf16[64,6144]{1,0:T(8,128)(2,1)} %copy-done.13, bf16[6144,2048]{1,0:T(8,128)(2,1)S(1)} %load.1.refs_2_), custom_call_target="tpu_custom_call" | custom-call | flops 1024 | bytes 1024 | tf_op jit(solution)/shard_map/forward/pallas_call | solution.py:147
  114.9 6.5 %forward.9 = (f32[4,1,16,2048]{3,2,1,0:T(8,128)}, bf16[4,1,16,2048]{3,2,1,0:T(8,128)(2,1)}) custom-call(s32[3]{0:T(128)S(1)} %pad_add_fusion.place_ref, bf16[64,6144]{1,0:T(8,128)(2,1)} %copy-done.14, bf16[64,6144]{1,0:T(8,128)(2,1)} %copy-done.15, bf16[6144,2048]{1,0:T(8,128)(2,1)S(1)} %load.1.refs_2_), custom_call_target="tpu_custom_call" | custom-call | flops 1024 | bytes 1024 | tf_op jit(solution)/shard_map/forward/pallas_call | solution.py:147
  124.3 1.0 copy-done.5
  126.0 1.5 collective-permute-start.23
  127.5 2.9 %collective-permute-start.24 = (bf16[32,2048]{1,0:T(8,128)(2,1)S(1)}, bf16[32,2048]{1,0:T(8,128)(2,1)S(1)}, u32[]{:S(2)}, u32[]{:S(2)}) collective-permute-start(bf16[32,2048]{1,0:T(8,128)(2,1)S(1)} %get-tuple-element.124), channel_id=1, source_target_pairs={{0,6},{1,7},{2,4},{3,5},{4,2},{5,3},{6,0},{7,1},{8,14},{9,15},{10,... | collective-permute-start | bytes 393224 | tf_op jit(solution)/shard_map/ppermute | solution.py:22
  130.4 2.4 %collective-permute-done.22.refs_1_ = bf16[32,2048]{1,0:T(8,128)(2,1)S(1)} collective-permute-done((bf16[32,2048]{1,0:T(8,128)(2,1)S(1)}, bf16[32,2048]{1,0:T(8,128)(2,1)S(1)}, u32[]{:S(2)}, u32[]{:S(2)}) %collective-permute-start.22) | collective-permute-done | bytes 131104 | tf_op jit(solution)/shard_map/ppermute | solution.py:22
  132.8 6.2 %collective-permute-done.23.refs_2_ = bf16[32,2048]{1,0:T(8,128)(2,1)S(1)} collective-permute-done((bf16[32,2048]{1,0:T(8,128)(2,1)S(1)}, bf16[32,2048]{1,0:T(8,128)(2,1)S(1)}, u32[]{:S(2)}, u32[]{:S(2)}) %collective-permute-start.23) | collective-permute-done | bytes 131104 | tf_op jit(solution)/shard_map/ppermute | solution.py:22
  139.0 1.1 sum_rows.1
  140.1 1.5 collective-permute-start.27
  141.5 1.5 collective-permute-start.26
  143.6 1.7 collective-permute-done.27.refs_3_
  146.0 1.4 collective-permute-done.25.refs_1_
  147.3 1.3 gradient.1
  148.7 1.4 collective-permute-start.30
  150.1 2.6 %collective-permute-start.29 = (bf16[128,1152]{1,0:T(8,128)(2,1)S(1)}, bf16[128,1152]{1,0:T(8,128)(2,1)S(1)}, u32[]{:S(2)}, u32[]{:S(2)}) collective-permute-start(bf16[128,1152]{1,0:T(8,128)(2,1)S(1)} %get-tuple-element.129), channel_id=1, source_target_pairs={{0,4},{1,5},{2,6},{3,7},{4,0},{5,1},{6,2},{7,3},{8,12},{9,13},{10,... | collective-permute-start | bytes 884744 | tf_op jit(solution)/shard_map/ppermute | solution.py:22
  153.1 7.4 %collective-permute-done.30 = bf16[128,1152]{1,0:T(8,128)(2,1)S(1)} collective-permute-done((bf16[128,1152]{1,0:T(8,128)(2,1)S(1)}, bf16[128,1152]{1,0:T(8,128)(2,1)S(1)}, u32[]{:S(2)}, u32[]{:S(2)}) %collective-permute-start.30) | collective-permute-done | bytes 294944 | tf_op jit(solution)/shard_map/ppermute | solution.py:22
  160.5 15.7 %collective-permute-done.29 = bf16[128,1152]{1,0:T(8,128)(2,1)S(1)} collective-permute-done((bf16[128,1152]{1,0:T(8,128)(2,1)S(1)}, bf16[128,1152]{1,0:T(8,128)(2,1)S(1)}, u32[]{:S(2)}, u32[]{:S(2)}) %collective-permute-start.29) | collective-permute-done | bytes 294944 | tf_op jit(solution)/shard_map/ppermute | solution.py:22
  177.2 3.9 %collective-permute-start.35 = (bf16[128,1024]{1,0:T(8,128)(2,1)S(1)}, bf16[128,1024]{1,0:T(8,128)(2,1)S(1)}, u32[]{:S(2)}, u32[]{:S(2)}) collective-permute-start(bf16[128,1024]{1,0:T(8,128)(2,1)S(1)} %get-tuple-element.134), channel_id=1, source_target_pairs={{0,2},{1,3},{2,0},{3,1},{4,6},{5,7},{6,4},{7,5},{8,10},{9,11},{10,... | collective-permute-start | bytes 786440 | tf_op jit(solution)/shard_map/ppermute | solution.py:22
  181.9 19.2 %backward.2 = (bf16[6144,2048]{1,0:T(8,128)(2,1)}, f32[16,128]{1,0:T(8,128)S(1)}) custom-call(s32[3]{0:T(128)S(1)} %pad_add_fusion.place_ref, bf16[128,6144]{1,0:T(8,128)(2,1)} %get-tuple-element.72.refs_0_, bf16[128,6144]{1,0:T(8,128)(2,1)} %copy-done.11, bf16[128,6144]{1,0:T(8,128)(2,1)} %copy-done.10, bf16[64,6144]{1,0:T(8,128)(2,1)} %copy-done.12, ...), custom_call_target="tpu_custom_call" | custom-call | flops 1024 | bytes 1024 | tf_op jit(solution)/shard_map/backward/pallas_call | solution.py:395
  204.6 19.2 %backward.3 = bf16[6144,2048]{1,0:T(8,128)(2,1)} custom-call(s32[3]{0:T(128)S(1)} %pad_add_fusion.place_ref, bf16[128,6144]{1,0:T(8,128)(2,1)} %get-tuple-element.72.refs_0_, bf16[128,6144]{1,0:T(8,128)(2,1)} %copy-done.11, bf16[128,6144]{1,0:T(8,128)(2,1)} %copy-done.10, bf16[64,6144]{1,0:T(8,128)(2,1)} %copy-done.12, ...), custom_call_target="tpu_custom_call", output_to_operand_aliasing={{}: (19, {})} | custom-call | flops 1024 | bytes 1024 | tf_op jit(solution)/shard_map/backward/pallas_call | solution.py:395
  (144 shorter events, 18.6 us)
Async XLA Ops:
  4.4 38.5 %collective-permute-start.2 = (bf16[128,6144]{1,0:T(8,128)(2,1)}, bf16[128,6144]{1,0:T(8,128)(2,1)S(1)}, u32[]{:S(2)}, u32[]{:S(2)}) collective-permute-start(bf16[128,6144]{1,0:T(8,128)(2,1)} %get-tuple-element.72.refs_0_), channel_id=1, source_target_pairs={{0,16},{8,24},{16,0},{24,8},{1,17},{9,25},{17,1},{25,9},{2,18},{10... | collective-permute-start | bytes 4718600 | tf_op jit(solution)/shard_map/ppermute | solution.py:22
  7.4 38.6 %collective-permute-start.1 = (bf16[128,6144]{1,0:T(8,128)(2,1)}, bf16[128,6144]{1,0:T(8,128)(2,1)S(1)}, u32[]{:S(2)}, u32[]{:S(2)}) collective-permute-start(bf16[128,6144]{1,0:T(8,128)(2,1)} %get-tuple-element.72.refs_0_), channel_id=1, source_target_pairs={{0,8},{8,0},{16,24},{24,16},{1,9},{9,1},{17,25},{25,17},{2,10},{10... | collective-permute-start | bytes 4718600 | tf_op jit(solution)/shard_map/ppermute | solution.py:22
  8.9 67.8 %collective-permute-start.8 = (bf16[128,6144]{1,0:T(8,128)(2,1)}, bf16[128,6144]{1,0:T(8,128)(2,1)}, u32[]{:S(2)}, u32[]{:S(2)}) collective-permute-start(bf16[128,6144]{1,0:T(8,128)(2,1)} %get-tuple-element.73.refs_1_.refs_5_), channel_id=1, source_target_pairs={{0,16},{8,24},{16,0},{24,8},{1,17},{9,25},{17,1},{25,9},{2,18},{10... | collective-permute-start | bytes 4718600 | tf_op jit(solution)/shard_map/ppermute | solution.py:22
  9.4 69.3 %collective-permute-start.7 = (bf16[128,6144]{1,0:T(8,128)(2,1)}, bf16[128,6144]{1,0:T(8,128)(2,1)}, u32[]{:S(2)}, u32[]{:S(2)}) collective-permute-start(bf16[128,6144]{1,0:T(8,128)(2,1)} %get-tuple-element.73.refs_1_.refs_5_), channel_id=1, source_target_pairs={{0,8},{8,0},{16,24},{24,16},{1,9},{9,1},{17,25},{25,17},{2,10},{10... | collective-permute-start | bytes 4718600 | tf_op jit(solution)/shard_map/ppermute | solution.py:22
  34.6 2.2 collective-permute-start
  38.6 23.2 %collective-permute-start.3 = (bf16[32,2048]{1,0:T(8,128)(2,1)S(1)}, bf16[32,2048]{1,0:T(8,128)(2,1)S(1)}, u32[]{:S(2)}, u32[]{:S(2)}) collective-permute-start(bf16[32,2048]{1,0:T(8,128)(2,1)S(1)} %get-tuple-element.82), channel_id=1, source_target_pairs={{0,2},{1,3},{2,0},{3,1},{4,6},{5,7},{6,4},{7,5},{8,10},{9,11},{10,... | collective-permute-start | bytes 393224 | tf_op jit(solution)/shard_map/ppermute | solution.py:22
  42.8 19.1 %collective-permute-start.4 = (bf16[32,2048]{1,0:T(8,128)(2,1)S(1)}, bf16[32,2048]{1,0:T(8,128)(2,1)S(1)}, u32[]{:S(2)}, u32[]{:S(2)}) collective-permute-start(bf16[32,2048]{1,0:T(8,128)(2,1)S(1)} %get-tuple-element.83), channel_id=1, source_target_pairs={{0,4},{1,5},{2,6},{3,7},{4,0},{5,1},{6,2},{7,3},{8,12},{9,13},{10,... | collective-permute-start | bytes 393224 | tf_op jit(solution)/shard_map/ppermute | solution.py:22
  46.0 15.9 %collective-permute-start.5 = (bf16[32,2048]{1,0:T(8,128)(2,1)S(1)}, bf16[32,2048]{1,0:T(8,128)(2,1)S(1)}, u32[]{:S(2)}, u32[]{:S(2)}) collective-permute-start(bf16[32,2048]{1,0:T(8,128)(2,1)S(1)} %get-tuple-element.84), channel_id=1, source_target_pairs={{0,6},{1,7},{2,4},{3,5},{4,2},{5,3},{6,0},{7,1},{8,14},{9,15},{10,... | collective-permute-start | bytes 393224 | tf_op jit(solution)/shard_map/ppermute | solution.py:22
  51.4 25.3 %copy-start.30 = (bf16[64,6144]{1,0:T(8,128)(2,1)S(1)}, bf16[64,6144]{1,0:T(8,128)(2,1)}, u32[]{:S(2)}) copy-start(bf16[64,6144]{1,0:T(8,128)(2,1)} %get-tuple-element.87) | copy-start | bytes 2359300
  62.5 2.2 collective-permute-start.6
  66.6 18.7 %collective-permute-start.9 = (bf16[32,2048]{1,0:T(8,128)(2,1)S(1)}, bf16[32,2048]{1,0:T(8,128)(2,1)S(1)}, u32[]{:S(2)}, u32[]{:S(2)}) collective-permute-start(bf16[32,2048]{1,0:T(8,128)(2,1)S(1)} %get-tuple-element.95), channel_id=1, source_target_pairs={{0,2},{1,3},{2,0},{3,1},{4,6},{5,7},{6,4},{7,5},{8,10},{9,11},{10,... | collective-permute-start | bytes 393224 | tf_op jit(solution)/shard_map/ppermute | solution.py:22
  66.9 19.9 %collective-permute-start.10 = (bf16[32,2048]{1,0:T(8,128)(2,1)S(1)}, bf16[32,2048]{1,0:T(8,128)(2,1)S(1)}, u32[]{:S(2)}, u32[]{:S(2)}) collective-permute-start(bf16[32,2048]{1,0:T(8,128)(2,1)S(1)} %get-tuple-element.96), channel_id=1, source_target_pairs={{0,4},{1,5},{2,6},{3,7},{4,0},{5,1},{6,2},{7,3},{8,12},{9,13},{10,... | collective-permute-start | bytes 393224 | tf_op jit(solution)/shard_map/ppermute | solution.py:22
  68.5 34.3 %collective-permute-start.13 = (bf16[64,6144]{1,0:T(8,128)(2,1)S(1)}, bf16[64,6144]{1,0:T(8,128)(2,1)S(1)}, u32[]{:S(2)}, u32[]{:S(2)}) collective-permute-start(bf16[64,6144]{1,0:T(8,128)(2,1)S(1)} %copy-done.31), channel_id=1, source_target_pairs={{0,16},{8,24},{16,0},{24,8},{1,17},{9,25},{17,1},{25,9},{2,18},{10... | collective-permute-start | bytes 2359304 | tf_op jit(solution)/shard_map/ppermute | solution.py:22
  76.6 26.9 %collective-permute-start.14 = (bf16[64,6144]{1,0:T(8,128)(2,1)S(1)}, bf16[64,6144]{1,0:T(8,128)(2,1)S(1)}, u32[]{:S(2)}, u32[]{:S(2)}) collective-permute-start(bf16[64,6144]{1,0:T(8,128)(2,1)S(1)} %copy-done.30), channel_id=1, source_target_pairs={{0,8},{8,0},{16,24},{24,16},{1,9},{9,1},{17,25},{25,17},{2,10},{10... | collective-permute-start | bytes 2359304 | tf_op jit(solution)/shard_map/ppermute | solution.py:22
  78.7 19.4 %collective-permute-start.11 = (bf16[32,2048]{1,0:T(8,128)(2,1)S(1)}, bf16[32,2048]{1,0:T(8,128)(2,1)S(1)}, u32[]{:S(2)}, u32[]{:S(2)}) collective-permute-start(bf16[32,2048]{1,0:T(8,128)(2,1)S(1)} %get-tuple-element.97), channel_id=1, source_target_pairs={{0,6},{1,7},{2,4},{3,5},{4,2},{5,3},{6,0},{7,1},{8,14},{9,15},{10,... | collective-permute-start | bytes 393224 | tf_op jit(solution)/shard_map/ppermute | solution.py:22
  85.2 28.4 %collective-permute-start.15 = (bf16[64,6144]{1,0:T(8,128)(2,1)}, bf16[64,6144]{1,0:T(8,128)(2,1)S(1)}, u32[]{:S(2)}, u32[]{:S(2)}) collective-permute-start(bf16[64,6144]{1,0:T(8,128)(2,1)} %get-tuple-element.99), channel_id=1, source_target_pairs={{0,16},{8,24},{16,0},{24,8},{1,17},{9,25},{17,1},{25,9},{2,18},{10... | collective-permute-start | bytes 2359304 | tf_op jit(solution)/shard_map/ppermute | solution.py:22
  86.8 26.8 %collective-permute-start.16 = (bf16[64,6144]{1,0:T(8,128)(2,1)}, bf16[64,6144]{1,0:T(8,128)(2,1)S(1)}, u32[]{:S(2)}, u32[]{:S(2)}) collective-permute-start(bf16[64,6144]{1,0:T(8,128)(2,1)} %get-tuple-element.100), channel_id=1, source_target_pairs={{0,8},{8,0},{16,24},{24,16},{1,9},{9,1},{17,25},{25,17},{2,10},{10... | collective-permute-start | bytes 2359304 | tf_op jit(solution)/shard_map/ppermute | solution.py:22
  98.6 2.2 collective-permute-start.12
  102.7 18.7 %collective-permute-start.17 = (bf16[32,2048]{1,0:T(8,128)(2,1)S(1)}, bf16[32,2048]{1,0:T(8,128)(2,1)S(1)}, u32[]{:S(2)}, u32[]{:S(2)}) collective-permute-start(bf16[32,2048]{1,0:T(8,128)(2,1)S(1)} %get-tuple-element.108), channel_id=1, source_target_pairs={{0,2},{1,3},{2,0},{3,1},{4,6},{5,7},{6,4},{7,5},{8,10},{9,11},{10,... | collective-permute-start | bytes 393224 | tf_op jit(solution)/shard_map/ppermute | solution.py:22
  102.8 18.6 %collective-permute-start.18 = (bf16[32,2048]{1,0:T(8,128)(2,1)S(1)}, bf16[32,2048]{1,0:T(8,128)(2,1)S(1)}, u32[]{:S(2)}, u32[]{:S(2)}) collective-permute-start(bf16[32,2048]{1,0:T(8,128)(2,1)S(1)} %get-tuple-element.109), channel_id=1, source_target_pairs={{0,4},{1,5},{2,6},{3,7},{4,0},{5,1},{6,2},{7,3},{8,12},{9,13},{10,... | collective-permute-start | bytes 393224 | tf_op jit(solution)/shard_map/ppermute | solution.py:22
  103.5 17.9 %collective-permute-start.19 = (bf16[32,2048]{1,0:T(8,128)(2,1)S(1)}, bf16[32,2048]{1,0:T(8,128)(2,1)S(1)}, u32[]{:S(2)}, u32[]{:S(2)}) collective-permute-start(bf16[32,2048]{1,0:T(8,128)(2,1)S(1)} %get-tuple-element.110), channel_id=1, source_target_pairs={{0,6},{1,7},{2,4},{3,5},{4,2},{5,3},{6,0},{7,1},{8,14},{9,15},{10,... | collective-permute-start | bytes 393224 | tf_op jit(solution)/shard_map/ppermute | solution.py:22
  114.9 24.1 %copy-start = (bf16[128,2048]{1,0:T(8,128)(2,1)S(1)}, bf16[128,2048]{1,0:T(8,128)(2,1)}, u32[]{:S(2)}) copy-start(bf16[128,2048]{1,0:T(8,128)(2,1)} %take_targets.1.target_ref) | copy-start | bytes 1572868
  114.9 24.1 %copy-start.8 = (f32[2048]{0:T(1024)S(1)}, f32[2048]{0:T(1024)}, u32[]{:S(2)}) copy-start(f32[2048]{0:T(1024)} %param.7) | copy-start | bytes 24580
  122.1 1.6 collective-permute-start.20
  122.2 2.1 collective-permute-start.21
  125.9 6.8 %collective-permute-start.22 = (bf16[32,2048]{1,0:T(8,128)(2,1)S(1)}, bf16[32,2048]{1,0:T(8,128)(2,1)S(1)}, u32[]{:S(2)}, u32[]{:S(2)}) collective-permute-start(bf16[32,2048]{1,0:T(8,128)(2,1)S(1)} %get-tuple-element.122), channel_id=1, source_target_pairs={{0,2},{1,3},{2,0},{3,1},{4,6},{5,7},{6,4},{7,5},{8,10},{9,11},{10,... | collective-permute-start | bytes 393224 | tf_op jit(solution)/shard_map/ppermute | solution.py:22
  126.0 13.0 %collective-permute-start.23 = (bf16[32,2048]{1,0:T(8,128)(2,1)S(1)}, bf16[32,2048]{1,0:T(8,128)(2,1)S(1)}, u32[]{:S(2)}, u32[]{:S(2)}) collective-permute-start(bf16[32,2048]{1,0:T(8,128)(2,1)S(1)} %get-tuple-element.123), channel_id=1, source_target_pairs={{0,4},{1,5},{2,6},{3,7},{4,0},{5,1},{6,2},{7,3},{8,12},{9,13},{10,... | collective-permute-start | bytes 393224 | tf_op jit(solution)/shard_map/ppermute | solution.py:22
  127.5 11.5 %collective-permute-start.24 = (bf16[32,2048]{1,0:T(8,128)(2,1)S(1)}, bf16[32,2048]{1,0:T(8,128)(2,1)S(1)}, u32[]{:S(2)}, u32[]{:S(2)}) collective-permute-start(bf16[32,2048]{1,0:T(8,128)(2,1)S(1)} %get-tuple-element.124), channel_id=1, source_target_pairs={{0,6},{1,7},{2,4},{3,5},{4,2},{5,3},{6,0},{7,1},{8,14},{9,15},{10,... | collective-permute-start | bytes 393224 | tf_op jit(solution)/shard_map/ppermute | solution.py:22
  140.1 5.2 %collective-permute-start.27 = (f32[128,128]{1,0:T(8,128)S(1)}, f32[128,128]{1,0:T(8,128)S(1)}, u32[]{:S(2)}, u32[]{:S(2)}) collective-permute-start(f32[128,128]{1,0:T(8,128)S(1)} %get-tuple-element.127.refs_0_), channel_id=1, source_target_pairs={{0,24},{8,16},{16,8},{24,0},{1,25},{9,17},{17,9},{25,1},{2,26},{10... | collective-permute-start | bytes 196616 | tf_op jit(solution)/shard_map/ppermute | solution.py:22
  141.5 4.5 %collective-permute-start.26 = (f32[128,128]{1,0:T(8,128)S(1)}, f32[128,128]{1,0:T(8,128)S(1)}, u32[]{:S(2)}, u32[]{:S(2)}) collective-permute-start(f32[128,128]{1,0:T(8,128)S(1)} %get-tuple-element.127.refs_0_), channel_id=1, source_target_pairs={{0,16},{8,24},{16,0},{24,8},{1,17},{9,25},{17,1},{25,9},{2,18},{10... | collective-permute-start | bytes 196616 | tf_op jit(solution)/shard_map/ppermute | solution.py:22
  143.1 4.3 %collective-permute-start.25 = (f32[128,128]{1,0:T(8,128)S(1)}, f32[128,128]{1,0:T(8,128)S(1)}, u32[]{:S(2)}, u32[]{:S(2)}) collective-permute-start(f32[128,128]{1,0:T(8,128)S(1)} %get-tuple-element.127.refs_0_), channel_id=1, source_target_pairs={{0,8},{8,0},{16,24},{24,16},{1,9},{9,1},{17,25},{25,17},{2,10},{10... | collective-permute-start | bytes 196616 | tf_op jit(solution)/shard_map/ppermute | solution.py:22
  148.6 32.5 %copy-start.6 = (bf16[128,1152]{1,0:T(8,128)(2,1)}, bf16[128,1152]{1,0:T(8,128)(2,1)S(1)}, u32[]{:S(2)}) copy-start(bf16[128,1152]{1,0:T(8,128)(2,1)S(1)} %get-tuple-element.129) | copy-start | bytes 884740
  148.6 52.5 %copy-start.7 = (bf16[128,1024]{1,0:T(8,128)(2,1)}, bf16[128,1024]{1,0:T(8,128)(2,1)S(1)}, u32[]{:S(2)}) copy-start(bf16[128,1024]{1,0:T(8,128)(2,1)S(1)} %get-tuple-element.134) | copy-start | bytes 786436
  148.7 11.8 %collective-permute-start.30 = (bf16[128,1152]{1,0:T(8,128)(2,1)S(1)}, bf16[128,1152]{1,0:T(8,128)(2,1)S(1)}, u32[]{:S(2)}, u32[]{:S(2)}) collective-permute-start(bf16[128,1152]{1,0:T(8,128)(2,1)S(1)} %get-tuple-element.129), channel_id=1, source_target_pairs={{0,6},{1,7},{2,4},{3,5},{4,2},{5,3},{6,0},{7,1},{8,14},{9,15},{10,... | collective-permute-start | bytes 884744 | tf_op jit(solution)/shard_map/ppermute | solution.py:22
  150.1 26.1 %collective-permute-start.29 = (bf16[128,1152]{1,0:T(8,128)(2,1)S(1)}, bf16[128,1152]{1,0:T(8,128)(2,1)S(1)}, u32[]{:S(2)}, u32[]{:S(2)}) collective-permute-start(bf16[128,1152]{1,0:T(8,128)(2,1)S(1)} %get-tuple-element.129), channel_id=1, source_target_pairs={{0,4},{1,5},{2,6},{3,7},{4,0},{5,1},{6,2},{7,3},{8,12},{9,13},{10,... | collective-permute-start | bytes 884744 | tf_op jit(solution)/shard_map/ppermute | solution.py:22
  152.7 23.4 %collective-permute-start.28 = (bf16[128,1152]{1,0:T(8,128)(2,1)S(1)}, bf16[128,1152]{1,0:T(8,128)(2,1)S(1)}, u32[]{:S(2)}, u32[]{:S(2)}) collective-permute-start(bf16[128,1152]{1,0:T(8,128)(2,1)S(1)} %get-tuple-element.129), channel_id=1, source_target_pairs={{0,2},{1,3},{2,0},{3,1},{4,6},{5,7},{6,4},{7,5},{8,10},{9,11},{10,... | collective-permute-start | bytes 884744 | tf_op jit(solution)/shard_map/ppermute | solution.py:22
  153.1 24.0 %collective-permute-start.31 = (bf16[128,1152]{1,0:T(8,128)(2,1)S(1)}, bf16[128,1152]{1,0:T(8,128)(2,1)S(1)}, u32[]{:S(2)}, u32[]{:S(2)}) collective-permute-start(bf16[128,1152]{1,0:T(8,128)(2,1)S(1)} %get-tuple-element.129), channel_id=1, source_target_pairs={{0,1},{1,0},{2,3},{3,2},{4,5},{5,4},{6,7},{7,6},{8,9},{9,8},{10,11... | collective-permute-start | bytes 884744 | tf_op jit(solution)/shard_map/ppermute | solution.py:22
  160.5 20.6 %copy-start.16 = (bf16[128,1152]{1,0:T(8,128)(2,1)}, bf16[128,1152]{1,0:T(8,128)(2,1)S(1)}, u32[]{:S(2)}) copy-start(bf16[128,1152]{1,0:T(8,128)(2,1)S(1)} %collective-permute-done.30) | copy-start | bytes 884740
  160.5 16.7 %collective-permute-start.34 = (bf16[128,1152]{1,0:T(8,128)(2,1)S(1)}, bf16[128,1152]{1,0:T(8,128)(2,1)S(1)}, u32[]{:S(2)}, u32[]{:S(2)}) collective-permute-start(bf16[128,1152]{1,0:T(8,128)(2,1)S(1)} %collective-permute-done.30), channel_id=1, source_target_pairs={{0,1},{1,0},{2,3},{3,2},{4,5},{5,4},{6,7},{7,6},{8,9},{9,8},{10,11... | collective-permute-start | bytes 884744 | tf_op jit(solution)/shard_map/ppermute | solution.py:22
  176.2 4.9 %collective-permute-start.33 = (bf16[128,1152]{1,0:T(8,128)(2,1)S(1)}, bf16[128,1152]{1,0:T(8,128)(2,1)S(1)}, u32[]{:S(2)}, u32[]{:S(2)}) collective-permute-start(bf16[128,1152]{1,0:T(8,128)(2,1)S(1)} %collective-permute-done.29), channel_id=1, source_target_pairs={{0,1},{1,0},{2,3},{3,2},{4,5},{5,4},{6,7},{7,6},{8,9},{9,8},{10,11... | collective-permute-start | bytes 884744 | tf_op jit(solution)/shard_map/ppermute | solution.py:22
  176.2 4.9 %collective-permute-start.32 = (bf16[128,1152]{1,0:T(8,128)(2,1)S(1)}, bf16[128,1152]{1,0:T(8,128)(2,1)S(1)}, u32[]{:S(2)}, u32[]{:S(2)}) collective-permute-start(bf16[128,1152]{1,0:T(8,128)(2,1)S(1)} %collective-permute-done.28), channel_id=1, source_target_pairs={{0,1},{1,0},{2,3},{3,2},{4,5},{5,4},{6,7},{7,6},{8,9},{9,8},{10,11... | collective-permute-start | bytes 884744 | tf_op jit(solution)/shard_map/ppermute | solution.py:22
  176.7 24.4 %collective-permute-start.37 = (bf16[128,1024]{1,0:T(8,128)(2,1)S(1)}, bf16[128,1024]{1,0:T(8,128)(2,1)S(1)}, u32[]{:S(2)}, u32[]{:S(2)}) collective-permute-start(bf16[128,1024]{1,0:T(8,128)(2,1)S(1)} %get-tuple-element.134), channel_id=1, source_target_pairs={{0,6},{1,7},{2,4},{3,5},{4,2},{5,3},{6,0},{7,1},{8,14},{9,15},{10,... | collective-permute-start | bytes 786440 | tf_op jit(solution)/shard_map/ppermute | solution.py:22
  177.1 24.0 %collective-permute-start.36 = (bf16[128,1024]{1,0:T(8,128)(2,1)S(1)}, bf16[128,1024]{1,0:T(8,128)(2,1)S(1)}, u32[]{:S(2)}, u32[]{:S(2)}) collective-permute-start(bf16[128,1024]{1,0:T(8,128)(2,1)S(1)} %get-tuple-element.134), channel_id=1, source_target_pairs={{0,4},{1,5},{2,6},{3,7},{4,0},{5,1},{6,2},{7,3},{8,12},{9,13},{10,... | collective-permute-start | bytes 786440 | tf_op jit(solution)/shard_map/ppermute | solution.py:22
  177.2 24.0 %collective-permute-start.35 = (bf16[128,1024]{1,0:T(8,128)(2,1)S(1)}, bf16[128,1024]{1,0:T(8,128)(2,1)S(1)}, u32[]{:S(2)}, u32[]{:S(2)}) collective-permute-start(bf16[128,1024]{1,0:T(8,128)(2,1)S(1)} %get-tuple-element.134), channel_id=1, source_target_pairs={{0,2},{1,3},{2,0},{3,1},{4,6},{5,7},{6,4},{7,5},{8,10},{9,11},{10,... | collective-permute-start | bytes 786440 | tf_op jit(solution)/shard_map/ppermute | solution.py:22
  201.2 1.7 collective-permute-start.38
  201.3 1.9 collective-permute-start.39
  201.8 1.8 collective-permute-start.40
  201.9 2.1 collective-permute-start.41
  (27 other events, 97.1 us)

commit v4 on v3

--- a/solution.py
+++ b/solution.py
@@ -344,16 +344,12 @@
     )(place, hidden, gain, target, share, *all_sums)
 
 
-def piece_copies(place_ref, pieces, target, sems):
+def place_pieces(place_ref, pieces, rows_ref):
     core, plane = place_ref[0], place_ref[1]
     slots = len(pieces) // 2
-    copies = []
     for i, piece in enumerate(pieces):
         owner = (plane ^ (i % slots)) * 2 + (core if i < slots else 1 - core)
-        copies.append(
-            pltpu.make_async_copy(piece, target.at[:, owner], sems.at[i])
-        )
-    return copies
+        rows_ref[:, owner] = piece[...]
 
 
 def by_block(pieces):
@@ -363,18 +359,18 @@
 def backward_kernel(part_count, piece_count, place_ref, *refs):
     parts, refs = refs[:part_count], refs[part_count:]
     pieces, refs = refs[:piece_count], refs[piece_count:]
-    rows_ref, sems = refs[-2:]
-    out_ref, *loss = refs[-4:-2] if refs[-3].shape[-1] == 128 else refs[-3:-2]
+    rows_ref = refs[-1]
+    out_ref, *loss = refs[-3:-1] if refs[-2].shape[-1] == 1 else refs[-2:-1]
     units = out_ref.shape[-1]
 
     @pl.when(pl.program_id(0) == 0)
     def _():
-        run_copies(piece_copies(place_ref, pieces, rows_ref, sems))
+        place_pieces(place_ref, pieces, rows_ref)
         for loss_ref in loss:
-            total = jnp.zeros(loss_ref.shape, f32)
+            total = jnp.zeros((ROWS, 128), f32)
             for owner in range(rows_ref.shape[1]):
                 total += rows_ref[0, owner, :, units:].astype(f32)
-            loss_ref[...] = total
+            loss_ref[0, 0] = jnp.sum(total[:1])
 
     left = jnp.concatenate([part[...] for part in parts], axis=0)
     out_ref[...] = lax.dot_general(
@@ -390,21 +386,22 @@
     tile = min(depth, 1024)
     width = units // PARTS
     blocks = pieces[0].shape[0] // ROWS
-    operands = [place, *in_hbm(*parts), *by_block(pieces)]
+    here = by_block(pieces)
+    operands = [place, *in_hbm(*parts), *here]
     first = result is None
     out = pl.pallas_call(
         functools.partial(backward_kernel, len(parts), len(pieces)),
         grid=(depth // tile,),
         in_specs=[SMEM]
         + [pl.BlockSpec((part.shape[0], tile), lambda k: (0, k)) for part in parts]
-        + [HBM] * (len(pieces) + (not first)),
+        + [whole(piece.shape) for piece in here]
+        + [HBM] * (not first),
         out_specs=[pl.BlockSpec((tile, width), lambda k: (k, index))]
-        + [pl.BlockSpec((ROWS, 128), lambda k: (0, 0))] * first,
+        + [SMEM] * first,
         out_shape=[jax.ShapeDtypeStruct((depth, units), bf16)]
-        + [jax.ShapeDtypeStruct((ROWS, 128), f32)] * first,
+        + [jax.ShapeDtypeStruct((1, 1), f32)] * first,
         scratch_shapes=[
             pltpu.VMEM((blocks, len(pieces), ROWS, pieces[0].shape[1]), bf16),
-            pltpu.SemaphoreType.DMA((len(pieces),)),
         ],
         input_output_aliases={} if first else {len(operands): 0},
         compiler_params=params(24),
@@ -540,7 +537,7 @@
         result, total = backward(turn(*pieces), parts, pieces, i, gain.shape[1], result)
         loss = total if i == 0 else loss
         ran(loss)
-    return (result, jnp.sum(loss[0]))
+    return (result, loss.reshape(()))
 
 
 def solution(mesh):

time: 225 us -> 224 us (level)
  transfers between devices with their start and end apart: 42 -> 42, of which waited for: 17 -> 18; matrix products, arithmetic and copies ran while one was open for 1% -> 1% of each run, Pallas kernels for 37% -> 37%
where the time goes in v4:
time: 224 us; the launch traced here: 223 us
  Pallas kernels  109 us (49%)
  waiting for transfers between devices  53.8 us (24%)
  starting transfers between devices  47.7 us (21%)
  local copies, waits for them, and re-layouts  9.32 us (4%)
    ppermute x42, waiting for transfers between devices, exchange(): return lax.ppermute(value, axis, [(i, i ^ mask) for i in range(size)])  53.8 us
    ppermute x42, starting transfers between devices, exchange(): return lax.ppermute(value, axis, [(i, i ^ mask) for i in range(size)])  47.7 us
    pallas_call x5, Pallas kernels, forward(): pl.pallas_call(functools.partial(forward_kernel, len(parts), tile), in_sp...  44.5 us
    pallas_call x2, Pallas kernels, backward(): pl.pallas_call(functools.partial(backward_kernel, len(parts), len(pieces)...  37.5 us
    pallas_call x3, Pallas kernels, copy_rows(): pl.pallas_call(functools.partial(copy_kernel, [(start, size) for _, start...  9.37 us
    pallas_call x1, Pallas kernels, load(): pl.pallas_call(load_kernel, in_specs=[SMEM, HBM], out_specs=VMEM, out_sha...  8.71 us
    unnamed x66, local copies, waits for them, and re-layouts  7.44 us
  transfers between devices with their start and end apart: 42, of which 18 were waited for; matrix products, arithmetic and copies ran while one was open for 1% of the time, Pallas kernels for 37%

profile of v4, /device:TPU:0, one launch (start us, length us, event | category | flops | bytes accessed | tf_op | source)
XLA Modules:
  0.0 223.0 jit_solution(18119304389910936879)
XLA Ops:
  0.7 3.6 %copy_rows.3 = (bf16[128,6144]{1,0:T(8,128)(2,1)}, bf16[128,6144]{1,0:T(8,128)(2,1)}) custom-call(s32[3]{0:T(128)S(1)} %pad_add_fusion.place_ref, bf16[256,6144]{1,0:T(8,128)(2,1)} %refs_1_.1, bf16[256,6144]{1,0:T(8,128)(2,1)} %refs_1_.1), custom_call_target="tpu_custom_call" | custom-call | flops 1024 | bytes 1024 | tf_op jit(solution)/shard_map/copy_rows/pallas_call | solution.py:74
  4.3 3.0 %collective-permute-start.2 = (bf16[128,6144]{1,0:T(8,128)(2,1)}, bf16[128,6144]{1,0:T(8,128)(2,1)S(1)}, u32[]{:S(2)}, u32[]{:S(2)}) collective-permute-start(bf16[128,6144]{1,0:T(8,128)(2,1)} %get-tuple-element.72.refs_0_), channel_id=1, source_target_pairs={{0,16},{8,24},{16,0},{24,8},{1,17},{9,25},{17,1},{25,9},{2,18},{10... | collective-permute-start | bytes 4718600 | tf_op jit(solution)/shard_map/ppermute | solution.py:22
  7.4 1.5 collective-permute-start.1
  11.5 1.2 gather_fusion
  12.9 2.5 %take_targets.1.target_ref = bf16[128,2048]{1,0:T(8,128)(2,1)} custom-call(s32[3]{0:T(128)S(1)} %pad_add_fusion.place_ref, bf16[1024,2048]{1,0:T(8,128)(2,1)} %target_ref.1), custom_call_target="tpu_custom_call" | custom-call | flops 1024 | bytes 1024 | tf_op jit(solution)/shard_map/take_targets/pallas_call | solution.py:238
  15.4 8.7 %load.1.refs_2_ = bf16[6144,2048]{1,0:T(8,128)(2,1)S(1)} custom-call(s32[3]{0:T(128)S(1)} %pad_add_fusion.place_ref, bf16[6144,2048]{1,0:T(8,128)(2,1)} %source_ref.1), custom_call_target="tpu_custom_call" | custom-call | flops 1024 | bytes 1024 | tf_op jit(solution)/shard_map/load/pallas_call | solution.py:92
  24.1 10.5 %forward.5 = (f32[4,2,16,2048]{3,2,1,0:T(8,128)}, bf16[4,2,16,2048]{3,2,1,0:T(8,128)(2,1)}) custom-call(s32[3]{0:T(128)S(1)} %pad_add_fusion.place_ref, bf16[128,6144]{1,0:T(8,128)(2,1)} %get-tuple-element.72.refs_0_, bf16[128,6144]{1,0:T(8,128)(2,1)} %get-tuple-element.73.refs_1_.refs_5_, bf16[6144,2048]{1,0:T(8,128)(2,1)S(1)} %load.1.refs_2_), custom_call_target="tpu_custom_call" | custom-call | flops 1024 | bytes 1024 | tf_op jit(solution)/shard_map/forward/pallas_call | solution.py:147
  34.6 2.1 collective-permute-done.refs_1_
  36.7 1.2 copy-done.3
  38.6 2.1 collective-permute-start.3
  40.7 2.1 collective-permute-done.2.refs_1_.refs_2_
  42.8 3.1 %collective-permute-start.4 = (bf16[32,2048]{1,0:T(8,128)(2,1)S(1)}, bf16[32,2048]{1,0:T(8,128)(2,1)S(1)}, u32[]{:S(2)}, u32[]{:S(2)}) collective-permute-start(bf16[32,2048]{1,0:T(8,128)(2,1)S(1)} %get-tuple-element.83), channel_id=1, source_target_pairs={{0,4},{1,5},{2,6},{3,7},{4,0},{5,1},{6,2},{7,3},{8,12},{9,13},{10,... | collective-permute-start | bytes 393224 | tf_op jit(solution)/shard_map/ppermute | solution.py:22
  45.9 2.6 %collective-permute-start.5 = (bf16[32,2048]{1,0:T(8,128)(2,1)S(1)}, bf16[32,2048]{1,0:T(8,128)(2,1)S(1)}, u32[]{:S(2)}, u32[]{:S(2)}) collective-permute-start(bf16[32,2048]{1,0:T(8,128)(2,1)S(1)} %get-tuple-element.84), channel_id=1, source_target_pairs={{0,6},{1,7},{2,4},{3,5},{4,2},{5,3},{6,0},{7,1},{8,14},{9,15},{10,... | collective-permute-start | bytes 393224 | tf_op jit(solution)/shard_map/ppermute | solution.py:22
  48.5 2.8 %copy_rows.4 = (bf16[64,6144]{1,0:T(8,128)(2,1)}, bf16[64,6144]{1,0:T(8,128)(2,1)}) custom-call(s32[3]{0:T(128)S(1)} %pad_add_fusion.place_ref, bf16[128,6144]{1,0:T(8,128)(2,1)} %copy-done.11, bf16[128,6144]{1,0:T(8,128)(2,1)} %copy-done.10), custom_call_target="tpu_custom_call" | custom-call | flops 1024 | bytes 1024 | tf_op jit(solution)/shard_map/copy_rows/pallas_call | solution.py:74
  51.4 10.5 %forward.6 = (f32[4,2,16,2048]{3,2,1,0:T(8,128)}, bf16[4,2,16,2048]{3,2,1,0:T(8,128)(2,1)}) custom-call(s32[3]{0:T(128)S(1)} %pad_add_fusion.place_ref, bf16[128,6144]{1,0:T(8,128)(2,1)} %copy-done.11, bf16[128,6144]{1,0:T(8,128)(2,1)} %copy-done.10, bf16[6144,2048]{1,0:T(8,128)(2,1)S(1)} %load.1.refs_2_), custom_call_target="tpu_custom_call" | custom-call | flops 1024 | bytes 1024 | tf_op jit(solution)/shard_map/forward/pallas_call | solution.py:147
  62.6 2.1 collective-permute-done.6.refs_1_
  64.7 1.2 copy-done.1
  66.8 1.6 collective-permute-start.10
  68.4 1.5 collective-permute-start.13
  69.9 6.7 %collective-permute-done.8.refs_1_.refs_7_ = bf16[128,6144]{1,0:T(8,128)(2,1)} collective-permute-done((bf16[128,6144]{1,0:T(8,128)(2,1)}, bf16[128,6144]{1,0:T(8,128)(2,1)}, u32[]{:S(2)}, u32[]{:S(2)}) %collective-permute-start.8) | collective-permute-done | bytes 1572896 | tf_op jit(solution)/shard_map/ppermute | solution.py:22
  76.6 2.0 collective-permute-start.14
  78.7 3.6 %collective-permute-start.11 = (bf16[32,2048]{1,0:T(8,128)(2,1)S(1)}, bf16[32,2048]{1,0:T(8,128)(2,1)S(1)}, u32[]{:S(2)}, u32[]{:S(2)}) collective-permute-start(bf16[32,2048]{1,0:T(8,128)(2,1)S(1)} %get-tuple-element.97), channel_id=1, source_target_pairs={{0,6},{1,7},{2,4},{3,5},{4,2},{5,3},{6,0},{7,1},{8,14},{9,15},{10,... | collective-permute-start | bytes 393224 | tf_op jit(solution)/shard_map/ppermute | solution.py:22
  82.3 2.9 %copy_rows.5 = (bf16[64,6144]{1,0:T(8,128)(2,1)}, bf16[64,6144]{1,0:T(8,128)(2,1)}) custom-call(s32[3]{0:T(128)S(1)} %pad_add_fusion.place_ref, bf16[128,6144]{1,0:T(8,128)(2,1)} %collective-permute-done.7.refs_0_.refs_6_, bf16[128,6144]{1,0:T(8,128)(2,1)} %collective-permute-done.8.refs_1_.refs_7_), custom_call_target="tpu_custom_call" | custom-call | flops 1024 | bytes 1024 | tf_op jit(solution)/shard_map/copy_rows/pallas_call | solution.py:74
  85.2 1.6 collective-permute-start.15
  87.3 10.7 %forward.7 = (f32[4,2,16,2048]{3,2,1,0:T(8,128)}, bf16[4,2,16,2048]{3,2,1,0:T(8,128)(2,1)}) custom-call(s32[3]{0:T(128)S(1)} %pad_add_fusion.place_ref, bf16[128,6144]{1,0:T(8,128)(2,1)} %collective-permute-done.7.refs_0_.refs_6_, bf16[128,6144]{1,0:T(8,128)(2,1)} %collective-permute-done.8.refs_1_.refs_7_, bf16[6144,2048]{1,0:T(8,128)(2,1)S(1)} %load.1.refs_2_), custom_call_target="tpu_custom_call" | custom-call | flops 1024 | bytes 1024 | tf_op jit(solution)/shard_map/forward/pallas_call | solution.py:147
  98.7 2.1 collective-permute-done.12.refs_1_
  100.8 1.2 copy-done.2
  103.5 3.6 %collective-permute-start.19 = (bf16[32,2048]{1,0:T(8,128)(2,1)S(1)}, bf16[32,2048]{1,0:T(8,128)(2,1)S(1)}, u32[]{:S(2)}, u32[]{:S(2)}) collective-permute-start(bf16[32,2048]{1,0:T(8,128)(2,1)S(1)} %get-tuple-element.110), channel_id=1, source_target_pairs={{0,6},{1,7},{2,4},{3,5},{4,2},{5,3},{6,0},{7,1},{8,14},{9,15},{10,... | collective-permute-start | bytes 393224 | tf_op jit(solution)/shard_map/ppermute | solution.py:22
  107.1 6.5 %forward.8 = (f32[4,1,16,2048]{3,2,1,0:T(8,128)}, bf16[4,1,16,2048]{3,2,1,0:T(8,128)(2,1)}) custom-call(s32[3]{0:T(128)S(1)} %pad_add_fusion.place_ref, bf16[64,6144]{1,0:T(8,128)(2,1)} %copy-done.12, bf16[64,6144]{1,0:T(8,128)(2,1)} %copy-done.13, bf16[6144,2048]{1,0:T(8,128)(2,1)S(1)} %load.1.refs_2_), custom_call_target="tpu_custom_call" | custom-call | flops 1024 | bytes 1024 | tf_op jit(solution)/shard_map/forward/pallas_call | solution.py:147
  114.9 6.5 %forward.9 = (f32[4,1,16,2048]{3,2,1,0:T(8,128)}, bf16[4,1,16,2048]{3,2,1,0:T(8,128)(2,1)}) custom-call(s32[3]{0:T(128)S(1)} %pad_add_fusion.place_ref, bf16[64,6144]{1,0:T(8,128)(2,1)} %copy-done.14, bf16[64,6144]{1,0:T(8,128)(2,1)} %copy-done.15, bf16[6144,2048]{1,0:T(8,128)(2,1)S(1)} %load.1.refs_2_), custom_call_target="tpu_custom_call" | custom-call | flops 1024 | bytes 1024 | tf_op jit(solution)/shard_map/forward/pallas_call | solution.py:147
  124.2 1.0 copy-done.5
  126.0 1.5 collective-permute-start.23
  127.5 2.9 %collective-permute-start.24 = (bf16[32,2048]{1,0:T(8,128)(2,1)S(1)}, bf16[32,2048]{1,0:T(8,128)(2,1)S(1)}, u32[]{:S(2)}, u32[]{:S(2)}) collective-permute-start(bf16[32,2048]{1,0:T(8,128)(2,1)S(1)} %get-tuple-element.124), channel_id=1, source_target_pairs={{0,6},{1,7},{2,4},{3,5},{4,2},{5,3},{6,0},{7,1},{8,14},{9,15},{10,... | collective-permute-start | bytes 393224 | tf_op jit(solution)/shard_map/ppermute | solution.py:22
  130.3 2.4 %collective-permute-done.22.refs_1_ = bf16[32,2048]{1,0:T(8,128)(2,1)S(1)} collective-permute-done((bf16[32,2048]{1,0:T(8,128)(2,1)S(1)}, bf16[32,2048]{1,0:T(8,128)(2,1)S(1)}, u32[]{:S(2)}, u32[]{:S(2)}) %collective-permute-start.22) | collective-permute-done | bytes 131104 | tf_op jit(solution)/shard_map/ppermute | solution.py:22
  132.7 6.2 %collective-permute-done.23.refs_2_ = bf16[32,2048]{1,0:T(8,128)(2,1)S(1)} collective-permute-done((bf16[32,2048]{1,0:T(8,128)(2,1)S(1)}, bf16[32,2048]{1,0:T(8,128)(2,1)S(1)}, u32[]{:S(2)}, u32[]{:S(2)}) %collective-permute-start.23) | collective-permute-done | bytes 131104 | tf_op jit(solution)/shard_map/ppermute | solution.py:22
  138.9 1.1 sum_rows.1
  140.0 1.5 collective-permute-start.27
  141.5 1.5 collective-permute-start.26
  143.6 1.7 collective-permute-done.27.refs_3_
  145.9 1.3 collective-permute-done.25.refs_1_
  147.3 1.3 gradient.1
  148.6 1.5 collective-permute-start.30
  150.0 2.6 %collective-permute-start.29 = (bf16[128,1152]{1,0:T(8,128)(2,1)S(1)}, bf16[128,1152]{1,0:T(8,128)(2,1)S(1)}, u32[]{:S(2)}, u32[]{:S(2)}) collective-permute-start(bf16[128,1152]{1,0:T(8,128)(2,1)S(1)} %get-tuple-element.129), channel_id=1, source_target_pairs={{0,4},{1,5},{2,6},{3,7},{4,0},{5,1},{6,2},{7,3},{8,12},{9,13},{10,... | collective-permute-start | bytes 884744 | tf_op jit(solution)/shard_map/ppermute | solution.py:22
  153.0 7.4 %collective-permute-done.30 = bf16[128,1152]{1,0:T(8,128)(2,1)S(1)} collective-permute-done((bf16[128,1152]{1,0:T(8,128)(2,1)S(1)}, bf16[128,1152]{1,0:T(8,128)(2,1)S(1)}, u32[]{:S(2)}, u32[]{:S(2)}) %collective-permute-start.30) | collective-permute-done | bytes 294944 | tf_op jit(solution)/shard_map/ppermute | solution.py:22
  160.4 15.7 %collective-permute-done.29 = bf16[128,1152]{1,0:T(8,128)(2,1)S(1)} collective-permute-done((bf16[128,1152]{1,0:T(8,128)(2,1)S(1)}, bf16[128,1152]{1,0:T(8,128)(2,1)S(1)}, u32[]{:S(2)}, u32[]{:S(2)}) %collective-permute-start.29) | collective-permute-done | bytes 294944 | tf_op jit(solution)/shard_map/ppermute | solution.py:22
  177.1 3.9 %collective-permute-start.35 = (bf16[128,1024]{1,0:T(8,128)(2,1)S(1)}, bf16[128,1024]{1,0:T(8,128)(2,1)S(1)}, u32[]{:S(2)}, u32[]{:S(2)}) collective-permute-start(bf16[128,1024]{1,0:T(8,128)(2,1)S(1)} %get-tuple-element.134), channel_id=1, source_target_pairs={{0,2},{1,3},{2,0},{3,1},{4,6},{5,7},{6,4},{7,5},{8,10},{9,11},{10,... | collective-permute-start | bytes 786440 | tf_op jit(solution)/shard_map/ppermute | solution.py:22
  181.8 18.9 %backward.2 = (bf16[6144,2048]{1,0:T(8,128)(2,1)}, f32[1,1]{1,0:T(1,128)}) custom-call(s32[3]{0:T(128)S(1)} %pad_add_fusion.place_ref, bf16[128,6144]{1,0:T(8,128)(2,1)} %get-tuple-element.72.refs_0_, bf16[128,6144]{1,0:T(8,128)(2,1)} %copy-done.11, bf16[128,6144]{1,0:T(8,128)(2,1)} %copy-done.10, bf16[64,6144]{1,0:T(8,128)(2,1)} %copy-done.12, ...), custom_call_target="tpu_custom_call" | custom-call | flops 1024 | bytes 1024 | tf_op jit(solution)/shard_map/backward/pallas_call | solution.py:392
  204.2 18.6 %backward.3 = bf16[6144,2048]{1,0:T(8,128)(2,1)} custom-call(s32[3]{0:T(128)S(1)} %pad_add_fusion.place_ref, bf16[128,6144]{1,0:T(8,128)(2,1)} %get-tuple-element.72.refs_0_, bf16[128,6144]{1,0:T(8,128)(2,1)} %copy-done.11, bf16[128,6144]{1,0:T(8,128)(2,1)} %copy-done.10, bf16[64,6144]{1,0:T(8,128)(2,1)} %copy-done.12, ...), custom_call_target="tpu_custom_call", output_to_operand_aliasing={{}: (19, {})} | custom-call | flops 1024 | bytes 1024 | tf_op jit(solution)/shard_map/backward/pallas_call | solution.py:392
  (143 shorter events, 18.6 us)
Async XLA Ops:
  4.3 38.5 %collective-permute-start.2 = (bf16[128,6144]{1,0:T(8,128)(2,1)}, bf16[128,6144]{1,0:T(8,128)(2,1)S(1)}, u32[]{:S(2)}, u32[]{:S(2)}) collective-permute-start(bf16[128,6144]{1,0:T(8,128)(2,1)} %get-tuple-element.72.refs_0_), channel_id=1, source_target_pairs={{0,16},{8,24},{16,0},{24,8},{1,17},{9,25},{17,1},{25,9},{2,18},{10... | collective-permute-start | bytes 4718600 | tf_op jit(solution)/shard_map/ppermute | solution.py:22
  7.4 38.6 %collective-permute-start.1 = (bf16[128,6144]{1,0:T(8,128)(2,1)}, bf16[128,6144]{1,0:T(8,128)(2,1)S(1)}, u32[]{:S(2)}, u32[]{:S(2)}) collective-permute-start(bf16[128,6144]{1,0:T(8,128)(2,1)} %get-tuple-element.72.refs_0_), channel_id=1, source_target_pairs={{0,8},{8,0},{16,24},{24,16},{1,9},{9,1},{17,25},{25,17},{2,10},{10... | collective-permute-start | bytes 4718600 | tf_op jit(solution)/shard_map/ppermute | solution.py:22
  8.9 67.8 %collective-permute-start.8 = (bf16[128,6144]{1,0:T(8,128)(2,1)}, bf16[128,6144]{1,0:T(8,128)(2,1)}, u32[]{:S(2)}, u32[]{:S(2)}) collective-permute-start(bf16[128,6144]{1,0:T(8,128)(2,1)} %get-tuple-element.73.refs_1_.refs_5_), channel_id=1, source_target_pairs={{0,16},{8,24},{16,0},{24,8},{1,17},{9,25},{17,1},{25,9},{2,18},{10... | collective-permute-start | bytes 4718600 | tf_op jit(solution)/shard_map/ppermute | solution.py:22
  9.4 69.3 %collective-permute-start.7 = (bf16[128,6144]{1,0:T(8,128)(2,1)}, bf16[128,6144]{1,0:T(8,128)(2,1)}, u32[]{:S(2)}, u32[]{:S(2)}) collective-permute-start(bf16[128,6144]{1,0:T(8,128)(2,1)} %get-tuple-element.73.refs_1_.refs_5_), channel_id=1, source_target_pairs={{0,8},{8,0},{16,24},{24,16},{1,9},{9,1},{17,25},{25,17},{2,10},{10... | collective-permute-start | bytes 4718600 | tf_op jit(solution)/shard_map/ppermute | solution.py:22
  34.5 2.2 collective-permute-start
  38.6 23.2 %collective-permute-start.3 = (bf16[32,2048]{1,0:T(8,128)(2,1)S(1)}, bf16[32,2048]{1,0:T(8,128)(2,1)S(1)}, u32[]{:S(2)}, u32[]{:S(2)}) collective-permute-start(bf16[32,2048]{1,0:T(8,128)(2,1)S(1)} %get-tuple-element.82), channel_id=1, source_target_pairs={{0,2},{1,3},{2,0},{3,1},{4,6},{5,7},{6,4},{7,5},{8,10},{9,11},{10,... | collective-permute-start | bytes 393224 | tf_op jit(solution)/shard_map/ppermute | solution.py:22
  42.8 19.0 %collective-permute-start.4 = (bf16[32,2048]{1,0:T(8,128)(2,1)S(1)}, bf16[32,2048]{1,0:T(8,128)(2,1)S(1)}, u32[]{:S(2)}, u32[]{:S(2)}) collective-permute-start(bf16[32,2048]{1,0:T(8,128)(2,1)S(1)} %get-tuple-element.83), channel_id=1, source_target_pairs={{0,4},{1,5},{2,6},{3,7},{4,0},{5,1},{6,2},{7,3},{8,12},{9,13},{10,... | collective-permute-start | bytes 393224 | tf_op jit(solution)/shard_map/ppermute | solution.py:22
  45.9 15.9 %collective-permute-start.5 = (bf16[32,2048]{1,0:T(8,128)(2,1)S(1)}, bf16[32,2048]{1,0:T(8,128)(2,1)S(1)}, u32[]{:S(2)}, u32[]{:S(2)}) collective-permute-start(bf16[32,2048]{1,0:T(8,128)(2,1)S(1)} %get-tuple-element.84), channel_id=1, source_target_pairs={{0,6},{1,7},{2,4},{3,5},{4,2},{5,3},{6,0},{7,1},{8,14},{9,15},{10,... | collective-permute-start | bytes 393224 | tf_op jit(solution)/shard_map/ppermute | solution.py:22
  51.4 25.3 %copy-start.30 = (bf16[64,6144]{1,0:T(8,128)(2,1)S(1)}, bf16[64,6144]{1,0:T(8,128)(2,1)}, u32[]{:S(2)}) copy-start(bf16[64,6144]{1,0:T(8,128)(2,1)} %get-tuple-element.87) | copy-start | bytes 2359300
  62.5 2.2 collective-permute-start.6
  66.5 18.7 %collective-permute-start.9 = (bf16[32,2048]{1,0:T(8,128)(2,1)S(1)}, bf16[32,2048]{1,0:T(8,128)(2,1)S(1)}, u32[]{:S(2)}, u32[]{:S(2)}) collective-permute-start(bf16[32,2048]{1,0:T(8,128)(2,1)S(1)} %get-tuple-element.95), channel_id=1, source_target_pairs={{0,2},{1,3},{2,0},{3,1},{4,6},{5,7},{6,4},{7,5},{8,10},{9,11},{10,... | collective-permute-start | bytes 393224 | tf_op jit(solution)/shard_map/ppermute | solution.py:22
  66.8 20.0 %collective-permute-start.10 = (bf16[32,2048]{1,0:T(8,128)(2,1)S(1)}, bf16[32,2048]{1,0:T(8,128)(2,1)S(1)}, u32[]{:S(2)}, u32[]{:S(2)}) collective-permute-start(bf16[32,2048]{1,0:T(8,128)(2,1)S(1)} %get-tuple-element.96), channel_id=1, source_target_pairs={{0,4},{1,5},{2,6},{3,7},{4,0},{5,1},{6,2},{7,3},{8,12},{9,13},{10,... | collective-permute-start | bytes 393224 | tf_op jit(solution)/shard_map/ppermute | solution.py:22
  68.4 34.3 %collective-permute-start.13 = (bf16[64,6144]{1,0:T(8,128)(2,1)S(1)}, bf16[64,6144]{1,0:T(8,128)(2,1)S(1)}, u32[]{:S(2)}, u32[]{:S(2)}) collective-permute-start(bf16[64,6144]{1,0:T(8,128)(2,1)S(1)} %copy-done.31), channel_id=1, source_target_pairs={{0,16},{8,24},{16,0},{24,8},{1,17},{9,25},{17,1},{25,9},{2,18},{10... | collective-permute-start | bytes 2359304 | tf_op jit(solution)/shard_map/ppermute | solution.py:22
  76.6 26.9 %collective-permute-start.14 = (bf16[64,6144]{1,0:T(8,128)(2,1)S(1)}, bf16[64,6144]{1,0:T(8,128)(2,1)S(1)}, u32[]{:S(2)}, u32[]{:S(2)}) collective-permute-start(bf16[64,6144]{1,0:T(8,128)(2,1)S(1)} %copy-done.30), channel_id=1, source_target_pairs={{0,8},{8,0},{16,24},{24,16},{1,9},{9,1},{17,25},{25,17},{2,10},{10... | collective-permute-start | bytes 2359304 | tf_op jit(solution)/shard_map/ppermute | solution.py:22
  78.7 19.3 %collective-permute-start.11 = (bf16[32,2048]{1,0:T(8,128)(2,1)S(1)}, bf16[32,2048]{1,0:T(8,128)(2,1)S(1)}, u32[]{:S(2)}, u32[]{:S(2)}) collective-permute-start(bf16[32,2048]{1,0:T(8,128)(2,1)S(1)} %get-tuple-element.97), channel_id=1, source_target_pairs={{0,6},{1,7},{2,4},{3,5},{4,2},{5,3},{6,0},{7,1},{8,14},{9,15},{10,... | collective-permute-start | bytes 393224 | tf_op jit(solution)/shard_map/ppermute | solution.py:22
  85.2 28.4 %collective-permute-start.15 = (bf16[64,6144]{1,0:T(8,128)(2,1)}, bf16[64,6144]{1,0:T(8,128)(2,1)S(1)}, u32[]{:S(2)}, u32[]{:S(2)}) collective-permute-start(bf16[64,6144]{1,0:T(8,128)(2,1)} %get-tuple-element.99), channel_id=1, source_target_pairs={{0,16},{8,24},{16,0},{24,8},{1,17},{9,25},{17,1},{25,9},{2,18},{10... | collective-permute-start | bytes 2359304 | tf_op jit(solution)/shard_map/ppermute | solution.py:22
  86.8 26.8 %collective-permute-start.16 = (bf16[64,6144]{1,0:T(8,128)(2,1)}, bf16[64,6144]{1,0:T(8,128)(2,1)S(1)}, u32[]{:S(2)}, u32[]{:S(2)}) collective-permute-start(bf16[64,6144]{1,0:T(8,128)(2,1)} %get-tuple-element.100), channel_id=1, source_target_pairs={{0,8},{8,0},{16,24},{24,16},{1,9},{9,1},{17,25},{25,17},{2,10},{10... | collective-permute-start | bytes 2359304 | tf_op jit(solution)/shard_map/ppermute | solution.py:22
  98.6 2.2 collective-permute-start.12
  102.7 18.7 %collective-permute-start.17 = (bf16[32,2048]{1,0:T(8,128)(2,1)S(1)}, bf16[32,2048]{1,0:T(8,128)(2,1)S(1)}, u32[]{:S(2)}, u32[]{:S(2)}) collective-permute-start(bf16[32,2048]{1,0:T(8,128)(2,1)S(1)} %get-tuple-element.108), channel_id=1, source_target_pairs={{0,2},{1,3},{2,0},{3,1},{4,6},{5,7},{6,4},{7,5},{8,10},{9,11},{10,... | collective-permute-start | bytes 393224 | tf_op jit(solution)/shard_map/ppermute | solution.py:22
  102.8 18.6 %collective-permute-start.18 = (bf16[32,2048]{1,0:T(8,128)(2,1)S(1)}, bf16[32,2048]{1,0:T(8,128)(2,1)S(1)}, u32[]{:S(2)}, u32[]{:S(2)}) collective-permute-start(bf16[32,2048]{1,0:T(8,128)(2,1)S(1)} %get-tuple-element.109), channel_id=1, source_target_pairs={{0,4},{1,5},{2,6},{3,7},{4,0},{5,1},{6,2},{7,3},{8,12},{9,13},{10,... | collective-permute-start | bytes 393224 | tf_op jit(solution)/shard_map/ppermute | solution.py:22
  103.5 17.9 %collective-permute-start.19 = (bf16[32,2048]{1,0:T(8,128)(2,1)S(1)}, bf16[32,2048]{1,0:T(8,128)(2,1)S(1)}, u32[]{:S(2)}, u32[]{:S(2)}) collective-permute-start(bf16[32,2048]{1,0:T(8,128)(2,1)S(1)} %get-tuple-element.110), channel_id=1, source_target_pairs={{0,6},{1,7},{2,4},{3,5},{4,2},{5,3},{6,0},{7,1},{8,14},{9,15},{10,... | collective-permute-start | bytes 393224 | tf_op jit(solution)/shard_map/ppermute | solution.py:22
  114.8 24.1 %copy-start = (bf16[128,2048]{1,0:T(8,128)(2,1)S(1)}, bf16[128,2048]{1,0:T(8,128)(2,1)}, u32[]{:S(2)}) copy-start(bf16[128,2048]{1,0:T(8,128)(2,1)} %take_targets.1.target_ref) | copy-start | bytes 1572868
  114.9 24.1 %copy-start.8 = (f32[2048]{0:T(1024)S(1)}, f32[2048]{0:T(1024)}, u32[]{:S(2)}) copy-start(f32[2048]{0:T(1024)} %param.7) | copy-start | bytes 24580
  122.0 1.6 collective-permute-start.20
  122.1 2.1 collective-permute-start.21
  125.9 6.9 %collective-permute-start.22 = (bf16[32,2048]{1,0:T(8,128)(2,1)S(1)}, bf16[32,2048]{1,0:T(8,128)(2,1)S(1)}, u32[]{:S(2)}, u32[]{:S(2)}) collective-permute-start(bf16[32,2048]{1,0:T(8,128)(2,1)S(1)} %get-tuple-element.122), channel_id=1, source_target_pairs={{0,2},{1,3},{2,0},{3,1},{4,6},{5,7},{6,4},{7,5},{8,10},{9,11},{10,... | collective-permute-start | bytes 393224 | tf_op jit(solution)/shard_map/ppermute | solution.py:22
  126.0 13.0 %collective-permute-start.23 = (bf16[32,2048]{1,0:T(8,128)(2,1)S(1)}, bf16[32,2048]{1,0:T(8,128)(2,1)S(1)}, u32[]{:S(2)}, u32[]{:S(2)}) collective-permute-start(bf16[32,2048]{1,0:T(8,128)(2,1)S(1)} %get-tuple-element.123), channel_id=1, source_target_pairs={{0,4},{1,5},{2,6},{3,7},{4,0},{5,1},{6,2},{7,3},{8,12},{9,13},{10,... | collective-permute-start | bytes 393224 | tf_op jit(solution)/shard_map/ppermute | solution.py:22
  127.5 11.5 %collective-permute-start.24 = (bf16[32,2048]{1,0:T(8,128)(2,1)S(1)}, bf16[32,2048]{1,0:T(8,128)(2,1)S(1)}, u32[]{:S(2)}, u32[]{:S(2)}) collective-permute-start(bf16[32,2048]{1,0:T(8,128)(2,1)S(1)} %get-tuple-element.124), channel_id=1, source_target_pairs={{0,6},{1,7},{2,4},{3,5},{4,2},{5,3},{6,0},{7,1},{8,14},{9,15},{10,... | collective-permute-start | bytes 393224 | tf_op jit(solution)/shard_map/ppermute | solution.py:22
  140.0 5.2 %collective-permute-start.27 = (f32[128,128]{1,0:T(8,128)S(1)}, f32[128,128]{1,0:T(8,128)S(1)}, u32[]{:S(2)}, u32[]{:S(2)}) collective-permute-start(f32[128,128]{1,0:T(8,128)S(1)} %get-tuple-element.127.refs_0_), channel_id=1, source_target_pairs={{0,24},{8,16},{16,8},{24,0},{1,25},{9,17},{17,9},{25,1},{2,26},{10... | collective-permute-start | bytes 196616 | tf_op jit(solution)/shard_map/ppermute | solution.py:22
  141.5 4.4 %collective-permute-start.26 = (f32[128,128]{1,0:T(8,128)S(1)}, f32[128,128]{1,0:T(8,128)S(1)}, u32[]{:S(2)}, u32[]{:S(2)}) collective-permute-start(f32[128,128]{1,0:T(8,128)S(1)} %get-tuple-element.127.refs_0_), channel_id=1, source_target_pairs={{0,16},{8,24},{16,0},{24,8},{1,17},{9,25},{17,1},{25,9},{2,18},{10... | collective-permute-start | bytes 196616 | tf_op jit(solution)/shard_map/ppermute | solution.py:22
  143.0 4.3 %collective-permute-start.25 = (f32[128,128]{1,0:T(8,128)S(1)}, f32[128,128]{1,0:T(8,128)S(1)}, u32[]{:S(2)}, u32[]{:S(2)}) collective-permute-start(f32[128,128]{1,0:T(8,128)S(1)} %get-tuple-element.127.refs_0_), channel_id=1, source_target_pairs={{0,8},{8,0},{16,24},{24,16},{1,9},{9,1},{17,25},{25,17},{2,10},{10... | collective-permute-start | bytes 196616 | tf_op jit(solution)/shard_map/ppermute | solution.py:22
  148.6 32.5 %copy-start.6 = (bf16[128,1152]{1,0:T(8,128)(2,1)}, bf16[128,1152]{1,0:T(8,128)(2,1)S(1)}, u32[]{:S(2)}) copy-start(bf16[128,1152]{1,0:T(8,128)(2,1)S(1)} %get-tuple-element.129) | copy-start | bytes 884740
  148.6 52.2 %copy-start.7 = (bf16[128,1024]{1,0:T(8,128)(2,1)}, bf16[128,1024]{1,0:T(8,128)(2,1)S(1)}, u32[]{:S(2)}) copy-start(bf16[128,1024]{1,0:T(8,128)(2,1)S(1)} %get-tuple-element.134) | copy-start | bytes 786436
  148.6 11.8 %collective-permute-start.30 = (bf16[128,1152]{1,0:T(8,128)(2,1)S(1)}, bf16[128,1152]{1,0:T(8,128)(2,1)S(1)}, u32[]{:S(2)}, u32[]{:S(2)}) collective-permute-start(bf16[128,1152]{1,0:T(8,128)(2,1)S(1)} %get-tuple-element.129), channel_id=1, source_target_pairs={{0,6},{1,7},{2,4},{3,5},{4,2},{5,3},{6,0},{7,1},{8,14},{9,15},{10,... | collective-permute-start | bytes 884744 | tf_op jit(solution)/shard_map/ppermute | solution.py:22
  150.0 26.1 %collective-permute-start.29 = (bf16[128,1152]{1,0:T(8,128)(2,1)S(1)}, bf16[128,1152]{1,0:T(8,128)(2,1)S(1)}, u32[]{:S(2)}, u32[]{:S(2)}) collective-permute-start(bf16[128,1152]{1,0:T(8,128)(2,1)S(1)} %get-tuple-element.129), channel_id=1, source_target_pairs={{0,4},{1,5},{2,6},{3,7},{4,0},{5,1},{6,2},{7,3},{8,12},{9,13},{10,... | collective-permute-start | bytes 884744 | tf_op jit(solution)/shard_map/ppermute | solution.py:22
  152.7 23.4 %collective-permute-start.28 = (bf16[128,1152]{1,0:T(8,128)(2,1)S(1)}, bf16[128,1152]{1,0:T(8,128)(2,1)S(1)}, u32[]{:S(2)}, u32[]{:S(2)}) collective-permute-start(bf16[128,1152]{1,0:T(8,128)(2,1)S(1)} %get-tuple-element.129), channel_id=1, source_target_pairs={{0,2},{1,3},{2,0},{3,1},{4,6},{5,7},{6,4},{7,5},{8,10},{9,11},{10,... | collective-permute-start | bytes 884744 | tf_op jit(solution)/shard_map/ppermute | solution.py:22
  153.0 24.0 %collective-permute-start.31 = (bf16[128,1152]{1,0:T(8,128)(2,1)S(1)}, bf16[128,1152]{1,0:T(8,128)(2,1)S(1)}, u32[]{:S(2)}, u32[]{:S(2)}) collective-permute-start(bf16[128,1152]{1,0:T(8,128)(2,1)S(1)} %get-tuple-element.129), channel_id=1, source_target_pairs={{0,1},{1,0},{2,3},{3,2},{4,5},{5,4},{6,7},{7,6},{8,9},{9,8},{10,11... | collective-permute-start | bytes 884744 | tf_op jit(solution)/shard_map/ppermute | solution.py:22
  160.4 20.6 %copy-start.16 = (bf16[128,1152]{1,0:T(8,128)(2,1)}, bf16[128,1152]{1,0:T(8,128)(2,1)S(1)}, u32[]{:S(2)}) copy-start(bf16[128,1152]{1,0:T(8,128)(2,1)S(1)} %collective-permute-done.30) | copy-start | bytes 884740
  160.4 16.7 %collective-permute-start.34 = (bf16[128,1152]{1,0:T(8,128)(2,1)S(1)}, bf16[128,1152]{1,0:T(8,128)(2,1)S(1)}, u32[]{:S(2)}, u32[]{:S(2)}) collective-permute-start(bf16[128,1152]{1,0:T(8,128)(2,1)S(1)} %collective-permute-done.30), channel_id=1, source_target_pairs={{0,1},{1,0},{2,3},{3,2},{4,5},{5,4},{6,7},{7,6},{8,9},{9,8},{10,11... | collective-permute-start | bytes 884744 | tf_op jit(solution)/shard_map/ppermute | solution.py:22
  176.1 4.9 %collective-permute-start.33 = (bf16[128,1152]{1,0:T(8,128)(2,1)S(1)}, bf16[128,1152]{1,0:T(8,128)(2,1)S(1)}, u32[]{:S(2)}, u32[]{:S(2)}) collective-permute-start(bf16[128,1152]{1,0:T(8,128)(2,1)S(1)} %collective-permute-done.29), channel_id=1, source_target_pairs={{0,1},{1,0},{2,3},{3,2},{4,5},{5,4},{6,7},{7,6},{8,9},{9,8},{10,11... | collective-permute-start | bytes 884744 | tf_op jit(solution)/shard_map/ppermute | solution.py:22
  176.1 4.9 %collective-permute-start.32 = (bf16[128,1152]{1,0:T(8,128)(2,1)S(1)}, bf16[128,1152]{1,0:T(8,128)(2,1)S(1)}, u32[]{:S(2)}, u32[]{:S(2)}) collective-permute-start(bf16[128,1152]{1,0:T(8,128)(2,1)S(1)} %collective-permute-done.28), channel_id=1, source_target_pairs={{0,1},{1,0},{2,3},{3,2},{4,5},{5,4},{6,7},{7,6},{8,9},{9,8},{10,11... | collective-permute-start | bytes 884744 | tf_op jit(solution)/shard_map/ppermute | solution.py:22
  176.6 24.1 %collective-permute-start.37 = (bf16[128,1024]{1,0:T(8,128)(2,1)S(1)}, bf16[128,1024]{1,0:T(8,128)(2,1)S(1)}, u32[]{:S(2)}, u32[]{:S(2)}) collective-permute-start(bf16[128,1024]{1,0:T(8,128)(2,1)S(1)} %get-tuple-element.134), channel_id=1, source_target_pairs={{0,6},{1,7},{2,4},{3,5},{4,2},{5,3},{6,0},{7,1},{8,14},{9,15},{10,... | collective-permute-start | bytes 786440 | tf_op jit(solution)/shard_map/ppermute | solution.py:22
  177.1 23.7 %collective-permute-start.36 = (bf16[128,1024]{1,0:T(8,128)(2,1)S(1)}, bf16[128,1024]{1,0:T(8,128)(2,1)S(1)}, u32[]{:S(2)}, u32[]{:S(2)}) collective-permute-start(bf16[128,1024]{1,0:T(8,128)(2,1)S(1)} %get-tuple-element.134), channel_id=1, source_target_pairs={{0,4},{1,5},{2,6},{3,7},{4,0},{5,1},{6,2},{7,3},{8,12},{9,13},{10,... | collective-permute-start | bytes 786440 | tf_op jit(solution)/shard_map/ppermute | solution.py:22
  177.1 23.7 %collective-permute-start.35 = (bf16[128,1024]{1,0:T(8,128)(2,1)S(1)}, bf16[128,1024]{1,0:T(8,128)(2,1)S(1)}, u32[]{:S(2)}, u32[]{:S(2)}) collective-permute-start(bf16[128,1024]{1,0:T(8,128)(2,1)S(1)} %get-tuple-element.134), channel_id=1, source_target_pairs={{0,2},{1,3},{2,0},{3,1},{4,6},{5,7},{6,4},{7,5},{8,10},{9,11},{10,... | collective-permute-start | bytes 786440 | tf_op jit(solution)/shard_map/ppermute | solution.py:22
  200.8 1.6 collective-permute-start.38
  200.9 1.9 collective-permute-start.39
  201.4 1.8 collective-permute-start.40
  201.5 2.1 collective-permute-start.41
  (27 other events, 97.1 us)

commit v5 on v4

--- a/solution.py
+++ b/solution.py
@@ -146,7 +146,7 @@
     shape = (slots, count, ROWS, units)
     keep, send = pl.pallas_call(
         functools.partial(forward_kernel, len(parts), tile),
-        in_specs=[SMEM] + [HBM] * len(parts) + [VMEM],
+        in_specs=[SMEM] + [pl.BlockSpec(memory_space=pl.ANY)] * len(parts) + [VMEM],
         out_specs=[HBM, HBM],
         out_shape=[pltpu.HBM(shape, f32), pltpu.HBM(shape, bf16)],
         scratch_shapes=[
@@ -159,7 +159,7 @@
         compiler_params=params(12),
         cost_estimate=cost(),
         name="forward",
-    )(place, *in_hbm(*parts), weight)
+    )(place, *(parts if total_rows <= 128 else in_hbm(*parts)), weight)
     shape = (slots, count * ROWS, units)
     return keep.reshape(shape), send.reshape(shape)
 

time: 224 us -> 219 us (0.978)
    pallas_call x5, Pallas kernels: 44.5 us -> 42.3 us  [forward(): pl.pallas_call(functools.partial(forward_kernel, len(parts), tile), in_sp...]
    unnamed x66 -> x64, local copies, waits for them, and re-layouts: 7.44 us -> 6.26 us
where the time goes in v5:
time: 219 us; the launch traced here: 218 us
  Pallas kernels  107 us (49%)
  waiting for transfers between devices  52.7 us (24%)
  starting transfers between devices  47.7 us (22%)
  local copies, waits for them, and re-layouts  8.14 us (4%)
    ppermute x42, waiting for transfers between devices, exchange(): return lax.ppermute(value, axis, [(i, i ^ mask) for i in range(size)])  52.7 us
    ppermute x42, starting transfers between devices, exchange(): return lax.ppermute(value, axis, [(i, i ^ mask) for i in range(size)])  47.7 us
    pallas_call x5, Pallas kernels, forward(): pl.pallas_call(functools.partial(forward_kernel, len(parts), tile), in_sp...  42.3 us
    pallas_call x2, Pallas kernels, backward(): pl.pallas_call(functools.partial(backward_kernel, len(parts), len(pieces)...  37.5 us
    pallas_call x3, Pallas kernels, copy_rows(): pl.pallas_call(functools.partial(copy_kernel, [(start, size) for _, start...  9.38 us
    pallas_call x1, Pallas kernels, load(): pl.pallas_call(load_kernel, in_specs=[SMEM, HBM], out_specs=VMEM, out_sha...  8.71 us
    unnamed x64, local copies, waits for them, and re-layouts  6.26 us
  transfers between devices with their start and end apart: 42, of which 18 were waited for; matrix products, arithmetic and copies ran while one was open for 1% of the time, Pallas kernels for 37%

profile of v5, /device:TPU:0, one launch (start us, length us, event | category | flops | bytes accessed | tf_op | source)
XLA Modules:
  0.0 218.3 jit_solution(2383451954187766109)
XLA Ops:
  0.7 3.6 %copy_rows.3 = (bf16[128,6144]{1,0:T(8,128)(2,1)}, bf16[128,6144]{1,0:T(8,128)(2,1)}) custom-call(s32[3]{0:T(128)S(1)} %pad_add_fusion.place_ref, bf16[256,6144]{1,0:T(8,128)(2,1)} %refs_1_.1, bf16[256,6144]{1,0:T(8,128)(2,1)} %refs_1_.1), custom_call_target="tpu_custom_call" | custom-call | flops 1024 | bytes 1024 | tf_op jit(solution)/shard_map/copy_rows/pallas_call | solution.py:74
  4.3 3.0 %collective-permute-start.2 = (bf16[128,6144]{1,0:T(8,128)(2,1)}, bf16[128,6144]{1,0:T(8,128)(2,1)S(1)}, u32[]{:S(2)}, u32[]{:S(2)}) collective-permute-start(bf16[128,6144]{1,0:T(8,128)(2,1)} %get-tuple-element.72.refs_0_), channel_id=1, source_target_pairs={{0,16},{8,24},{16,0},{24,8},{1,17},{9,25},{17,1},{25,9},{2,18},{10... | collective-permute-start | bytes 4718600 | tf_op jit(solution)/shard_map/ppermute | solution.py:22
  7.4 1.5 collective-permute-start.1
  11.5 1.2 gather_fusion
  12.9 2.5 %take_targets.1.target_ref = bf16[128,2048]{1,0:T(8,128)(2,1)} custom-call(s32[3]{0:T(128)S(1)} %pad_add_fusion.place_ref, bf16[1024,2048]{1,0:T(8,128)(2,1)} %target_ref.1), custom_call_target="tpu_custom_call" | custom-call | flops 1024 | bytes 1024 | tf_op jit(solution)/shard_map/take_targets/pallas_call | solution.py:238
  15.4 8.7 %load.1.refs_2_ = bf16[6144,2048]{1,0:T(8,128)(2,1)S(1)} custom-call(s32[3]{0:T(128)S(1)} %pad_add_fusion.place_ref, bf16[6144,2048]{1,0:T(8,128)(2,1)} %source_ref.1), custom_call_target="tpu_custom_call" | custom-call | flops 1024 | bytes 1024 | tf_op jit(solution)/shard_map/load/pallas_call | solution.py:92
  24.1 10.5 %forward.5 = (f32[4,2,16,2048]{3,2,1,0:T(8,128)}, bf16[4,2,16,2048]{3,2,1,0:T(8,128)(2,1)}) custom-call(s32[3]{0:T(128)S(1)} %pad_add_fusion.place_ref, bf16[128,6144]{1,0:T(8,128)(2,1)} %get-tuple-element.72.refs_0_, bf16[128,6144]{1,0:T(8,128)(2,1)} %get-tuple-element.73.refs_1_.refs_5_, bf16[6144,2048]{1,0:T(8,128)(2,1)S(1)} %load.1.refs_2_), custom_call_target="tpu_custom_call" | custom-call | flops 1024 | bytes 1024 | tf_op jit(solution)/shard_map/forward/pallas_call | solution.py:147
  34.6 2.1 collective-permute-done.refs_1_
  36.7 1.2 copy-done.7
  38.6 2.1 collective-permute-start.3
  40.7 2.1 collective-permute-done.2.refs_1_.refs_2_
  42.8 3.1 %collective-permute-start.4 = (bf16[32,2048]{1,0:T(8,128)(2,1)S(1)}, bf16[32,2048]{1,0:T(8,128)(2,1)S(1)}, u32[]{:S(2)}, u32[]{:S(2)}) collective-permute-start(bf16[32,2048]{1,0:T(8,128)(2,1)S(1)} %get-tuple-element.83), channel_id=1, source_target_pairs={{0,4},{1,5},{2,6},{3,7},{4,0},{5,1},{6,2},{7,3},{8,12},{9,13},{10,... | collective-permute-start | bytes 393224 | tf_op jit(solution)/shard_map/ppermute | solution.py:22
  45.9 2.7 %collective-permute-start.5 = (bf16[32,2048]{1,0:T(8,128)(2,1)S(1)}, bf16[32,2048]{1,0:T(8,128)(2,1)S(1)}, u32[]{:S(2)}, u32[]{:S(2)}) collective-permute-start(bf16[32,2048]{1,0:T(8,128)(2,1)S(1)} %get-tuple-element.84), channel_id=1, source_target_pairs={{0,6},{1,7},{2,4},{3,5},{4,2},{5,3},{6,0},{7,1},{8,14},{9,15},{10,... | collective-permute-start | bytes 393224 | tf_op jit(solution)/shard_map/ppermute | solution.py:22
  48.6 2.8 %copy_rows.4 = (bf16[64,6144]{1,0:T(8,128)(2,1)}, bf16[64,6144]{1,0:T(8,128)(2,1)}) custom-call(s32[3]{0:T(128)S(1)} %pad_add_fusion.place_ref, bf16[128,6144]{1,0:T(8,128)(2,1)} %collective-permute-done.1.refs_0_.refs_1_, bf16[128,6144]{1,0:T(8,128)(2,1)} %copy-done.14), custom_call_target="tpu_custom_call" | custom-call | flops 1024 | bytes 1024 | tf_op jit(solution)/shard_map/copy_rows/pallas_call | solution.py:74
  51.5 10.5 %forward.6 = (f32[4,2,16,2048]{3,2,1,0:T(8,128)}, bf16[4,2,16,2048]{3,2,1,0:T(8,128)(2,1)}) custom-call(s32[3]{0:T(128)S(1)} %pad_add_fusion.place_ref, bf16[128,6144]{1,0:T(8,128)(2,1)} %collective-permute-done.1.refs_0_.refs_1_, bf16[128,6144]{1,0:T(8,128)(2,1)} %copy-done.14, bf16[6144,2048]{1,0:T(8,128)(2,1)S(1)} %load.1.refs_2_), custom_call_target="tpu_custom_call" | custom-call | flops 1024 | bytes 1024 | tf_op jit(solution)/shard_map/forward/pallas_call | solution.py:147
  62.7 2.1 collective-permute-done.6.refs_1_
  64.8 1.2 copy-done.5
  66.7 1.7 collective-permute-start.10
  68.4 1.5 collective-permute-start.13
  70.0 6.7 %collective-permute-done.8.refs_1_.refs_7_ = bf16[128,6144]{1,0:T(8,128)(2,1)} collective-permute-done((bf16[128,6144]{1,0:T(8,128)(2,1)}, bf16[128,6144]{1,0:T(8,128)(2,1)}, u32[]{:S(2)}, u32[]{:S(2)}) %collective-permute-start.8) | collective-permute-done | bytes 1572896 | tf_op jit(solution)/shard_map/ppermute | solution.py:22
  76.6 2.0 collective-permute-start.14
  78.7 3.6 %collective-permute-start.11 = (bf16[32,2048]{1,0:T(8,128)(2,1)S(1)}, bf16[32,2048]{1,0:T(8,128)(2,1)S(1)}, u32[]{:S(2)}, u32[]{:S(2)}) collective-permute-start(bf16[32,2048]{1,0:T(8,128)(2,1)S(1)} %get-tuple-element.97), channel_id=1, source_target_pairs={{0,6},{1,7},{2,4},{3,5},{4,2},{5,3},{6,0},{7,1},{8,14},{9,15},{10,... | collective-permute-start | bytes 393224 | tf_op jit(solution)/shard_map/ppermute | solution.py:22
  82.3 2.9 %copy_rows.5 = (bf16[64,6144]{1,0:T(8,128)(2,1)}, bf16[64,6144]{1,0:T(8,128)(2,1)}) custom-call(s32[3]{0:T(128)S(1)} %pad_add_fusion.place_ref, bf16[128,6144]{1,0:T(8,128)(2,1)} %collective-permute-done.7.refs_0_.refs_6_, bf16[128,6144]{1,0:T(8,128)(2,1)} %collective-permute-done.8.refs_1_.refs_7_), custom_call_target="tpu_custom_call" | custom-call | flops 1024 | bytes 1024 | tf_op jit(solution)/shard_map/copy_rows/pallas_call | solution.py:74
  85.2 1.6 collective-permute-start.15
  87.3 10.7 %forward.7 = (f32[4,2,16,2048]{3,2,1,0:T(8,128)}, bf16[4,2,16,2048]{3,2,1,0:T(8,128)(2,1)}) custom-call(s32[3]{0:T(128)S(1)} %pad_add_fusion.place_ref, bf16[128,6144]{1,0:T(8,128)(2,1)} %collective-permute-done.7.refs_0_.refs_6_, bf16[128,6144]{1,0:T(8,128)(2,1)} %collective-permute-done.8.refs_1_.refs_7_, bf16[6144,2048]{1,0:T(8,128)(2,1)S(1)} %load.1.refs_2_), custom_call_target="tpu_custom_call" | custom-call | flops 1024 | bytes 1024 | tf_op jit(solution)/shard_map/forward/pallas_call | solution.py:147
  98.7 2.1 collective-permute-done.12.refs_1_
  100.8 1.2 copy-done.6
  103.5 3.6 %collective-permute-start.19 = (bf16[32,2048]{1,0:T(8,128)(2,1)S(1)}, bf16[32,2048]{1,0:T(8,128)(2,1)S(1)}, u32[]{:S(2)}, u32[]{:S(2)}) collective-permute-start(bf16[32,2048]{1,0:T(8,128)(2,1)S(1)} %get-tuple-element.110), channel_id=1, source_target_pairs={{0,6},{1,7},{2,4},{3,5},{4,2},{5,3},{6,0},{7,1},{8,14},{9,15},{10,... | collective-permute-start | bytes 393224 | tf_op jit(solution)/shard_map/ppermute | solution.py:22
  107.2 5.2 %forward.8 = (f32[4,1,16,2048]{3,2,1,0:T(8,128)}, bf16[4,1,16,2048]{3,2,1,0:T(8,128)(2,1)}) custom-call(s32[3]{0:T(128)S(1)} %pad_add_fusion.place_ref, bf16[64,6144]{1,0:T(8,128)(2,1)S(1)} %collective-permute-done.13.refs_0_.refs_3_, bf16[64,6144]{1,0:T(8,128)(2,1)S(1)} %collective-permute-done.14.refs_1_.refs_4_, bf16[6144,2048]{1,0:T(8,128)(2,1)S(1)} %load.1.refs_2_), custom_call_target="tpu_custom_call" | custom-call | flops 1024 | bytes 1024 | tf_op jit(solution)/shard_map/forward/pallas_call | solution.py:147
  112.5 5.5 %forward.9 = (f32[4,1,16,2048]{3,2,1,0:T(8,128)}, bf16[4,1,16,2048]{3,2,1,0:T(8,128)(2,1)}) custom-call(s32[3]{0:T(128)S(1)} %pad_add_fusion.place_ref, bf16[64,6144]{1,0:T(8,128)(2,1)S(1)} %collective-permute-done.15.refs_0_.refs_8_, bf16[64,6144]{1,0:T(8,128)(2,1)S(1)} %collective-permute-done.16.refs_1_.refs_9_, bf16[6144,2048]{1,0:T(8,128)(2,1)S(1)} %load.1.refs_2_), custom_call_target="tpu_custom_call" | custom-call | flops 1024 | bytes 1024 | tf_op jit(solution)/shard_map/forward/pallas_call | solution.py:147
  120.8 1.0 copy-done.9
  123.0 2.6 %collective-permute-start.23 = (bf16[32,2048]{1,0:T(8,128)(2,1)S(1)}, bf16[32,2048]{1,0:T(8,128)(2,1)S(1)}, u32[]{:S(2)}, u32[]{:S(2)}) collective-permute-start(bf16[32,2048]{1,0:T(8,128)(2,1)S(1)} %get-tuple-element.123), channel_id=1, source_target_pairs={{0,4},{1,5},{2,6},{3,7},{4,0},{5,1},{6,2},{7,3},{8,12},{9,13},{10,... | collective-permute-start | bytes 393224 | tf_op jit(solution)/shard_map/ppermute | solution.py:22
  125.6 1.4 collective-permute-start.24
  127.0 3.4 %collective-permute-done.22.refs_1_ = bf16[32,2048]{1,0:T(8,128)(2,1)S(1)} collective-permute-done((bf16[32,2048]{1,0:T(8,128)(2,1)S(1)}, bf16[32,2048]{1,0:T(8,128)(2,1)S(1)}, u32[]{:S(2)}, u32[]{:S(2)}) %collective-permute-start.22) | collective-permute-done | bytes 131104 | tf_op jit(solution)/shard_map/ppermute | solution.py:22
  130.3 5.5 %collective-permute-done.23.refs_2_ = bf16[32,2048]{1,0:T(8,128)(2,1)S(1)} collective-permute-done((bf16[32,2048]{1,0:T(8,128)(2,1)S(1)}, bf16[32,2048]{1,0:T(8,128)(2,1)S(1)}, u32[]{:S(2)}, u32[]{:S(2)}) %collective-permute-start.23) | collective-permute-done | bytes 131104 | tf_op jit(solution)/shard_map/ppermute | solution.py:22
  135.9 1.1 sum_rows.1
  136.9 2.5 %collective-permute-start.27 = (f32[128,128]{1,0:T(8,128)S(1)}, f32[128,128]{1,0:T(8,128)S(1)}, u32[]{:S(2)}, u32[]{:S(2)}) collective-permute-start(f32[128,128]{1,0:T(8,128)S(1)} %get-tuple-element.127.refs_0_), channel_id=1, source_target_pairs={{0,24},{8,16},{16,8},{24,0},{1,25},{9,17},{17,9},{25,1},{2,26},{10... | collective-permute-start | bytes 196616 | tf_op jit(solution)/shard_map/ppermute | solution.py:22
  140.5 1.9 collective-permute-done.27.refs_3_
  142.4 1.3 collective-permute-done.26.refs_2_
  144.2 1.1 gradient.1
  145.3 2.5 %collective-permute-start.30 = (bf16[128,1152]{1,0:T(8,128)(2,1)S(1)}, bf16[128,1152]{1,0:T(8,128)(2,1)S(1)}, u32[]{:S(2)}, u32[]{:S(2)}) collective-permute-start(bf16[128,1152]{1,0:T(8,128)(2,1)S(1)} %get-tuple-element.129), channel_id=1, source_target_pairs={{0,6},{1,7},{2,4},{3,5},{4,2},{5,3},{6,0},{7,1},{8,14},{9,15},{10,... | collective-permute-start | bytes 884744 | tf_op jit(solution)/shard_map/ppermute | solution.py:22
  147.8 1.3 collective-permute-start.29
  149.8 7.3 %collective-permute-done.30 = bf16[128,1152]{1,0:T(8,128)(2,1)S(1)} collective-permute-done((bf16[128,1152]{1,0:T(8,128)(2,1)S(1)}, bf16[128,1152]{1,0:T(8,128)(2,1)S(1)}, u32[]{:S(2)}, u32[]{:S(2)}) %collective-permute-start.30) | collective-permute-done | bytes 294944 | tf_op jit(solution)/shard_map/ppermute | solution.py:22
  157.1 14.3 %collective-permute-done.29 = bf16[128,1152]{1,0:T(8,128)(2,1)S(1)} collective-permute-done((bf16[128,1152]{1,0:T(8,128)(2,1)S(1)}, bf16[128,1152]{1,0:T(8,128)(2,1)S(1)}, u32[]{:S(2)}, u32[]{:S(2)}) %collective-permute-start.29) | collective-permute-done | bytes 294944 | tf_op jit(solution)/shard_map/ppermute | solution.py:22
  171.9 2.4 %collective-permute-start.37 = (bf16[128,1024]{1,0:T(8,128)(2,1)S(1)}, bf16[128,1024]{1,0:T(8,128)(2,1)S(1)}, u32[]{:S(2)}, u32[]{:S(2)}) collective-permute-start(bf16[128,1024]{1,0:T(8,128)(2,1)S(1)} %get-tuple-element.134), channel_id=1, source_target_pairs={{0,6},{1,7},{2,4},{3,5},{4,2},{5,3},{6,0},{7,1},{8,14},{9,15},{10,... | collective-permute-start | bytes 786440 | tf_op jit(solution)/shard_map/ppermute | solution.py:22
  174.3 2.0 collective-permute-start.35
  177.1 18.9 %backward.2 = (bf16[6144,2048]{1,0:T(8,128)(2,1)}, f32[1,1]{1,0:T(1,128)}) custom-call(s32[3]{0:T(128)S(1)} %pad_add_fusion.place_ref, bf16[128,6144]{1,0:T(8,128)(2,1)} %get-tuple-element.72.refs_0_, bf16[128,6144]{1,0:T(8,128)(2,1)} %collective-permute-done.1.refs_0_.refs_1_, bf16[128,6144]{1,0:T(8,128)(2,1)} %copy-done.14, bf16[64,6144]{1,0:T(8,128)(2,1)} %copy-done, ...), custom_call_target="tpu_custom_call" | custom-call | flops 1024 | bytes 1024 | tf_op jit(solution)/shard_map/backward/pallas_call | solution.py:392
  199.6 18.6 %backward.3 = bf16[6144,2048]{1,0:T(8,128)(2,1)} custom-call(s32[3]{0:T(128)S(1)} %pad_add_fusion.place_ref, bf16[128,6144]{1,0:T(8,128)(2,1)} %get-tuple-element.72.refs_0_, bf16[128,6144]{1,0:T(8,128)(2,1)} %collective-permute-done.1.refs_0_.refs_1_, bf16[128,6144]{1,0:T(8,128)(2,1)} %copy-done.14, ...), custom_call_target="tpu_custom_call", output_to_operand_aliasing={{}: (19, {})} | custom-call | flops 1024 | bytes 1024 | tf_op jit(solution)/shard_map/backward/pallas_call | solution.py:392
  (141 shorter events, 17.7 us)
Async XLA Ops:
  4.3 38.5 %collective-permute-start.2 = (bf16[128,6144]{1,0:T(8,128)(2,1)}, bf16[128,6144]{1,0:T(8,128)(2,1)S(1)}, u32[]{:S(2)}, u32[]{:S(2)}) collective-permute-start(bf16[128,6144]{1,0:T(8,128)(2,1)} %get-tuple-element.72.refs_0_), channel_id=1, source_target_pairs={{0,16},{8,24},{16,0},{24,8},{1,17},{9,25},{17,1},{25,9},{2,18},{10... | collective-permute-start | bytes 4718600 | tf_op jit(solution)/shard_map/ppermute | solution.py:22
  7.4 38.6 %collective-permute-start.1 = (bf16[128,6144]{1,0:T(8,128)(2,1)}, bf16[128,6144]{1,0:T(8,128)(2,1)}, u32[]{:S(2)}, u32[]{:S(2)}) collective-permute-start(bf16[128,6144]{1,0:T(8,128)(2,1)} %get-tuple-element.72.refs_0_), channel_id=1, source_target_pairs={{0,8},{8,0},{16,24},{24,16},{1,9},{9,1},{17,25},{25,17},{2,10},{10... | collective-permute-start | bytes 4718600 | tf_op jit(solution)/shard_map/ppermute | solution.py:22
  8.9 67.8 %collective-permute-start.8 = (bf16[128,6144]{1,0:T(8,128)(2,1)}, bf16[128,6144]{1,0:T(8,128)(2,1)}, u32[]{:S(2)}, u32[]{:S(2)}) collective-permute-start(bf16[128,6144]{1,0:T(8,128)(2,1)} %get-tuple-element.73.refs_1_.refs_5_), channel_id=1, source_target_pairs={{0,16},{8,24},{16,0},{24,8},{1,17},{9,25},{17,1},{25,9},{2,18},{10... | collective-permute-start | bytes 4718600 | tf_op jit(solution)/shard_map/ppermute | solution.py:22
  9.4 69.3 %collective-permute-start.7 = (bf16[128,6144]{1,0:T(8,128)(2,1)}, bf16[128,6144]{1,0:T(8,128)(2,1)}, u32[]{:S(2)}, u32[]{:S(2)}) collective-permute-start(bf16[128,6144]{1,0:T(8,128)(2,1)} %get-tuple-element.73.refs_1_.refs_5_), channel_id=1, source_target_pairs={{0,8},{8,0},{16,24},{24,16},{1,9},{9,1},{17,25},{25,17},{2,10},{10... | collective-permute-start | bytes 4718600 | tf_op jit(solution)/shard_map/ppermute | solution.py:22
  34.5 2.2 %collective-permute-start = (bf16[4,32,2048]{2,1,0:T(8,128)(2,1)}, bf16[4,32,2048]{2,1,0:T(8,128)(2,1)S(1)}, u32[]{:S(2)}, u32[]{:S(2)}) collective-permute-start(bf16[4,32,2048]{2,1,0:T(8,128)(2,1)} %bitcast.60), channel_id=1, source_target_pairs={{0,1},{1,0},{2,3},{3,2},{4,5},{5,4},{6,7},{7,6},{8,9},{9,8},{10,11... | collective-permute-start | bytes 1572872 | tf_op jit(solution)/shard_map/ppermute | solution.py:22
  38.6 23.4 %collective-permute-start.3 = (bf16[32,2048]{1,0:T(8,128)(2,1)S(1)}, bf16[32,2048]{1,0:T(8,128)(2,1)S(1)}, u32[]{:S(2)}, u32[]{:S(2)}) collective-permute-start(bf16[32,2048]{1,0:T(8,128)(2,1)S(1)} %get-tuple-element.82), channel_id=1, source_target_pairs={{0,2},{1,3},{2,0},{3,1},{4,6},{5,7},{6,4},{7,5},{8,10},{9,11},{10,... | collective-permute-start | bytes 393224 | tf_op jit(solution)/shard_map/ppermute | solution.py:22
  42.8 19.2 %collective-permute-start.4 = (bf16[32,2048]{1,0:T(8,128)(2,1)S(1)}, bf16[32,2048]{1,0:T(8,128)(2,1)S(1)}, u32[]{:S(2)}, u32[]{:S(2)}) collective-permute-start(bf16[32,2048]{1,0:T(8,128)(2,1)S(1)} %get-tuple-element.83), channel_id=1, source_target_pairs={{0,4},{1,5},{2,6},{3,7},{4,0},{5,1},{6,2},{7,3},{8,12},{9,13},{10,... | collective-permute-start | bytes 393224 | tf_op jit(solution)/shard_map/ppermute | solution.py:22
  45.9 16.0 %collective-permute-start.5 = (bf16[32,2048]{1,0:T(8,128)(2,1)S(1)}, bf16[32,2048]{1,0:T(8,128)(2,1)S(1)}, u32[]{:S(2)}, u32[]{:S(2)}) collective-permute-start(bf16[32,2048]{1,0:T(8,128)(2,1)S(1)} %get-tuple-element.84), channel_id=1, source_target_pairs={{0,6},{1,7},{2,4},{3,5},{4,2},{5,3},{6,0},{7,1},{8,14},{9,15},{10,... | collective-permute-start | bytes 393224 | tf_op jit(solution)/shard_map/ppermute | solution.py:22
  51.5 25.2 %copy-start.29 = (bf16[64,6144]{1,0:T(8,128)(2,1)S(1)}, bf16[64,6144]{1,0:T(8,128)(2,1)}, u32[]{:S(2)}) copy-start(bf16[64,6144]{1,0:T(8,128)(2,1)} %get-tuple-element.87) | copy-start | bytes 2359300
  62.6 2.2 %collective-permute-start.6 = (bf16[4,32,2048]{2,1,0:T(8,128)(2,1)}, bf16[4,32,2048]{2,1,0:T(8,128)(2,1)S(1)}, u32[]{:S(2)}, u32[]{:S(2)}) collective-permute-start(bf16[4,32,2048]{2,1,0:T(8,128)(2,1)} %bitcast.58), channel_id=1, source_target_pairs={{0,1},{1,0},{2,3},{3,2},{4,5},{5,4},{6,7},{7,6},{8,9},{9,8},{10,11... | collective-permute-start | bytes 1572872 | tf_op jit(solution)/shard_map/ppermute | solution.py:22
  66.6 18.6 %collective-permute-start.9 = (bf16[32,2048]{1,0:T(8,128)(2,1)S(1)}, bf16[32,2048]{1,0:T(8,128)(2,1)S(1)}, u32[]{:S(2)}, u32[]{:S(2)}) collective-permute-start(bf16[32,2048]{1,0:T(8,128)(2,1)S(1)} %get-tuple-element.95), channel_id=1, source_target_pairs={{0,2},{1,3},{2,0},{3,1},{4,6},{5,7},{6,4},{7,5},{8,10},{9,11},{10,... | collective-permute-start | bytes 393224 | tf_op jit(solution)/shard_map/ppermute | solution.py:22
  66.7 20.1 %collective-permute-start.10 = (bf16[32,2048]{1,0:T(8,128)(2,1)S(1)}, bf16[32,2048]{1,0:T(8,128)(2,1)S(1)}, u32[]{:S(2)}, u32[]{:S(2)}) collective-permute-start(bf16[32,2048]{1,0:T(8,128)(2,1)S(1)} %get-tuple-element.96), channel_id=1, source_target_pairs={{0,4},{1,5},{2,6},{3,7},{4,0},{5,1},{6,2},{7,3},{8,12},{9,13},{10,... | collective-permute-start | bytes 393224 | tf_op jit(solution)/shard_map/ppermute | solution.py:22
  68.4 34.3 %collective-permute-start.13 = (bf16[64,6144]{1,0:T(8,128)(2,1)S(1)}, bf16[64,6144]{1,0:T(8,128)(2,1)S(1)}, u32[]{:S(2)}, u32[]{:S(2)}) collective-permute-start(bf16[64,6144]{1,0:T(8,128)(2,1)S(1)} %copy-done.30), channel_id=1, source_target_pairs={{0,16},{8,24},{16,0},{24,8},{1,17},{9,25},{17,1},{25,9},{2,18},{10... | collective-permute-start | bytes 2359304 | tf_op jit(solution)/shard_map/ppermute | solution.py:22
  76.6 26.9 %collective-permute-start.14 = (bf16[64,6144]{1,0:T(8,128)(2,1)S(1)}, bf16[64,6144]{1,0:T(8,128)(2,1)S(1)}, u32[]{:S(2)}, u32[]{:S(2)}) collective-permute-start(bf16[64,6144]{1,0:T(8,128)(2,1)S(1)} %copy-done.29), channel_id=1, source_target_pairs={{0,8},{8,0},{16,24},{24,16},{1,9},{9,1},{17,25},{25,17},{2,10},{10... | collective-permute-start | bytes 2359304 | tf_op jit(solution)/shard_map/ppermute | solution.py:22
  78.7 19.4 %collective-permute-start.11 = (bf16[32,2048]{1,0:T(8,128)(2,1)S(1)}, bf16[32,2048]{1,0:T(8,128)(2,1)S(1)}, u32[]{:S(2)}, u32[]{:S(2)}) collective-permute-start(bf16[32,2048]{1,0:T(8,128)(2,1)S(1)} %get-tuple-element.97), channel_id=1, source_target_pairs={{0,6},{1,7},{2,4},{3,5},{4,2},{5,3},{6,0},{7,1},{8,14},{9,15},{10,... | collective-permute-start | bytes 393224 | tf_op jit(solution)/shard_map/ppermute | solution.py:22
  85.2 27.2 %collective-permute-start.15 = (bf16[64,6144]{1,0:T(8,128)(2,1)}, bf16[64,6144]{1,0:T(8,128)(2,1)S(1)}, u32[]{:S(2)}, u32[]{:S(2)}) collective-permute-start(bf16[64,6144]{1,0:T(8,128)(2,1)} %get-tuple-element.99), channel_id=1, source_target_pairs={{0,16},{8,24},{16,0},{24,8},{1,17},{9,25},{17,1},{25,9},{2,18},{10... | collective-permute-start | bytes 2359304 | tf_op jit(solution)/shard_map/ppermute | solution.py:22
  86.8 25.6 %collective-permute-start.16 = (bf16[64,6144]{1,0:T(8,128)(2,1)}, bf16[64,6144]{1,0:T(8,128)(2,1)S(1)}, u32[]{:S(2)}, u32[]{:S(2)}) collective-permute-start(bf16[64,6144]{1,0:T(8,128)(2,1)} %get-tuple-element.100), channel_id=1, source_target_pairs={{0,8},{8,0},{16,24},{24,16},{1,9},{9,1},{17,25},{25,17},{2,10},{10... | collective-permute-start | bytes 2359304 | tf_op jit(solution)/shard_map/ppermute | solution.py:22
  98.6 2.2 %collective-permute-start.12 = (bf16[4,32,2048]{2,1,0:T(8,128)(2,1)}, bf16[4,32,2048]{2,1,0:T(8,128)(2,1)S(1)}, u32[]{:S(2)}, u32[]{:S(2)}) collective-permute-start(bf16[4,32,2048]{2,1,0:T(8,128)(2,1)} %bitcast.59), channel_id=1, source_target_pairs={{0,1},{1,0},{2,3},{3,2},{4,5},{5,4},{6,7},{7,6},{8,9},{9,8},{10,11... | collective-permute-start | bytes 1572872 | tf_op jit(solution)/shard_map/ppermute | solution.py:22
  102.7 15.3 %collective-permute-start.17 = (bf16[32,2048]{1,0:T(8,128)(2,1)S(1)}, bf16[32,2048]{1,0:T(8,128)(2,1)S(1)}, u32[]{:S(2)}, u32[]{:S(2)}) collective-permute-start(bf16[32,2048]{1,0:T(8,128)(2,1)S(1)} %get-tuple-element.108), channel_id=1, source_target_pairs={{0,2},{1,3},{2,0},{3,1},{4,6},{5,7},{6,4},{7,5},{8,10},{9,11},{10,... | collective-permute-start | bytes 393224 | tf_op jit(solution)/shard_map/ppermute | solution.py:22
  102.8 15.2 %collective-permute-start.18 = (bf16[32,2048]{1,0:T(8,128)(2,1)S(1)}, bf16[32,2048]{1,0:T(8,128)(2,1)S(1)}, u32[]{:S(2)}, u32[]{:S(2)}) collective-permute-start(bf16[32,2048]{1,0:T(8,128)(2,1)S(1)} %get-tuple-element.109), channel_id=1, source_target_pairs={{0,4},{1,5},{2,6},{3,7},{4,0},{5,1},{6,2},{7,3},{8,12},{9,13},{10,... | collective-permute-start | bytes 393224 | tf_op jit(solution)/shard_map/ppermute | solution.py:22
  103.5 14.5 %collective-permute-start.19 = (bf16[32,2048]{1,0:T(8,128)(2,1)S(1)}, bf16[32,2048]{1,0:T(8,128)(2,1)S(1)}, u32[]{:S(2)}, u32[]{:S(2)}) collective-permute-start(bf16[32,2048]{1,0:T(8,128)(2,1)S(1)} %get-tuple-element.110), channel_id=1, source_target_pairs={{0,6},{1,7},{2,4},{3,5},{4,2},{5,3},{6,0},{7,1},{8,14},{9,15},{10,... | collective-permute-start | bytes 393224 | tf_op jit(solution)/shard_map/ppermute | solution.py:22
  112.5 23.4 %copy-start.4 = (bf16[128,2048]{1,0:T(8,128)(2,1)S(1)}, bf16[128,2048]{1,0:T(8,128)(2,1)}, u32[]{:S(2)}) copy-start(bf16[128,2048]{1,0:T(8,128)(2,1)} %take_targets.1.target_ref) | copy-start | bytes 1572868
  112.5 23.4 %copy-start.12 = (f32[2048]{0:T(1024)S(1)}, f32[2048]{0:T(1024)}, u32[]{:S(2)}) copy-start(f32[2048]{0:T(1024)} %param.7) | copy-start | bytes 24580
  118.6 1.6 collective-permute-start.20
  118.7 2.1 collective-permute-start.21
  122.5 7.8 %collective-permute-start.22 = (bf16[32,2048]{1,0:T(8,128)(2,1)S(1)}, bf16[32,2048]{1,0:T(8,128)(2,1)S(1)}, u32[]{:S(2)}, u32[]{:S(2)}) collective-permute-start(bf16[32,2048]{1,0:T(8,128)(2,1)S(1)} %get-tuple-element.122), channel_id=1, source_target_pairs={{0,2},{1,3},{2,0},{3,1},{4,6},{5,7},{6,4},{7,5},{8,10},{9,11},{10,... | collective-permute-start | bytes 393224 | tf_op jit(solution)/shard_map/ppermute | solution.py:22
  123.0 12.9 %collective-permute-start.23 = (bf16[32,2048]{1,0:T(8,128)(2,1)S(1)}, bf16[32,2048]{1,0:T(8,128)(2,1)S(1)}, u32[]{:S(2)}, u32[]{:S(2)}) collective-permute-start(bf16[32,2048]{1,0:T(8,128)(2,1)S(1)} %get-tuple-element.123), channel_id=1, source_target_pairs={{0,4},{1,5},{2,6},{3,7},{4,0},{5,1},{6,2},{7,3},{8,12},{9,13},{10,... | collective-permute-start | bytes 393224 | tf_op jit(solution)/shard_map/ppermute | solution.py:22
  125.6 10.3 %collective-permute-start.24 = (bf16[32,2048]{1,0:T(8,128)(2,1)S(1)}, bf16[32,2048]{1,0:T(8,128)(2,1)S(1)}, u32[]{:S(2)}, u32[]{:S(2)}) collective-permute-start(bf16[32,2048]{1,0:T(8,128)(2,1)S(1)} %get-tuple-element.124), channel_id=1, source_target_pairs={{0,6},{1,7},{2,4},{3,5},{4,2},{5,3},{6,0},{7,1},{8,14},{9,15},{10,... | collective-permute-start | bytes 393224 | tf_op jit(solution)/shard_map/ppermute | solution.py:22
  136.9 5.5 %collective-permute-start.27 = (f32[128,128]{1,0:T(8,128)S(1)}, f32[128,128]{1,0:T(8,128)S(1)}, u32[]{:S(2)}, u32[]{:S(2)}) collective-permute-start(f32[128,128]{1,0:T(8,128)S(1)} %get-tuple-element.127.refs_0_), channel_id=1, source_target_pairs={{0,24},{8,16},{16,8},{24,0},{1,25},{9,17},{17,9},{25,1},{2,26},{10... | collective-permute-start | bytes 196616 | tf_op jit(solution)/shard_map/ppermute | solution.py:22
  139.4 4.3 %collective-permute-start.26 = (f32[128,128]{1,0:T(8,128)S(1)}, f32[128,128]{1,0:T(8,128)S(1)}, u32[]{:S(2)}, u32[]{:S(2)}) collective-permute-start(f32[128,128]{1,0:T(8,128)S(1)} %get-tuple-element.127.refs_0_), channel_id=1, source_target_pairs={{0,16},{8,24},{16,0},{24,8},{1,17},{9,25},{17,1},{25,9},{2,18},{10... | collective-permute-start | bytes 196616 | tf_op jit(solution)/shard_map/ppermute | solution.py:22
  139.9 4.3 %collective-permute-start.25 = (f32[128,128]{1,0:T(8,128)S(1)}, f32[128,128]{1,0:T(8,128)S(1)}, u32[]{:S(2)}, u32[]{:S(2)}) collective-permute-start(f32[128,128]{1,0:T(8,128)S(1)} %get-tuple-element.127.refs_0_), channel_id=1, source_target_pairs={{0,8},{8,0},{16,24},{24,16},{1,9},{9,1},{17,25},{25,17},{2,10},{10... | collective-permute-start | bytes 196616 | tf_op jit(solution)/shard_map/ppermute | solution.py:22
  145.3 31.0 %copy-start.10 = (bf16[128,1152]{1,0:T(8,128)(2,1)}, bf16[128,1152]{1,0:T(8,128)(2,1)S(1)}, u32[]{:S(2)}) copy-start(bf16[128,1152]{1,0:T(8,128)(2,1)S(1)} %get-tuple-element.129) | copy-start | bytes 884740
  145.3 50.8 %copy-start.11 = (bf16[128,1024]{1,0:T(8,128)(2,1)}, bf16[128,1024]{1,0:T(8,128)(2,1)S(1)}, u32[]{:S(2)}) copy-start(bf16[128,1024]{1,0:T(8,128)(2,1)S(1)} %get-tuple-element.134) | copy-start | bytes 786436
  145.3 11.7 %collective-permute-start.30 = (bf16[128,1152]{1,0:T(8,128)(2,1)S(1)}, bf16[128,1152]{1,0:T(8,128)(2,1)S(1)}, u32[]{:S(2)}, u32[]{:S(2)}) collective-permute-start(bf16[128,1152]{1,0:T(8,128)(2,1)S(1)} %get-tuple-element.129), channel_id=1, source_target_pairs={{0,6},{1,7},{2,4},{3,5},{4,2},{5,3},{6,0},{7,1},{8,14},{9,15},{10,... | collective-permute-start | bytes 884744 | tf_op jit(solution)/shard_map/ppermute | solution.py:22
  147.8 23.6 %collective-permute-start.29 = (bf16[128,1152]{1,0:T(8,128)(2,1)S(1)}, bf16[128,1152]{1,0:T(8,128)(2,1)S(1)}, u32[]{:S(2)}, u32[]{:S(2)}) collective-permute-start(bf16[128,1152]{1,0:T(8,128)(2,1)S(1)} %get-tuple-element.129), channel_id=1, source_target_pairs={{0,4},{1,5},{2,6},{3,7},{4,0},{5,1},{6,2},{7,3},{8,12},{9,13},{10,... | collective-permute-start | bytes 884744 | tf_op jit(solution)/shard_map/ppermute | solution.py:22
  149.1 22.3 %collective-permute-start.28 = (bf16[128,1152]{1,0:T(8,128)(2,1)S(1)}, bf16[128,1152]{1,0:T(8,128)(2,1)S(1)}, u32[]{:S(2)}, u32[]{:S(2)}) collective-permute-start(bf16[128,1152]{1,0:T(8,128)(2,1)S(1)} %get-tuple-element.129), channel_id=1, source_target_pairs={{0,2},{1,3},{2,0},{3,1},{4,6},{5,7},{6,4},{7,5},{8,10},{9,11},{10,... | collective-permute-start | bytes 884744 | tf_op jit(solution)/shard_map/ppermute | solution.py:22
  149.8 24.5 %collective-permute-start.31 = (bf16[128,1152]{1,0:T(8,128)(2,1)S(1)}, bf16[128,1152]{1,0:T(8,128)(2,1)S(1)}, u32[]{:S(2)}, u32[]{:S(2)}) collective-permute-start(bf16[128,1152]{1,0:T(8,128)(2,1)S(1)} %get-tuple-element.129), channel_id=1, source_target_pairs={{0,1},{1,0},{2,3},{3,2},{4,5},{5,4},{6,7},{7,6},{8,9},{9,8},{10,11... | collective-permute-start | bytes 884744 | tf_op jit(solution)/shard_map/ppermute | solution.py:22
  157.0 19.3 %copy-start.15 = (bf16[128,1152]{1,0:T(8,128)(2,1)}, bf16[128,1152]{1,0:T(8,128)(2,1)S(1)}, u32[]{:S(2)}) copy-start(bf16[128,1152]{1,0:T(8,128)(2,1)S(1)} %collective-permute-done.30) | copy-start | bytes 884740
  157.0 17.3 %collective-permute-start.34 = (bf16[128,1152]{1,0:T(8,128)(2,1)S(1)}, bf16[128,1152]{1,0:T(8,128)(2,1)S(1)}, u32[]{:S(2)}, u32[]{:S(2)}) collective-permute-start(bf16[128,1152]{1,0:T(8,128)(2,1)S(1)} %collective-permute-done.30), channel_id=1, source_target_pairs={{0,1},{1,0},{2,3},{3,2},{4,5},{5,4},{6,7},{7,6},{8,9},{9,8},{10,11... | collective-permute-start | bytes 884744 | tf_op jit(solution)/shard_map/ppermute | solution.py:22
  171.4 4.9 %collective-permute-start.33 = (bf16[128,1152]{1,0:T(8,128)(2,1)S(1)}, bf16[128,1152]{1,0:T(8,128)(2,1)S(1)}, u32[]{:S(2)}, u32[]{:S(2)}) collective-permute-start(bf16[128,1152]{1,0:T(8,128)(2,1)S(1)} %collective-permute-done.29), channel_id=1, source_target_pairs={{0,1},{1,0},{2,3},{3,2},{4,5},{5,4},{6,7},{7,6},{8,9},{9,8},{10,11... | collective-permute-start | bytes 884744 | tf_op jit(solution)/shard_map/ppermute | solution.py:22
  171.4 4.9 %collective-permute-start.32 = (bf16[128,1152]{1,0:T(8,128)(2,1)S(1)}, bf16[128,1152]{1,0:T(8,128)(2,1)S(1)}, u32[]{:S(2)}, u32[]{:S(2)}) collective-permute-start(bf16[128,1152]{1,0:T(8,128)(2,1)S(1)} %collective-permute-done.28), channel_id=1, source_target_pairs={{0,1},{1,0},{2,3},{3,2},{4,5},{5,4},{6,7},{7,6},{8,9},{9,8},{10,11... | collective-permute-start | bytes 884744 | tf_op jit(solution)/shard_map/ppermute | solution.py:22
  171.9 24.1 %collective-permute-start.37 = (bf16[128,1024]{1,0:T(8,128)(2,1)S(1)}, bf16[128,1024]{1,0:T(8,128)(2,1)S(1)}, u32[]{:S(2)}, u32[]{:S(2)}) collective-permute-start(bf16[128,1024]{1,0:T(8,128)(2,1)S(1)} %get-tuple-element.134), channel_id=1, source_target_pairs={{0,6},{1,7},{2,4},{3,5},{4,2},{5,3},{6,0},{7,1},{8,14},{9,15},{10,... | collective-permute-start | bytes 786440 | tf_op jit(solution)/shard_map/ppermute | solution.py:22
  174.3 21.7 %collective-permute-start.36 = (bf16[128,1024]{1,0:T(8,128)(2,1)S(1)}, bf16[128,1024]{1,0:T(8,128)(2,1)S(1)}, u32[]{:S(2)}, u32[]{:S(2)}) collective-permute-start(bf16[128,1024]{1,0:T(8,128)(2,1)S(1)} %get-tuple-element.134), channel_id=1, source_target_pairs={{0,4},{1,5},{2,6},{3,7},{4,0},{5,1},{6,2},{7,3},{8,12},{9,13},{10,... | collective-permute-start | bytes 786440 | tf_op jit(solution)/shard_map/ppermute | solution.py:22
  174.3 21.7 %collective-permute-start.35 = (bf16[128,1024]{1,0:T(8,128)(2,1)S(1)}, bf16[128,1024]{1,0:T(8,128)(2,1)S(1)}, u32[]{:S(2)}, u32[]{:S(2)}) collective-permute-start(bf16[128,1024]{1,0:T(8,128)(2,1)S(1)} %get-tuple-element.134), channel_id=1, source_target_pairs={{0,2},{1,3},{2,0},{3,1},{4,6},{5,7},{6,4},{7,5},{8,10},{9,11},{10,... | collective-permute-start | bytes 786440 | tf_op jit(solution)/shard_map/ppermute | solution.py:22
  196.1 1.6 collective-permute-start.38
  196.2 1.9 collective-permute-start.39
  196.7 1.8 collective-permute-start.40
  196.8 2.1 collective-permute-start.41
  (26 other events, 108.1 us)
